TPU v7x, 32 devices: a whole 2x2x4 slice. The times are simulated.
32 devices in a mesh: wave: 4 (over z), lev: 2 (over y), grp: 4 (over x, core).
Axes of the slice: x: 2, y: 2, z: 4, core: 2. Of those that a mesh axis runs over, the one named last changes fastest.
Arguments:
- spectra: bfloat16 [2, 4, 2, 16, 1024], P(None, None, 'lev', ('wave', 'grp')), may hold values from -6 to 6
- legendre: bfloat16 [16, 1024, 64], P(('wave', 'grp')), may hold values from -0.1875 to 0.1875
- wavenumbers: int32 [16], replicated, may hold values from 0 to 1023, as said below
- quad_weights: float32 [64], replicated, may hold values from 0.5 to 2
- tracers: float32 [8, 2, 64, 4096], P(None, 'lev', ('wave', 'grp')), may hold values from 0.2 to 2
- kinetics: float32 [8, 8], replicated, may hold values from -2 to 2
- photolysis: float32 [8], replicated, may hold values from -1 to 1
- heat_weights: float32 [3, 8], replicated, may hold values from -2 to 2
Outputs:
- tracers_out: float32 [8, 2, 64, 4096], P(None, 'lev', ('wave', 'grp'))
- heating_spectra: float32 [2, 3, 2, 16, 1024], P(None, None, 'lev', ('wave', 'grp'))
Inputs may be any that keep to these rules, and one draw needn't show every extreme that they name: `wavenumbers`: ascending and distinct; slot s holds a value from s * (64) to (s + 1) * 64 - 1.
All inputs are finite; a program needn't handle non-finite values.
Results may differ from a plain program's by a relative error of at most 0.0025.
Values sent between devices are 32-bit elements; how exact they have to be, the bound alone decides.
No kernel may reach another device: no remote copies, remote signals or barrier semaphores. Data moves between devices by JAX's collectives and lax.ppermute only.
A program may use at most 64 MiB of HBM per device.

v0:
```python
import math

import jax
import jax.numpy as jnp
from jax import lax
from jax.sharding import PartitionSpec as P

NLON = 4096


highest = lax.Precision.HIGHEST


def prefix(part, axis, combine, identity):
    place = lax.axis_index(axis)
    gathered = lax.all_gather(part, axis)
    state = jnp.zeros_like(part) + jnp.asarray(identity, part.dtype)

    def one(step, state):
        return combine(state, lax.dynamic_index_in_dim(gathered, step, 0, False))

    return lax.fori_loop(0, place, one, state)


def with_halo(cells, sides, width):
    for axis, dim in sides:
        count = lax.axis_size(axis)
        ends = count - 1
        head = lax.slice_in_dim(cells, 0, width, axis=dim)
        tail = lax.slice_in_dim(cells, cells.shape[dim] - width, cells.shape[dim], axis=dim)
        cells = jnp.concatenate(
            [
                lax.ppermute(tail, axis, [(i, (i + 1) % count) for i in range(ends)]),
                cells,
                lax.ppermute(head, axis, [((i + 1) % count, i) for i in range(ends)]),
            ],
            axis=dim,
        )
    return cells


def fourier_table(wavenumbers):
    longitudes = jnp.arange(NLON, dtype=jnp.int32)
    phase_index = wavenumbers[:, None] * longitudes[None, :] % NLON
    angles = phase_index.astype(jnp.float32) * (2.0 * math.pi / NLON)
    return jnp.stack([jnp.cos(angles), -jnp.sin(angles)])


def advect(padded, courant_x, courant_y):
    centre = padded[..., 1:-1, :]
    northern = padded[..., :-2, :]
    southern = padded[..., 2:, :]
    western = jnp.roll(centre, 1, axis=-1)
    eastern = jnp.roll(centre, -1, axis=-1)
    return (
        centre
        - jnp.maximum(courant_x, 0.0) * (centre - western)
        - jnp.minimum(courant_x, 0.0) * (eastern - centre)
        - jnp.maximum(courant_y, 0.0) * (centre - northern)
        - jnp.minimum(courant_y, 0.0) * (southern - centre)
    )


def react(tracer_now, react_rate, photo_rate, kinetics, photolysis):
    mixed = jnp.tensordot(kinetics, tracer_now, axes=1, precision=highest)
    yields = photolysis.reshape((-1,) + (1,) * (tracer_now.ndim - 1))
    return tracer_now + 0.2 * react_rate * mixed + 0.2 * photo_rate * yields * tracer_now[0]


def add_levels(earlier, later):
    return earlier + later


def body(spectra, legendre, wavenumbers, quad_weights, tracers, kinetics, photolysis, heat_weights):
    local_count = legendre.shape[0]
    ndegree = legendre.shape[1]
    position = lax.axis_index(("wave", "grp"))
    own_waves = lax.dynamic_slice_in_dim(wavenumbers, position * local_count, local_count)
    degree_mask = jnp.arange(ndegree, dtype=jnp.int32)[None, :] < (ndegree - own_waves)[:, None]
    masked_coeffs = jnp.where(degree_mask, spectra[:, :, 0], jnp.zeros((), spectra.dtype))
    fourier = jnp.einsum(
        "pfsj,sjy->pfsy", masked_coeffs, legendre, preferred_element_type=jnp.float32
    )
    total_waves = wavenumbers.shape[0]
    shared_table = fourier_table(wavenumbers)
    synth_scale = 1.0 / math.sqrt(total_waves)
    grid_fields = (
        jnp.einsum(
            "pksy,psx->kyx",
            lax.all_to_all(fourier, ("wave", "grp"), split_axis=3, concat_axis=2, tiled=True),
            shared_table,
            precision=highest,
        )
        * synth_scale
    )
    courant_x = 0.45 * jnp.tanh(grid_fields[0])
    courant_y = 0.45 * jnp.tanh(grid_fields[1])
    react_rate = jnp.exp(0.3 * grid_fields[2])
    tracer_now = tracers[:, 0]
    levels = lax.axis_size("lev")
    overhead = prefix(tracer_now[0], "lev", add_levels, jnp.zeros_like(tracer_now[0]))
    photo_rate = jnp.exp(-2.0 * overhead / levels)
    for substep in range(2):
        padded = with_halo(tracer_now, ((("wave", "grp"), 1),), 1)
        tracer_now = react(
            advect(padded, courant_x, courant_y), react_rate, photo_rate, kinetics, photolysis
        )
    heating = jnp.tensordot(heat_weights, tracer_now, axes=1, precision=highest) * (
        1.0 + 0.5 * jnp.tanh(grid_fields[3])
    )
    heat_fourier = jnp.einsum("kyx,psx->pksy", heating, shared_table, precision=highest) * (
        1.0 / math.sqrt(NLON)
    )
    weighted = (
        lax.all_to_all(heat_fourier, ("wave", "grp"), split_axis=2, concat_axis=3, tiled=True)
        * quad_weights
    ).astype(jnp.bfloat16)
    heating_spectra = jnp.einsum(
        "pksy,sjy->pksj", weighted, legendre, preferred_element_type=jnp.float32
    )
    heating_spectra = jnp.where(degree_mask, heating_spectra, jnp.zeros((), jnp.float32))
    return (tracer_now[:, None], heating_spectra[:, :, None])


def solution(mesh):
    return jax.shard_map(
        body,
        mesh=mesh,
        in_specs=(
            P(None, None, "lev", ("wave", "grp"), None),
            P(("wave", "grp"), None, None),
            P(),
            P(),
            P(None, "lev", ("wave", "grp"), None),
            P(),
            P(),
            P(),
        ),
        out_specs=(
            P(None, "lev", ("wave", "grp"), None),
            P(None, None, "lev", ("wave", "grp"), None),
        ),
        check_vma=False,
    )
```

profile of v0, /device:TPU:0, one launch (start us, length us, event | category | flops | bytes accessed | tf_op | source)
XLA Modules:
  0.0 56.9 jit_solution(1519610543019506378)
XLA Ops:
  0.6 0.0 copy-start
  0.7 0.7 %copy-done.4 = s32[16]{0:T(128)S(1)} copy-done((s32[16]{0:T(128)S(1)}, s32[16]{0:T(128)}, u32[]{:S(2)}) %copy-start.4) | copy-done | bytes 88
  1.4 0.6 %dynamic_slice.7 = s32[1]{0:T(128)} dynamic-slice(s32[16]{0:T(128)S(1)} %copy-done.4, s32[]{:T(128)S(6)} %select_n.42), dynamic_slice_sizes={1} | dynamic-slice | bytes 12 | tf_op jit(solution)/shard_map/dynamic_slice | solution.py:78
  2.6 0.2 convolution_bitcast_fusion.2
  2.8 0.8 %copy.45 = f32[2,4,1,64]{1,0,2,3:T(2,128)} copy(f32[2,4,1,64]{3,1,0,2:T(4,128)S(1)} %convolution_bitcast_fusion.2) | data formatting | bytes 4096 | tf_op jit(solution)/shard_map/pfsj,sjy->pfsy/transpose | solution.py:81
  3.5 7.4 %all-to-all-start = ((f32[2,4,1,64]{1,0,2,3:T(2,128)}), f32[2,4,1,64]{1,0,2,3:T(2,128)S(1)}, u32[]{:S(2)}, u32[]{:S(2)}) async-start(f32[2,4,1,64]{1,0,2,3:T(2,128)} %copy.45), calls=%async_computation | async-start | bytes 131072 | tf_op jit(solution)/shard_map/all_to_all | solution.py:90
  10.9 1.4 %copy.72 = f32[8,1,4,4096]{3,0,2,1:T(8,128)S(1)} copy(f32[8,1,4,4096]{3,2,1,0:T(4,128)} %param.14) | data formatting | bytes 1048576 | tf_op args[4]
  12.3 2.3 %collective-permute-start = (f32[8,1,4096]{2,0,1:T(8,128)S(1)}, f32[8,1,4096]{2,0,1:T(8,128)S(1)}, u32[]{:S(2)}, u32[]{:S(2)}) collective-permute-start(f32[8,1,4096]{2,0,1:T(8,128)S(1)} %get-tuple-element.54), channel_id=1, source_target_pairs={{0,1},{1,2},{2,3},{3,8},{8,9},{9,10},{10,11},{11,16},{16,17},{17,1... | collective-permute-start | bytes 393224 | tf_op jit(solution)/shard_map/ppermute | solution.py:33
  14.6 1.3 %collective-permute-start.1 = (f32[8,1,4096]{2,0,1:T(8,128)S(1)}, f32[8,1,4096]{2,0,1:T(8,128)S(1)}, u32[]{:S(2)}, u32[]{:S(2)}) collective-permute-start(f32[8,1,4096]{2,0,1:T(8,128)S(1)} %get-tuple-element.55), channel_id=1, source_target_pairs={{1,0},{2,1},{3,2},{8,3},{9,8},{10,9},{11,10},{16,11},{17,16},{18,1... | collective-permute-start | bytes 393224 | tf_op jit(solution)/shard_map/ppermute | solution.py:35
  15.9 1.1 %fusion.41 = (f32[1,16,4096]{2,1,0:T(8,128)S(1)}, f32[1,16,4096]{2,1,0:T(8,128)S(1)}) fusion(s32[16]{0:T(128)S(1)} %copy-done.4), kind=kLoop, calls=%fused_computation.65 | loop fusion | flops 983040 | bytes 524352 | tf_op jit(solution)/shard_map/cos | solution.py:46
  17.0 0.2 fusion.63
  17.2 0.0 slice-start
  17.2 0.8 %slice-done = f32[1,1,4,4096]{3,2,1,0:T(4,128)S(1)} async-done(((f32[8,1,4,4096]{3,2,1,0:T(4,128)}), f32[1,1,4,4096]{3,2,1,0:T(4,128)S(1)}, s32[]{:S(2)}) %slice-start) | async-done | bytes 65560 | tf_op jit(solution)/shard_map/slice | solution.py:101
  18.1 4.9 %all-gather = f32[2,1,4,4096]{3,2,1,0:T(4,128)S(1)} all-gather(f32[1,1,4,4096]{3,2,1,0:T(4,128)S(1)} %slice-done), channel_id=2, replica_groups=mesh['wave'=4,'lev'=2,'grp'=4] {'lev'}, dimensions={0}, use_global_device_ids=true | all-gather | bytes 196608 | tf_op jit(solution)/shard_map/all_gather | solution.py:16
  23.1 0.1 fusion.64
  23.1 0.0 all-to-all-done
  23.1 0.3 copy.56
  23.5 0.6 %fusion.7 = f32[4,4,4096]{2,1,0:T(4,128)S(1)} fusion(f32[2,4,16,4]{3,2,1,0:T(8,128)S(1)} %copy.56, f32[1,16,4096]{2,1,0:T(8,128)S(1)} %get-tuple-element.63, f32[1,16,4096]{2,1,0:T(8,128)S(1)} %get-tuple-element.62), kind=kOutput, calls=%fused_computation.12 | convolution fusion | flops 25362432 | bytes 788480 | tf_op jit(solution)/shard_map/pksy,psx->kyx/dot_general | solution.py:88
  24.1 0.1 fusion.44
  24.2 0.3 fusion.19
  24.6 0.0 copy-start.1
  24.7 0.0 copy-start.3
  24.7 0.6 %copy-done.1 = f32[8,8]{1,0:T(8,128)S(1)} copy-done((f32[8,8]{1,0:T(8,128)S(1)}, f32[8,8]{1,0:T(8,128)}, u32[]{:S(2)}) %copy-start.1) | copy-done | bytes 280
  25.3 0.0 copy-done.3
  25.3 0.6 %fusion.5 = f32[8,4,4096]{2,0,1:T(8,128)S(1)} fusion(f32[8,4,4096]{2,0,1:T(8,128)S(1)} %fusion.19, f32[4,4096]{1,0:T(4,128)S(1)} %bitcast.107, f32[8]{0:T(128)S(1)} %copy-done.3, f32[4,4096]{1,0:T(4,128)S(1)} %exponential_multiply_fusion, f32[4,4096]{1,0:T(4,128)S(1)} %get-tuple-element.59, f32[8,8]{1,0:T(8,128)S(1)} %copy-done.1), kind=kOutput, calls=%fused_computation.8 | convolution fusion | flops 13238272 | bytes 1245472 | tf_op jit(solution)/shard_map/dot_general | solution.py:65
  26.0 0.2 fusion.60
  26.2 3.0 %collective-permute-start.2 = (f32[8,1,4096]{2,0,1:T(8,128)S(1)}, f32[8,1,4096]{2,0,1:T(8,128)S(1)}, u32[]{:S(2)}, u32[]{:S(2)}) collective-permute-start(f32[8,1,4096]{2,0,1:T(8,128)S(1)} %get-tuple-element.48), channel_id=1, source_target_pairs={{0,1},{1,2},{2,3},{3,8},{8,9},{9,10},{10,11},{11,16},{16,17},{17,1... | collective-permute-start | bytes 393224 | tf_op jit(solution)/shard_map/ppermute | solution.py:33
  29.2 1.3 %collective-permute-start.3 = (f32[8,1,4096]{2,0,1:T(8,128)S(1)}, f32[8,1,4096]{2,0,1:T(8,128)S(1)}, u32[]{:S(2)}, u32[]{:S(2)}) collective-permute-start(f32[8,1,4096]{2,0,1:T(8,128)S(1)} %get-tuple-element.49), channel_id=1, source_target_pairs={{1,0},{2,1},{3,2},{8,3},{9,8},{10,9},{11,10},{16,11},{17,16},{18,1... | collective-permute-start | bytes 393224 | tf_op jit(solution)/shard_map/ppermute | solution.py:35
  30.5 0.1 fusion.61
  30.6 0.0 collective-permute-done.2
  30.6 4.2 %collective-permute-done.3 = f32[8,1,4096]{2,0,1:T(8,128)S(1)} collective-permute-done((f32[8,1,4096]{2,0,1:T(8,128)S(1)}, f32[8,1,4096]{2,0,1:T(8,128)S(1)}, u32[]{:S(2)}, u32[]{:S(2)}) %collective-permute-start.3) | collective-permute-done | bytes 131104 | tf_op jit(solution)/shard_map/ppermute | solution.py:35
  34.9 0.3 fusion.13
  35.3 0.0 copy-start.2
  35.3 0.6 %fusion.2 = f32[8,4,4096]{2,0,1:T(8,128)S(1)} fusion(f32[8,4,4096]{2,0,1:T(8,128)S(1)} %fusion.13, f32[4,4096]{1,0:T(4,128)S(1)} %bitcast.106, f32[8]{0:T(128)S(1)} %copy-done.3, f32[4,4096]{1,0:T(4,128)S(1)} %exponential_multiply_fusion, f32[4,4096]{1,0:T(4,128)S(1)} %get-tuple-element.59, f32[8,8]{1,0:T(8,128)S(1)} %copy-done.1), kind=kOutput, calls=%fused_computation.4 | convolution fusion | flops 13238272 | bytes 1245472 | tf_op jit(solution)/shard_map/dot_general | solution.py:65
  35.9 0.0 copy-done.2
  36.0 0.6 fusion.6
  36.5 1.9 %fusion.10 = f32[2,3,16,4]{2,3,1,0:T(4,128)S(1)} fusion(f32[1,16,4096]{2,1,0:T(8,128)S(1)} %get-tuple-element.63, f32[1,16,4096]{2,1,0:T(8,128)S(1)} %get-tuple-element.62, f32[3,4,4096]{2,0,1:T(4,128)S(1)} %fusion.6), kind=kOutput, calls=%fused_computation.17 | convolution fusion | flops 19005824 | bytes 722432 | tf_op jit(solution)/shard_map/kyx,psx->pksy/dot_general | solution.py:111
  38.5 0.7 %copy.49 = f32[2,3,16,4]{3,0,1,2:T(2,128)} copy(f32[2,3,16,4]{2,3,1,0:T(4,128)S(1)} %fusion.10) | data formatting | bytes 3072 | tf_op jit(solution)/shard_map/mul | solution.py:111
  39.2 9.7 %all-to-all-start.1 = ((f32[2,3,16,4]{3,0,1,2:T(2,128)}), f32[2,3,16,4]{3,0,1,2:T(2,128)S(1)}, u32[]{:S(2)}, u32[]{:S(2)}) async-start(f32[2,3,16,4]{3,0,1,2:T(2,128)} %copy.49), calls=%async_computation.1 | async-start | bytes 98304 | tf_op jit(solution)/shard_map/all_to_all | solution.py:115
  49.0 0.1 mul.302
  49.1 0.1 copy.50
  49.1 1.1 %copy.54 = f32[8,1,4,4096]{3,2,1,0:T(4,128)} copy(f32[8,1,4,4096]{3,0,2,1:T(8,128)S(1)} %bitcast.104) | data formatting | bytes 1048576
  50.3 5.4 %all-to-all-done.1 = f32[2,3,16,4]{3,0,1,2:T(2,128)S(1)} async-done(((f32[2,3,16,4]{3,0,1,2:T(2,128)}), f32[2,3,16,4]{3,0,1,2:T(2,128)S(1)}, u32[]{:S(2)}, u32[]{:S(2)}) %all-to-all-start.1) | async-done | bytes 1568 | tf_op jit(solution)/shard_map/all_to_all | solution.py:115
  55.7 0.1 copy.51
  55.9 0.1 copy.61
  56.0 0.1 reshape.156
  56.1 0.1 fusion.9
  56.2 0.6 %copy.55 = f32[2,3,1,1,1024]{4,3,2,1,0:T(1,128)} copy(f32[2,3,1,1,1024]{4,1,0,3,2:T(4,128)S(1)} %fusion.9) | data formatting | bytes 49152
  (19 shorter events, 0.3 us)
Async XLA Ops:
  0.6 2.0 %copy-start = (bf16[1,1024,64]{1,2,0:T(8,128)(2,1)S(1)}, bf16[1,1024,64]{1,2,0:T(8,128)(2,1)}, u32[]{:S(2)}) copy-start(bf16[1,1024,64]{1,2,0:T(8,128)(2,1)} %param.11) | copy-start | bytes 393220
  0.6 2.0 %copy-start.6 = (bf16[2,4,1,1,1024]{4,1,3,2,0:T(4,128)(2,1)S(1)}, bf16[2,4,1,1,1024]{4,1,3,2,0:T(4,128)(2,1)}, u32[]{:S(2)}) copy-start(bf16[2,4,1,1,1024]{4,1,3,2,0:T(4,128)(2,1)} %param.10) | copy-start | bytes 49156
  0.7 0.7 %copy-start.4 = (s32[16]{0:T(128)S(1)}, s32[16]{0:T(128)}, u32[]{:S(2)}) copy-start(s32[16]{0:T(128)} %param.12) | copy-start | bytes 196
  3.5 19.6 %all-to-all-start = ((f32[2,4,1,64]{1,0,2,3:T(2,128)}), f32[2,4,1,64]{1,0,2,3:T(2,128)S(1)}, u32[]{:S(2)}, u32[]{:S(2)}) async-start(f32[2,4,1,64]{1,0,2,3:T(2,128)} %copy.45), calls=%async_computation | async-start | bytes 131072 | tf_op jit(solution)/shard_map/all_to_all | solution.py:90
  12.3 11.9 %collective-permute-start = (f32[8,1,4096]{2,0,1:T(8,128)S(1)}, f32[8,1,4096]{2,0,1:T(8,128)S(1)}, u32[]{:S(2)}, u32[]{:S(2)}) collective-permute-start(f32[8,1,4096]{2,0,1:T(8,128)S(1)} %get-tuple-element.54), channel_id=1, source_target_pairs={{0,1},{1,2},{2,3},{3,8},{8,9},{9,10},{10,11},{11,16},{16,17},{17,1... | collective-permute-start | bytes 393224 | tf_op jit(solution)/shard_map/ppermute | solution.py:33
  14.6 9.6 %collective-permute-start.1 = (f32[8,1,4096]{2,0,1:T(8,128)S(1)}, f32[8,1,4096]{2,0,1:T(8,128)S(1)}, u32[]{:S(2)}, u32[]{:S(2)}) collective-permute-start(f32[8,1,4096]{2,0,1:T(8,128)S(1)} %get-tuple-element.55), channel_id=1, source_target_pairs={{1,0},{2,1},{3,2},{8,3},{9,8},{10,9},{11,10},{16,11},{17,16},{18,1... | collective-permute-start | bytes 393224 | tf_op jit(solution)/shard_map/ppermute | solution.py:35
  17.2 0.8 %slice-start = ((f32[8,1,4,4096]{3,2,1,0:T(4,128)}), f32[1,1,4,4096]{3,2,1,0:T(4,128)S(1)}, s32[]{:S(2)}) async-start(f32[8,1,4,4096]{3,2,1,0:T(4,128)} %param.14), calls=%async_computation.2 | async-start | bytes 131072 | tf_op jit(solution)/shard_map/slice | solution.py:101
  24.6 0.7 %copy-start.1 = (f32[8,8]{1,0:T(8,128)S(1)}, f32[8,8]{1,0:T(8,128)}, u32[]{:S(2)}) copy-start(f32[8,8]{1,0:T(8,128)} %param.15) | copy-start | bytes 772
  24.7 0.7 %copy-start.3 = (f32[8]{0:T(128)S(1)}, f32[8]{0:T(128)}, u32[]{:S(2)}) copy-start(f32[8]{0:T(128)} %param.16) | copy-start | bytes 100
  26.2 4.4 %collective-permute-start.2 = (f32[8,1,4096]{2,0,1:T(8,128)S(1)}, f32[8,1,4096]{2,0,1:T(8,128)S(1)}, u32[]{:S(2)}, u32[]{:S(2)}) collective-permute-start(f32[8,1,4096]{2,0,1:T(8,128)S(1)} %get-tuple-element.48), channel_id=1, source_target_pairs={{0,1},{1,2},{2,3},{3,8},{8,9},{9,10},{10,11},{11,16},{16,17},{17,1... | collective-permute-start | bytes 393224 | tf_op jit(solution)/shard_map/ppermute | solution.py:33
  29.2 5.6 %collective-permute-start.3 = (f32[8,1,4096]{2,0,1:T(8,128)S(1)}, f32[8,1,4096]{2,0,1:T(8,128)S(1)}, u32[]{:S(2)}, u32[]{:S(2)}) collective-permute-start(f32[8,1,4096]{2,0,1:T(8,128)S(1)} %get-tuple-element.49), channel_id=1, source_target_pairs={{1,0},{2,1},{3,2},{8,3},{9,8},{10,9},{11,10},{16,11},{17,16},{18,1... | collective-permute-start | bytes 393224 | tf_op jit(solution)/shard_map/ppermute | solution.py:35
  35.3 0.7 %copy-start.2 = (f32[3,8]{1,0:T(4,128)S(1)}, f32[3,8]{1,0:T(4,128)}, u32[]{:S(2)}) copy-start(f32[3,8]{1,0:T(4,128)} %param.17) | copy-start | bytes 292
  39.2 9.7 %copy-start.5 = (f32[64]{0:T(128)S(1)}, f32[64]{0:T(128)}, u32[]{:S(2)}) copy-start(f32[64]{0:T(128)} %param.13) | copy-start | bytes 772
  39.2 16.5 %all-to-all-start.1 = ((f32[2,3,16,4]{3,0,1,2:T(2,128)}), f32[2,3,16,4]{3,0,1,2:T(2,128)S(1)}, u32[]{:S(2)}, u32[]{:S(2)}) async-start(f32[2,3,16,4]{3,0,1,2:T(2,128)} %copy.49), calls=%async_computation.1 | async-start | bytes 98304 | tf_op jit(solution)/shard_map/all_to_all | solution.py:115
where the time goes:
time: 57.4 us; the launch traced here: 56.9 us
  starting transfers between devices  25 us (44%)
  waiting for transfers between devices  9.7 us (17%)
  local copies, waits for them, and re-layouts  9.02 us (16%)
  blocking collectives  4.93 us (9%)
  matrix products  4.69 us (8%)
  other arithmetic  1.94 us (3%)
  between operations  1.58 us (3%)
    all_to_all x1, starting transfers between devices, body(): lax.all_to_all(heat_fourier, ('wave', 'grp'), split_axis=2, concat_axis=3...  9.72 us
    all_to_all x1, starting transfers between devices, body(): lax.all_to_all(fourier, ('wave', 'grp'), split_axis=3, concat_axis=2, til...  7.36 us
    all_to_all x1, waiting for transfers between devices, body(): lax.all_to_all(heat_fourier, ('wave', 'grp'), split_axis=2, concat_axis=3...  5.45 us
    ppermute x2, starting transfers between devices, with_halo(): lax.ppermute(tail, axis, [(i, (i + 1) % count) for i in range(ends)])  5.34 us
    all_gather x1, blocking collectives, prefix(): gathered = lax.all_gather(part, axis)  4.93 us
    unnamed x19, local copies, waits for them, and re-layouts  4.62 us
    ppermute x2, waiting for transfers between devices, with_halo(): lax.ppermute(head, axis, [((i + 1) % count, i) for i in range(ends)])  4.25 us
    ppermute x2, starting transfers between devices, with_halo(): lax.ppermute(head, axis, [((i + 1) % count, i) for i in range(ends)])  2.58 us
  transfers between devices with their start and end apart: 6, of which 2 were waited for; matrix products, arithmetic and copies ran while one was open for 9% of the time, Pallas kernels for 0%

commit v1 on v0

v1 whole, which is shorter than its diff:
```python
import functools
import math

import jax
import jax.numpy as jnp
from jax import lax
from jax.experimental import pallas as pl
from jax.experimental.pallas import tpu as pltpu
from jax.sharding import PartitionSpec as P

LANES = 128
SUB = 8
PLACE = ("wave", "grp")
VMEM_BYTES = 48 * 1024 * 1024


def split_bf16(value):
    high = value.astype(jnp.bfloat16)
    low = (value - high.astype(jnp.float32)).astype(jnp.bfloat16)
    return high, low


def call(body, out_shape, in_spaces, scratch=(), out_spaces=None, flops=1_000_000):
    shapes = out_shape if isinstance(out_shape, (list, tuple)) else (out_shape,)
    spaces = out_spaces or [pltpu.VMEM] * len(shapes)
    specs = [pl.BlockSpec(memory_space=s) for s in spaces]
    return pl.pallas_call(
        body,
        out_shape=out_shape,
        in_specs=[pl.BlockSpec(memory_space=s) for s in in_spaces],
        out_specs=specs if isinstance(out_shape, (list, tuple)) else specs[0],
        scratch_shapes=list(scratch),
        compiler_params=pltpu.CompilerParams(vmem_limit_bytes=VMEM_BYTES),
        cost_estimate=pl.CostEstimate(flops=flops, bytes_accessed=0, transcendentals=0),
    )


def fourier_kernel(waves_ref, spectra_ref, legendre_ref, out_ref, padded):
    parts, fields, degrees = spectra_ref.shape
    lats = legendre_ref.shape[0]
    places = out_ref.shape[0]
    band = lats // places
    margin = (SUB - band) // 2
    place = lax.axis_index(PLACE)
    limit = degrees - waves_ref[place]
    keep = lax.broadcasted_iota(jnp.int32, (SUB, degrees), 1) < limit
    rows = []
    for p in range(parts):
        block = spectra_ref[p].astype(jnp.float32)
        for f in range(fields):
            row = jnp.broadcast_to(block[f : f + 1], (SUB, degrees))
            rows.append(jnp.where(keep, row, 0.0))
    spread = jnp.concatenate(rows, axis=0).astype(jnp.bfloat16)
    fourier = lax.dot_general(
        legendre_ref[...], spread, (((1,), (1,)), ((), ())), preferred_element_type=jnp.float32
    )
    width = fourier.shape[1]
    padded[...] = jnp.zeros_like(padded)
    padded[SUB : SUB + lats, :width] = fourier
    lane = lax.broadcasted_iota(jnp.int32, (places, LANES), 1) % SUB
    total = jnp.zeros((places, LANES), jnp.float32)
    for r in range(SUB):
        rows_r = padded[pl.ds(SUB - margin + r, places, stride=band), :]
        total = jnp.where(lane == r, rows_r, total)
    out_ref[...] = total


def halo_kernel(width, tracers_ref, near_ref, far_ref):
    parity = lax.axis_index(PLACE) % 2
    band = tracers_ref.shape[1]
    tracers = tracers_ref[...]
    top = tracers[:, :width]
    bottom = tracers[:, band - width :]
    even = parity == 0
    near_ref[...] = jnp.where(even, bottom, top)
    far_ref[...] = jnp.where(even, top, bottom)


def band_kernel(tracers_ref, near_ref, far_ref, padded_ref, column_ref):
    even = lax.axis_index(PLACE) % 2 == 0
    lons = tracers_ref.shape[2]
    near, far = near_ref[...], far_ref[...]
    north = jnp.where(even, far, near)
    south = jnp.where(even, near, far)
    whole = jnp.concatenate([north, tracers_ref[...], south], axis=1)
    padded_ref[:, :, LANES : LANES + lons] = whole
    padded_ref[:, :, :LANES] = whole[:, :, lons - LANES :]
    padded_ref[:, :, LANES + lons :] = whole[:, :, :LANES]
    column_ref[...] = whole[0]


def table_kernel(waves_ref, table_ref):
    lons = table_ref.shape[1]
    waves = table_ref.shape[0] // 4
    row = lax.broadcasted_iota(jnp.int32, (waves, LANES), 0)
    column = lax.broadcasted_iota(jnp.int32, (waves, LANES), 1)
    numbers = jnp.zeros((waves, LANES), jnp.int32)
    for s in range(waves):
        numbers = jnp.where(row == s, waves_ref[s], numbers)

    def turn(longitude):
        index = (numbers * longitude) & (lons - 1)
        angle = index.astype(jnp.float32) * (2.0 * math.pi / lons)
        return jnp.cos(angle), jnp.sin(angle)

    blocks = [turn(column)]
    while len(blocks) * LANES < lons:
        step_cos, step_sin = turn(jnp.full_like(column, len(blocks) * LANES))
        blocks += [(c * step_cos - s * step_sin, s * step_cos + c * step_sin) for c, s in blocks]
    for b, (cosine, sine) in enumerate(blocks):
        span = slice(b * LANES, (b + 1) * LANES)
        cos_high, cos_low = split_bf16(cosine)
        sin_high, sin_low = split_bf16(-sine)
        table_ref[0:waves, span] = cos_high
        table_ref[waves : 2 * waves, span] = sin_high
        table_ref[2 * waves : 3 * waves, span] = cos_low
        table_ref[3 * waves :, span] = sin_low


def grid_kernel(
    levels,
    band,
    kinetics_ref,
    photolysis_ref,
    weights_ref,
    received_ref,
    padded_ref,
    overhead_ref,
    table_ref,
    tracers_ref,
    sent_ref,
    middle,
    coeffs,
    heat,
):
    tracers = padded_ref.shape[0]
    lons = table_ref.shape[1]
    places, waves = received_ref.shape[0], table_ref.shape[0] // 4
    heats = weights_ref.shape[0]
    margin = (SUB - band) // 2
    chunk = 2 * LANES
    fields = 4
    rows = fields * SUB
    turned = received_ref[...].T
    lhs = jnp.concatenate([turned[:rows], turned[rows : 2 * rows]], axis=1) * (
        1.0 / math.sqrt(waves)
    )
    high, low = split_bf16(lhs)
    both = jnp.concatenate(
        [
            jnp.concatenate([high, high], axis=1),
            jnp.concatenate([low, jnp.zeros_like(low)], axis=1),
        ],
        axis=0,
    )
    place = lax.axis_index(PLACE)
    latitude = (
        place * band - margin + lax.broadcasted_iota(jnp.int32, (SUB, chunk), 0)
    )
    inside = (latitude >= 0) & (latitude < places * band)

    def stencil(load, columns, coef, mix):
        west_c, east_c, north_c, south_c, own_c, react, photo = coef
        moved = []
        for t in range(tracers):
            wide = load(t)
            span = wide.shape[1]
            west = pltpu.roll(wide, 1, 1)[:, LANES : LANES + chunk]
            east = pltpu.roll(wide, span - 1, 1)[:, LANES : LANES + chunk]
            own = wide[:, LANES : LANES + chunk]
            north = pltpu.roll(own, 1, 0)
            south = pltpu.roll(own, SUB - 1, 0)
            moved.append(
                own_c * own + west_c * west + east_c * east + north_c * north + south_c * south
            )
        lit = photo * moved[0]
        out = []
        for i in range(tracers):
            mixed = kinetics_ref[i, 0] * moved[0]
            for j in range(1, tracers):
                mixed = mixed + kinetics_ref[i, j] * moved[j]
            out.append(moved[i] + react * mixed + photolysis_ref[i] * lit)
        return out

    def first(step, carry):
        start = pl.multiple_of(step * chunk, chunk)
        grid = jnp.dot(
            both, table_ref[:, pl.ds(start, chunk)], preferred_element_type=jnp.float32
        )
        grid = grid[:rows] + grid[rows:]
        courant_x = jnp.where(inside, 0.45 * jnp.tanh(grid[0:SUB]), 0.0)
        courant_y = jnp.where(inside, 0.45 * jnp.tanh(grid[SUB : 2 * SUB]), 0.0)
        react = 0.2 * jnp.exp(0.3 * grid[2 * SUB : 3 * SUB])
        warm = 1.0 + 0.5 * jnp.tanh(grid[3 * SUB :])
        photo = 0.2 * jnp.exp((-2.0 / levels) * overhead_ref[:, pl.ds(start, chunk)])
        own_c = jnp.where(inside, 1.0 - jnp.abs(courant_x) - jnp.abs(courant_y), 0.0)
        coef = (
            jnp.maximum(courant_x, 0.0),
            -jnp.minimum(courant_x, 0.0),
            jnp.maximum(courant_y, 0.0),
            -jnp.minimum(courant_y, 0.0),
            own_c,
            react,
            photo,
        )
        for n, value in enumerate(coef + (warm,)):
            coeffs[n, :, pl.ds(start, chunk)] = value
        out = stencil(lambda t: padded_ref[t, :, pl.ds(start, chunk + 2 * LANES)], chunk, coef, 0)
        for t in range(tracers):
            middle[t, :, pl.ds(start + LANES, chunk)] = out[t]
        return carry

    lax.fori_loop(0, lons // chunk, first, 0)
    for t in range(tracers):
        middle[t, :, 0:LANES] = middle[t, :, lons : lons + LANES]
        middle[t, :, LANES + lons :] = middle[t, :, LANES : 2 * LANES]

    def second(step, carry):
        start = pl.multiple_of(step * chunk, chunk)
        coef = tuple(coeffs[n, :, pl.ds(start, chunk)] for n in range(7))
        warm = coeffs[7, :, pl.ds(start, chunk)]
        out = stencil(lambda t: middle[t, :, pl.ds(start, chunk + 2 * LANES)], chunk, coef, 0)
        for t in range(tracers):
            tracers_ref[t, :, pl.ds(start, chunk)] = out[t][margin : margin + band]
        heated = []
        for k in range(heats):
            total = weights_ref[k, 0] * out[0]
            for i in range(1, tracers):
                total = total + weights_ref[k, i] * out[i]
            heated.append(total * warm)
        heated = jnp.concatenate(heated, axis=0)
        heat_high, heat_low = split_bf16(heated)
        stacked = jnp.concatenate([heat_high, heat_low], axis=0)
        return carry + lax.dot_general(
            table_ref[:, pl.ds(start, chunk)],
            stacked,
            (((1,), (1,)), ((), ())),
            preferred_element_type=jnp.float32,
        )

    wide = heats * SUB
    total = lax.fori_loop(
        0, lons // chunk, second, jnp.zeros((4 * waves, 2 * wide), jnp.float32)
    )
    heat[...] = jnp.zeros_like(heat)
    heat[:, 0 : 2 * wide] = total
    total = heat[...]
    half = 2 * waves
    total = total[:half] + total[half:] + pltpu.roll(total[:half], LANES - wide, 1)
    lane = lax.broadcasted_iota(jnp.int32, (waves, LANES), 1)
    sent_ref[...] = (
        jnp.where(
            lane < LANES // 2, total[:waves], pltpu.roll(total[waves:], LANES // 2, 1)
        )
        * (1.0 / math.sqrt(lons))
    )


def spectra_kernel(band, heats, waves_ref, received_ref, quad_ref, legendre_ref, out_ref, spread):
    lats, degrees = legendre_ref.shape
    places = received_ref.shape[0]
    margin = (SUB - band) // 2
    place = lax.axis_index(PLACE)
    limit = degrees - waves_ref[place]
    received = received_ref[...]
    for r in range(band):
        spread[pl.ds(r, places, stride=band), :] = pltpu.roll(received, LANES - margin - r, 1)
    weighted = (spread[...].T * quad_ref[...]).astype(jnp.bfloat16)
    out = jnp.dot(weighted, legendre_ref[...], preferred_element_type=jnp.float32)
    keep = lax.broadcasted_iota(jnp.int32, (1, degrees), 1) < limit
    for p in range(2):
        for k in range(heats):
            at = p * (LANES // 2) + k * SUB
            out_ref[p, k, 0] = jnp.where(keep, out[at : at + 1], 0.0)


def body(spectra, legendre, wavenumbers, quad_weights, tracers, kinetics, photolysis, heat_weights):
    places = lax.axis_size(PLACE)
    levels = lax.axis_size("lev")
    count, _, band, lons = tracers.shape
    waves = wavenumbers.shape[0]
    heats = heat_weights.shape[0]
    lats, degrees = legendre.shape[2], legendre.shape[1]
    width = (SUB - band) // 2
    f32 = jnp.float32
    VM, SM = pltpu.VMEM, pltpu.SMEM
    legendre_t = legendre[0].T
    own = tracers[:, 0]

    edge = jax.ShapeDtypeStruct((count, width, lons), f32)
    near, far = call(functools.partial(halo_kernel, width), (edge, edge), [VM])(own)
    near = lax.ppermute(near, PLACE, [(i, i ^ 1) for i in range(places)])
    far = lax.ppermute(
        far, PLACE, [(i, ((i + 1) ^ 1) - 1) for i in range(1, places - 1)]
    )
    sent = call(
        fourier_kernel,
        jax.ShapeDtypeStruct((places, LANES), f32),
        [SM, VM, VM],
        [pltpu.VMEM((lats + 2 * SUB, LANES), f32)],
    )(wavenumbers, spectra[:, :, 0, 0], legendre_t)
    received = lax.all_to_all(sent, PLACE, 0, 0, tiled=True)

    padded, column = call(
        band_kernel,
        (
            jax.ShapeDtypeStruct((count, SUB, lons + 2 * LANES), f32),
            jax.ShapeDtypeStruct((SUB, lons), f32),
        ),
        [VM, VM, VM],
    )(own, near, far)
    overhead = lax.ppermute(column, "lev", [(i, i + 1) for i in range(levels - 1)])
    reach = 1
    while reach < levels - 1:
        overhead = overhead + lax.ppermute(
            overhead, "lev", [(i, i + reach) for i in range(levels - reach)]
        )
        reach *= 2
    table = call(
        table_kernel, jax.ShapeDtypeStruct((4 * waves, lons), jnp.bfloat16), [SM]
    )(wavenumbers)

    tracers_out, heat_sent = call(
        functools.partial(grid_kernel, levels, band),
        (
            jax.ShapeDtypeStruct((count, band, lons), f32),
            jax.ShapeDtypeStruct((waves, LANES), f32),
        ),
        [SM, SM, SM, VM, VM, VM, VM],
        [
            pltpu.VMEM((count, SUB, lons + 2 * LANES), f32),
            pltpu.VMEM((8, SUB, lons), f32),
            pltpu.VMEM((4 * waves, LANES), f32),
        ],
    )(kinetics, photolysis, heat_weights, received, padded, overhead, table)
    heat_received = lax.all_to_all(heat_sent, PLACE, 0, 0, tiled=True)
    heating_spectra = call(
        functools.partial(spectra_kernel, band, heats),
        jax.ShapeDtypeStruct((2, heats, 1, 1, degrees), f32),
        [SM, VM, VM, VM],
        [pltpu.VMEM((lats, LANES), f32)],
    )(wavenumbers, heat_received, quad_weights.reshape(1, lats), legendre_t)
    return (tracers_out[:, None], heating_spectra)


def solution(mesh):
    return jax.shard_map(
        body,
        mesh=mesh,
        in_specs=(
            P(None, None, "lev", ("wave", "grp"), None),
            P(("wave", "grp"), None, None),
            P(),
            P(),
            P(None, "lev", ("wave", "grp"), None),
            P(),
            P(),
            P(),
        ),
        out_specs=(
            P(None, "lev", ("wave", "grp"), None),
            P(None, None, "lev", ("wave", "grp"), None),
        ),
        check_vma=False,
    )
```

time: 57.4 us -> 51.1 us (0.89)
  Pallas kernels: 0 us -> 14.3 us
  local copies, waits for them, and re-layouts: 9.02 us -> 1.07 us
  starting transfers between devices: 25 us -> 19.9 us
  matrix products: 4.69 us -> 0 us
  blocking collectives: 4.93 us -> 8.97 us
  waiting for transfers between devices: 9.7 us -> 5.93 us
  other arithmetic: 1.94 us -> 0 us
  between operations: 1.58 us -> 0.75 us
    pallas_call x0 -> x6, Pallas kernels: none -> 14.3 us  [the longest x1 10.2 us: body(): call(functools.partial(grid_kernel, levels, band), (jax.ShapeDtypeStruct(...]
    all_to_all x0 -> x1, blocking collectives: none -> 8.97 us  [body(): heat_received = lax.all_to_all(heat_sent, PLACE, 0, 0, tiled=True)]
    all_gather x1 -> x0, blocking collectives: 4.93 us -> none  [prefix(): gathered = lax.all_gather(part, axis)]
    dot_general x7 -> x0, matrix products: 4.69 us -> none  [the longest x1 1.95 us: body(): jnp.einsum('kyx,psx->pksy', heating, shared_table, precision=highest)]
    ppermute x4 -> x3, waiting for transfers between devices: 4.26 us -> 0.49 us  [the longest x1 0.49 us: body(): near = lax.ppermute(near, PLACE, [(i, i ^ 1) for i in range(places)])]
    unnamed x19 -> x16, local copies, waits for them, and re-layouts: 4.62 us -> 1.07 us
    all_to_all x2 -> x1, starting transfers between devices: 17.1 us -> 13.9 us  [body(): received = lax.all_to_all(sent, PLACE, 0, 0, tiled=True)]
    ppermute x4 -> x3, starting transfers between devices: 7.92 us -> 5.98 us  [the longest x1 4.8 us: body(): lax.ppermute(column, 'lev', [(i, i + 1) for i in range(levels - 1)])]
  transfers between devices with their start and end apart: 6 -> 4, of which waited for: 2 -> 2; matrix products, arithmetic and copies ran while one was open for 9% -> 0% of each run, Pallas kernels for 0% -> 4%
where the time goes in v1:
time: 51.1 us; the launch traced here: 50.8 us
  starting transfers between devices  19.9 us (39%)
  Pallas kernels  14.3 us (28%)
  blocking collectives  8.97 us (18%)
  waiting for transfers between devices  5.93 us (12%)
  local copies, waits for them, and re-layouts  1.07 us (2%)
  between operations  0.75 us (1%)
    all_to_all x1, starting transfers between devices, body(): received = lax.all_to_all(sent, PLACE, 0, 0, tiled=True)  13.9 us
    pallas_call x1, Pallas kernels, body(): call(functools.partial(grid_kernel, levels, band), (jax.ShapeDtypeStruct(...  10.2 us
    all_to_all x1, blocking collectives, body(): heat_received = lax.all_to_all(heat_sent, PLACE, 0, 0, tiled=True)  8.97 us
    all_to_all x1, waiting for transfers between devices, body(): received = lax.all_to_all(sent, PLACE, 0, 0, tiled=True)  5.44 us
    ppermute x1, starting transfers between devices, body(): lax.ppermute(column, 'lev', [(i, i + 1) for i in range(levels - 1)])  4.8 us
    pallas_call x1, Pallas kernels, body(): call(functools.partial(spectra_kernel, band, heats), jax.ShapeDtypeStruct...  1.49 us
    pallas_call x1, Pallas kernels, body(): call(fourier_kernel, jax.ShapeDtypeStruct((places, LANES), f32), [SM, VM,...  1.34 us
    unnamed x16, local copies, waits for them, and re-layouts  1.07 us
  transfers between devices with their start and end apart: 4, of which 2 were waited for; matrix products, arithmetic and copies ran while one was open for 0% of the time, Pallas kernels for 4%

profile of v1, /device:TPU:0, one launch (start us, length us, event | category | flops | bytes accessed | tf_op | source)
XLA Modules:
  0.0 50.8 jit_solution(8482773231156602892)
XLA Ops:
  0.6 0.0 copy-start.3
  0.6 0.0 copy-start
  0.7 1.0 %copy-done = f32[8,1,4,4096]{3,2,1,0:T(4,128)S(1)} copy-done((f32[8,1,4,4096]{3,2,1,0:T(4,128)S(1)}, f32[8,1,4,4096]{3,2,1,0:T(4,128)}, u32[]{:S(2)}) %copy-start) | copy-done | bytes 524312
  1.7 0.0 copy-start.1
  1.7 0.0 copy-start.2
  1.7 0.0 copy-start.4
  1.7 0.0 copy-start.5
  1.7 0.0 copy-start.6
  1.7 0.2 shard_map.96
  1.9 0.5 %collective-permute-start = (f32[8,2,4096]{2,1,0:T(2,128)S(1)}, f32[8,2,4096]{2,1,0:T(2,128)S(1)}, u32[]{:S(2)}, u32[]{:S(2)}) collective-permute-start(f32[8,2,4096]{2,1,0:T(2,128)S(1)} %get-tuple-element.8), channel_id=1, source_target_pairs={{0,1},{1,0},{2,3},{3,2},{8,9},{9,8},{10,11},{11,10},{16,17},{17,16... | collective-permute-start | bytes 786440 | tf_op jit(solution)/shard_map/ppermute | solution.py:292
  2.4 0.7 %collective-permute-start.1 = (f32[8,2,4096]{2,1,0:T(2,128)S(1)}, f32[8,2,4096]{2,1,0:T(2,128)S(1)}, u32[]{:S(2)}, u32[]{:S(2)}) collective-permute-start(f32[8,2,4096]{2,1,0:T(2,128)S(1)} %get-tuple-element.9), channel_id=1, source_target_pairs={{1,2},{2,1},{3,8},{8,3},{9,10},{10,9},{11,16},{16,11},{17,18},{18,... | collective-permute-start | bytes 786440 | tf_op jit(solution)/shard_map/ppermute | solution.py:293
  3.1 0.5 collective-permute-done.near_ref
  3.6 0.0 collective-permute-done.1.far_ref
  3.6 0.2 shard_map.97
  3.8 4.8 %collective-permute-start.2 = (f32[8,4096]{1,0:T(8,128)S(1)}, f32[8,4096]{1,0:T(8,128)S(1)}, u32[]{:S(2)}, u32[]{:S(2)}) collective-permute-start(f32[8,4096]{1,0:T(8,128)S(1)} %get-tuple-element.11), channel_id=1, source_target_pairs={{0,4},{1,5},{2,6},{3,7},{8,12},{9,13},{10,14},{11,15},{16,20},{17,... | collective-permute-start | bytes 393224 | tf_op jit(solution)/shard_map/ppermute | solution.py:312
  8.6 0.0 copy-done.3
  8.6 0.0 copy-done.1
  8.6 0.0 copy-done.2
  8.6 1.3 %shard_map.95 = f32[16,128]{1,0:T(8,128)} custom-call(s32[16]{0:T(128)S(1)} %copy-done.3, bf16[2,4,1024]{2,1,0:T(4,128)(2,1)S(1)} %bitcast.23, bf16[64,1024]{1,0:T(8,128)(2,1)S(1)} %bitcast.19), custom_call_target="tpu_custom_call" | custom-call | flops 1000000 | tf_op jit(solution)/shard_map/pallas_call | solution.py:296
  10.0 13.9 %all-to-all-start = ((f32[16,1,128]{2,1,0:T(1,128)}), f32[16,1,128]{2,1,0:T(1,128)S(1)}, u32[]{:S(2)}, u32[]{:S(2)}) async-start(f32[16,1,128]{2,1,0:T(1,128)} %bitcast.4), calls=%async_computation | async-start | bytes 16384 | tf_op jit(solution)/shard_map/all_to_all | solution.py:302
  23.9 0.0 copy-start.7
  23.9 0.9 %shard_map.98.table_ref = bf16[64,4096]{1,0:T(8,128)(2,1)S(1)} custom-call(s32[16]{0:T(128)S(1)} %copy-done.3), custom_call_target="tpu_custom_call" | custom-call | flops 1000000 | tf_op jit(solution)/shard_map/pallas_call | solution.py:319
  24.7 5.4 %all-to-all-done = f32[16,1,128]{2,1,0:T(1,128)S(1)} async-done(((f32[16,1,128]{2,1,0:T(1,128)}), f32[16,1,128]{2,1,0:T(1,128)S(1)}, u32[]{:S(2)}, u32[]{:S(2)}) %all-to-all-start) | async-done | bytes 8224 | tf_op jit(solution)/shard_map/all_to_all | solution.py:302
  30.2 0.0 collective-permute-done.2.overhead_ref
  30.2 0.0 copy-done.4
  30.2 0.0 copy-done.5
  30.2 0.0 copy-done.6
  30.2 10.2 %shard_map.99 = (f32[8,4,4096]{2,1,0:T(4,128)}, f32[16,128]{1,0:T(8,128)S(1)}) custom-call(f32[8,8]{1,0:T(8,128)S(1)} %copy-done.4, f32[8]{0:T(128)S(1)} %copy-done.6, f32[3,8]{1,0:T(4,128)S(1)} %copy-done.5, f32[16,128]{1,0:T(8,128)S(1)} %bitcast.21, f32[8,8,4352]{2,1,0:T(8,128)S(1)} %get-tuple-element.10.padded_ref, ...), custom_call_target="tpu_custom_call" | custom-call | flops 1000000 | tf_op jit(solution)/shard_map/pallas_call | solution.py:323
  40.4 9.0 %all_to_all.22 = f32[16,1,128]{2,1,0:T(1,128)S(1)} all-to-all(f32[16,1,128]{2,1,0:T(1,128)S(1)} %bitcast.24), channel_id=1, replica_groups=mesh['wave'=4,'lev'=2,'grp'=4] {'wave','grp'}, dimensions={0} | all-to-all | bytes 16384 | tf_op jit(solution)/shard_map/all_to_all | solution.py:336
  49.3 0.0 copy-done.7
  49.3 1.5 %shard_map.100 = f32[2,3,1,1,1024]{4,3,2,1,0:T(1,128)} custom-call(s32[16]{0:T(128)S(1)} %copy-done.3, f32[16,128]{1,0:T(8,128)S(1)} %bitcast.22, f32[1,64]{1,0:T(1,128)S(1)} %bitcast.25, bf16[64,1024]{1,0:T(8,128)(2,1)S(1)} %bitcast.20), custom_call_target="tpu_custom_call" | custom-call | flops 1000000 | tf_op jit(solution)/shard_map/pallas_call | solution.py:337
Async XLA Ops:
  0.6 8.0 %copy-start.3 = (s32[16]{0:T(128)S(1)}, s32[16]{0:T(128)}, u32[]{:S(2)}) copy-start(s32[16]{0:T(128)} %waves_ref.5) | copy-start | bytes 196
  0.6 1.0 %copy-start = (f32[8,1,4,4096]{3,2,1,0:T(4,128)S(1)}, f32[8,1,4,4096]{3,2,1,0:T(4,128)}, u32[]{:S(2)}) copy-start(f32[8,1,4,4096]{3,2,1,0:T(4,128)} %param.12) | copy-start | bytes 1572868
  1.7 6.9 %copy-start.1 = (bf16[1,1024,64]{1,2,0:T(8,128)(2,1)S(1)}, bf16[1,1024,64]{1,2,0:T(8,128)(2,1)}, u32[]{:S(2)}) copy-start(bf16[1,1024,64]{1,2,0:T(8,128)(2,1)} %param.9) | copy-start | bytes 393220
  1.7 6.9 %copy-start.2 = (bf16[2,4,1,1,1024]{4,1,3,2,0:T(4,128)(2,1)S(1)}, bf16[2,4,1,1,1024]{4,1,3,2,0:T(4,128)(2,1)}, u32[]{:S(2)}) copy-start(bf16[2,4,1,1,1024]{4,1,3,2,0:T(4,128)(2,1)} %param.8) | copy-start | bytes 49156
  1.7 28.5 %copy-start.4 = (f32[8,8]{1,0:T(8,128)S(1)}, f32[8,8]{1,0:T(8,128)}, u32[]{:S(2)}) copy-start(f32[8,8]{1,0:T(8,128)} %kinetics_ref.1) | copy-start | bytes 772
  1.7 28.5 %copy-start.5 = (f32[3,8]{1,0:T(4,128)S(1)}, f32[3,8]{1,0:T(4,128)}, u32[]{:S(2)}) copy-start(f32[3,8]{1,0:T(4,128)} %weights_ref.1) | copy-start | bytes 292
  1.7 28.5 %copy-start.6 = (f32[8]{0:T(128)S(1)}, f32[8]{0:T(128)}, u32[]{:S(2)}) copy-start(f32[8]{0:T(128)} %photolysis_ref.1) | copy-start | bytes 100
  1.9 1.7 %collective-permute-start = (f32[8,2,4096]{2,1,0:T(2,128)S(1)}, f32[8,2,4096]{2,1,0:T(2,128)S(1)}, u32[]{:S(2)}, u32[]{:S(2)}) collective-permute-start(f32[8,2,4096]{2,1,0:T(2,128)S(1)} %get-tuple-element.8), channel_id=1, source_target_pairs={{0,1},{1,0},{2,3},{3,2},{8,9},{9,8},{10,11},{11,10},{16,17},{17,16... | collective-permute-start | bytes 786440 | tf_op jit(solution)/shard_map/ppermute | solution.py:292
  2.4 1.2 %collective-permute-start.1 = (f32[8,2,4096]{2,1,0:T(2,128)S(1)}, f32[8,2,4096]{2,1,0:T(2,128)S(1)}, u32[]{:S(2)}, u32[]{:S(2)}) collective-permute-start(f32[8,2,4096]{2,1,0:T(2,128)S(1)} %get-tuple-element.9), channel_id=1, source_target_pairs={{1,2},{2,1},{3,8},{8,3},{9,10},{10,9},{11,16},{16,11},{17,18},{18,... | collective-permute-start | bytes 786440 | tf_op jit(solution)/shard_map/ppermute | solution.py:293
  3.8 26.4 %collective-permute-start.2 = (f32[8,4096]{1,0:T(8,128)S(1)}, f32[8,4096]{1,0:T(8,128)S(1)}, u32[]{:S(2)}, u32[]{:S(2)}) collective-permute-start(f32[8,4096]{1,0:T(8,128)S(1)} %get-tuple-element.11), channel_id=1, source_target_pairs={{0,4},{1,5},{2,6},{3,7},{8,12},{9,13},{10,14},{11,15},{16,20},{17,... | collective-permute-start | bytes 393224 | tf_op jit(solution)/shard_map/ppermute | solution.py:312
  10.0 20.2 %all-to-all-start = ((f32[16,1,128]{2,1,0:T(1,128)}), f32[16,1,128]{2,1,0:T(1,128)S(1)}, u32[]{:S(2)}, u32[]{:S(2)}) async-start(f32[16,1,128]{2,1,0:T(1,128)} %bitcast.4), calls=%async_computation | async-start | bytes 16384 | tf_op jit(solution)/shard_map/all_to_all | solution.py:302
  23.9 25.5 %copy-start.7 = (f32[64]{0:T(128)S(1)}, f32[64]{0:T(128)}, u32[]{:S(2)}) copy-start(f32[64]{0:T(128)} %param.11) | copy-start | bytes 772

commit v2 on v0

v2 whole, which is shorter than its diff:
```python
import functools
import math

import jax
import jax.numpy as jnp
from jax import lax
from jax.experimental import pallas as pl
from jax.experimental.pallas import tpu as pltpu
from jax.sharding import PartitionSpec as P

LANES = 128
SUB = 8
PLACE = ("wave", "grp")
VMEM_BYTES = 48 * 1024 * 1024
f32 = jnp.float32
bf16 = jnp.bfloat16


def split_bf16(value):
    high = value.astype(bf16)
    return high, value - high.astype(f32)


def call(body, out_shape, in_spaces, scratch=(), flops=1_000_000):
    several = isinstance(out_shape, (list, tuple))
    spec = pl.BlockSpec(memory_space=pltpu.VMEM)
    return pl.pallas_call(
        body,
        out_shape=out_shape,
        in_specs=[pl.BlockSpec(memory_space=s) for s in in_spaces],
        out_specs=[spec] * len(out_shape) if several else spec,
        scratch_shapes=list(scratch),
        compiler_params=pltpu.CompilerParams(vmem_limit_bytes=VMEM_BYTES),
        cost_estimate=pl.CostEstimate(flops=flops, bytes_accessed=0, transcendentals=0),
    )


def fold(tracers):
    count, band, lons = tracers.shape
    cut = tracers.reshape(count, band, lons // LANES, LANES)
    return cut.transpose(0, 2, 1, 3).reshape(-1, LANES)


def unfold(flat, count, band):
    cut = flat.reshape(count, -1, band, LANES)
    return cut.transpose(0, 2, 1, 3).reshape(count, band, -1)


def row_slices(flat_rows, count, band, t, r):
    each = flat_rows // count
    wide = each // band // SUB
    return [pl.ds(t * each + j * band + r, SUB, stride=wide * band) for j in range(wide)]


def load_row(ref, count, band, t, r):
    parts = [ref[s, :] for s in row_slices(ref.shape[0], count, band, t, r)]
    return jnp.concatenate(parts, axis=1)


def store_row(ref, count, band, t, r, value):
    for j, s in enumerate(row_slices(ref.shape[0], count, band, t, r)):
        ref[s, :] = value[:, j * LANES : (j + 1) * LANES]


def shift(row, forward):
    span = row.shape[1]
    lane = lax.broadcasted_iota(jnp.int32, row.shape, 1)
    if forward:
        moved = pltpu.roll(row, 1, 1)
        edge = pltpu.roll(moved[:, :LANES], 1, 0)
        head = jnp.where(lane[:, :LANES] == 0, edge, moved[:, :LANES])
        return jnp.concatenate([head, moved[:, LANES:]], axis=1)
    moved = pltpu.roll(row, span - 1, 1)
    edge = pltpu.roll(moved[:, span - LANES :], SUB - 1, 0)
    last = lane[:, :LANES] == LANES - 1
    tail = jnp.where(last, edge, moved[:, span - LANES :])
    return jnp.concatenate([moved[:, : span - LANES], tail], axis=1)


def fourier_kernel(waves_ref, spectra_ref, legendre_ref, out_ref, padded):
    parts, fields, degrees = spectra_ref.shape
    lats = legendre_ref.shape[0]
    places = out_ref.shape[0]
    band = lats // places
    margin = (SUB - band) // 2
    place = lax.axis_index(PLACE)
    limit = degrees - waves_ref[place]
    keep = lax.broadcasted_iota(jnp.int32, (SUB, degrees), 1) < limit
    rows = []
    for p in range(parts):
        block = spectra_ref[p].astype(f32)
        for f in range(fields):
            row = jnp.broadcast_to(block[f : f + 1], (SUB, degrees))
            rows.append(jnp.where(keep, row, 0.0))
    spread = jnp.concatenate(rows, axis=0).astype(bf16)
    fourier = lax.dot_general(
        legendre_ref[...], spread, (((1,), (1,)), ((), ())), preferred_element_type=f32
    )
    width = fourier.shape[1]
    padded[...] = jnp.zeros_like(padded)
    padded[SUB : SUB + lats, :width] = fourier
    lane = lax.broadcasted_iota(jnp.int32, (places, LANES), 1) % SUB
    total = jnp.zeros((places, LANES), f32)
    for r in range(SUB):
        rows_r = padded[pl.ds(SUB - margin + r, places, stride=band), :]
        total = jnp.where(lane == r, rows_r, total)
    out_ref[...] = total


def edges_kernel(count, band, width, flat_ref, near_ref, far_ref, near_top_ref, far_top_ref):
    even = lax.axis_index(PLACE) % 2 == 0

    def fill(near_first, far_first, near_edge, far_edge):
        for t in range(count):
            for r in range(width):
                near_ref[t, r] = load_row(flat_ref, count, band, t, near_first + r)
                far_ref[t, r] = load_row(flat_ref, count, band, t, far_first + r)
        near_top_ref[...] = load_row(flat_ref, count, band, 0, near_edge)
        far_top_ref[...] = load_row(flat_ref, count, band, 0, far_edge)

    @pl.when(even)
    def _():
        fill(band - width, 0, band - 1, 0)

    @pl.when(jnp.logical_not(even))
    def _():
        fill(0, band - width, 0, band - 1)


def table_kernel(waves_ref, table_ref, turn_ref):
    span = table_ref.shape[1]
    waves = table_ref.shape[0] // 8
    lons = span * SUB
    row = lax.broadcasted_iota(jnp.int32, (waves, LANES), 0)
    column = lax.broadcasted_iota(jnp.int32, (waves, LANES), 1)
    numbers = jnp.zeros((waves, LANES), jnp.int32)
    wide = 8 * waves
    slot = lax.broadcasted_iota(jnp.int32, (SUB, wide), 1) % waves
    by_lane = jnp.zeros((SUB, wide), jnp.int32)
    for s in range(waves):
        numbers = jnp.where(row == s, waves_ref[s], numbers)
        by_lane = jnp.where(slot == s, waves_ref[s], by_lane)

    def wheel(product):
        angle = (product % lons).astype(f32) * (2.0 * math.pi / lons)
        return jnp.cos(angle), jnp.sin(angle)

    sub = lax.broadcasted_iota(jnp.int32, (SUB, wide), 0)
    turn_ref[0], turn_ref[1] = wheel(by_lane * sub * span)

    blocks = [wheel(numbers * column)]
    while len(blocks) * LANES < span:
        step_cos, step_sin = wheel(numbers * (len(blocks) * LANES))
        blocks += [(c * step_cos - s * step_sin, s * step_cos + c * step_sin) for c, s in blocks]
    for b, (cosine, sine) in enumerate(blocks[: span // LANES]):
        columns = slice(b * LANES, (b + 1) * LANES)
        both = split_bf16(cosine) + split_bf16(-sine)
        for n, part in enumerate((0, 2, 1, 3) * 2):
            table_ref[n * waves : (n + 1) * waves, columns] = both[part].astype(bf16)


def ready_kernel(
    levels,
    count,
    band,
    flat_ref,
    near_ref,
    far_ref,
    above_ref,
    near_top_ref,
    far_top_ref,
    cells_ref,
    west_ref,
    east_ref,
    photo_ref,
):
    even = lax.axis_index(PLACE) % 2 == 0
    width = near_ref.shape[1]

    def fill(north, south, north_top, south_top):
        for t in range(count):
            rows = [north[t, r] for r in range(width)]
            rows += [load_row(flat_ref, count, band, t, r) for r in range(band)]
            rows += [south[t, r] for r in range(width)]
            for r, row in enumerate(rows):
                cells_ref[t, r] = row
            for r in range(band + 2):
                row = rows[r + width - 1]
                west_ref[t, r] = shift(row, True)
                east_ref[t, r] = shift(row, False)
        above = [north_top[...]]
        above += [load_row(above_ref, 1, band, 0, r) for r in range(band)]
        above += [south_top[...]]
        for r, row in enumerate(above):
            photo_ref[r] = 0.2 * jnp.exp(row * (-2.0 / levels))

    @pl.when(even)
    def _():
        fill(far_ref, near_ref, far_top_ref, near_top_ref)

    @pl.when(jnp.logical_not(even))
    def _():
        fill(near_ref, far_ref, near_top_ref, far_top_ref)


def grid_kernel(
    kinetics_ref,
    photolysis_ref,
    weights_ref,
    received_ref,
    cells_ref,
    west_ref,
    east_ref,
    photo_ref,
    table_ref,
    turn_ref,
    flat_ref,
    sent_ref,
    middle,
    coeffs,
):
    count, depth, _, span = cells_ref.shape
    rows = west_ref.shape[1]
    band = rows - 2
    margin = (SUB - band) // 2
    halo = (depth - band) // 2
    waves = table_ref.shape[0] // 8
    heats = weights_ref.shape[0]
    fields = 4
    lons = span * SUB
    place = lax.axis_index(PLACE)
    places = lax.axis_size(PLACE)

    lane = lax.broadcasted_iota(jnp.int32, (SUB, 8 * waves), 1)
    real = (lane // waves) % 2 == 0
    turn_cos, turn_sin = turn_ref[0], turn_ref[1]
    scale = 1.0 / math.sqrt(waves)
    turn_a = jnp.where(real, turn_cos, turn_sin) * scale
    turn_b = jnp.where(real, -turn_sin, turn_cos) * scale
    turned = jnp.concatenate([received_ref[...]] * 8, axis=0).T
    wanted = [(f, r) for f in range(fields - 1) for r in range(-1, band + 1)]
    wanted += [(fields - 1, r) for r in range(band)]
    left = []
    for f, r in wanted:
        at = f * SUB + margin + r
        re = turned[at : at + 1]
        im = turned[fields * SUB + at : fields * SUB + at + 1]
        left.append(re * turn_a + im * turn_b)
    left = jnp.concatenate(left, axis=0)
    high, low = split_bf16(left)
    whole_lane = lax.broadcasted_iota(jnp.int32, left.shape, 1)
    left = jnp.where(whole_lane < 4 * waves, high.astype(f32), low).astype(bf16)
    grid = jnp.dot(left, table_ref[...], preferred_element_type=f32)

    for r in range(rows):
        across = grid[r * SUB : (r + 1) * SUB]
        along = grid[(rows + r) * SUB : (rows + r + 1) * SUB]
        warmth = grid[(2 * rows + r) * SUB : (2 * rows + r + 1) * SUB]
        courant_x = 0.45 * jnp.tanh(across)
        courant_y = 0.45 * jnp.tanh(along)
        own = 1.0 - jnp.abs(courant_x) - jnp.abs(courant_y)
        if r == 0 or r == rows - 1:
            inside = (place > 0) if r == 0 else (place < places - 1)
            courant_x = jnp.where(inside, courant_x, 0.0)
            courant_y = jnp.where(inside, courant_y, 0.0)
            own = jnp.where(inside, own, 0.0)
        coeffs[0, r] = own
        coeffs[1, r] = jnp.maximum(courant_x, 0.0)
        coeffs[2, r] = -jnp.minimum(courant_x, 0.0)
        coeffs[3, r] = jnp.maximum(courant_y, 0.0)
        coeffs[4, r] = -jnp.minimum(courant_y, 0.0)
        coeffs[5, r] = 0.2 * jnp.exp(0.3 * warmth)

    def react(moved, r):
        lit = photo_ref[r] * moved[0]
        rate = coeffs[5, r]
        out = []
        for i in range(count):
            mixed = kinetics_ref[i, 0] * moved[0]
            for j in range(1, count):
                mixed = mixed + kinetics_ref[i, j] * moved[j]
            out.append(moved[i] + rate * mixed + photolysis_ref[i] * lit)
        return out

    for r in range(rows):
        moved = []
        for t in range(count):
            at = r + halo - 1
            moved.append(
                coeffs[0, r] * cells_ref[t, at]
                + coeffs[1, r] * west_ref[t, r]
                + coeffs[2, r] * east_ref[t, r]
                + coeffs[3, r] * cells_ref[t, at - 1]
                + coeffs[4, r] * cells_ref[t, at + 1]
            )
        for t, value in enumerate(react(moved, r)):
            middle[t, r] = value

    first = 3 * rows * SUB
    heated = [[None] * band for _ in range(heats)]
    for r in range(band):
        moved = []
        for t in range(count):
            row = middle[t, r + 1]
            moved.append(
                coeffs[0, r + 1] * row
                + coeffs[1, r + 1] * shift(row, True)
                + coeffs[2, r + 1] * shift(row, False)
                + coeffs[3, r + 1] * middle[t, r]
                + coeffs[4, r + 1] * middle[t, r + 2]
            )
        out = react(moved, r + 1)
        for t in range(count):
            store_row(flat_ref, count, band, t, r, out[t])
        warm = 1.0 + 0.5 * jnp.tanh(grid[first + r * SUB : first + (r + 1) * SUB])
        for k in range(heats):
            total = weights_ref[k, 0] * out[0]
            for i in range(1, count):
                total = total + weights_ref[k, i] * out[i]
            heated[k][r] = total * warm

    heat = jnp.concatenate([row for group in heated for row in group], axis=0)
    high, low = split_bf16(heat)
    nt = (((1,), (1,)), ((), ()))
    by_high = lax.dot_general(high, table_ref[...], nt, preferred_element_type=f32)
    by_low = lax.dot_general(low.astype(bf16), table_ref[...], nt, preferred_element_type=f32)
    wide = 8 * waves
    total = by_high + pltpu.roll(by_high, wide - 2 * waves, 1) + by_low
    sums_a, sums_b = [], []
    for n in range(heats * band):
        part = total[n * SUB : (n + 1) * SUB]
        sums_a.append(jnp.sum(part * turn_cos, axis=0, keepdims=True))
        sums_b.append(jnp.sum(part * turn_sin, axis=0, keepdims=True))
    pad = -len(sums_a) % SUB
    sums_a += [jnp.zeros_like(sums_a[0])] * pad
    sums_b += [jnp.zeros_like(sums_b[0])] * pad
    sums_a = jnp.concatenate(sums_a, axis=0)
    sums_b = jnp.concatenate(sums_b, axis=0)
    other = pltpu.roll(sums_b, wide - waves, 1)
    re = sums_a + other
    im = pltpu.roll(sums_a, wide - waves, 1) - sums_b
    size = re.shape[0]
    filler = jnp.zeros((LANES // 2 - size, wide), f32)
    both = jnp.concatenate([re, filler, im, filler], axis=0) * (1.0 / math.sqrt(lons))
    sent_ref[...] = both.T[:waves]


def spectra_kernel(band, heats, waves_ref, received_ref, quad_ref, legendre_ref, out_ref, spread):
    lats, degrees = legendre_ref.shape
    places = received_ref.shape[0]
    place = lax.axis_index(PLACE)
    limit = degrees - waves_ref[place]
    received = received_ref[...]
    for r in range(band):
        spread[pl.ds(r, places, stride=band), :] = pltpu.roll(received, (LANES - r) % LANES, 1)
    weighted = (spread[...].T * quad_ref[...]).astype(bf16)
    out = jnp.dot(weighted, legendre_ref[...], preferred_element_type=f32)
    keep = lax.broadcasted_iota(jnp.int32, (1, degrees), 1) < limit
    for p in range(2):
        for k in range(heats):
            at = p * (LANES // 2) + k * band
            out_ref[p, k, 0] = jnp.where(keep, out[at : at + 1], 0.0)


def body(spectra, legendre, wavenumbers, quad_weights, tracers, kinetics, photolysis, heat_weights):
    places = lax.axis_size(PLACE)
    levels = lax.axis_size("lev")
    count, _, band, lons = tracers.shape
    waves = wavenumbers.shape[0]
    heats = heat_weights.shape[0]
    lats, degrees = legendre.shape[2], legendre.shape[1]
    width = 2
    span = lons // SUB
    flat_rows = count * band * lons // LANES
    VM, SM = pltpu.VMEM, pltpu.SMEM
    legendre_t = legendre[0].T
    flat = fold(tracers[:, 0])
    shape = jax.ShapeDtypeStruct

    near_pairs = [(i, i ^ 1) for i in range(places)]
    far_pairs = [(i, ((i + 1) ^ 1) - 1) for i in range(1, places - 1)]

    near, far, near_top, far_top = call(
        functools.partial(edges_kernel, count, band, width),
        [shape((count, width, SUB, span), f32)] * 2 + [shape((SUB, span), f32)] * 2,
        [VM],
    )(flat)
    near = lax.ppermute(near, PLACE, near_pairs)
    far = lax.ppermute(far, PLACE, far_pairs)

    own_top = flat[: flat_rows // count]
    if levels == 2:
        full = ("wave", "lev", "grp")
        grps = lax.axis_size("grp")

        def upward(pairs):
            def flat_index(place, level):
                return (place // grps * levels + level) * grps + place % grps

            return [(flat_index(a, 0), flat_index(b, 1)) for a, b in pairs]

        above = lax.ppermute(own_top, full, upward([(i, i) for i in range(places)]))
        near_top = lax.ppermute(near_top, full, upward(near_pairs))
        far_top = lax.ppermute(far_top, full, upward(far_pairs))
    else:

        def over(value):
            value = lax.ppermute(value, "lev", [(i, i + 1) for i in range(levels - 1)])
            reach = 1
            while reach < levels - 1:
                value = value + lax.ppermute(
                    value, "lev", [(i, i + reach) for i in range(levels - reach)]
                )
                reach *= 2
            return value

        above = over(own_top)
        near_top = over(lax.ppermute(near_top, PLACE, near_pairs))
        far_top = over(lax.ppermute(far_top, PLACE, far_pairs))

    sent = call(
        fourier_kernel,
        shape((places, LANES), f32),
        [SM, VM, VM],
        [pltpu.VMEM((lats + 2 * SUB, LANES), f32)],
    )(wavenumbers, spectra[:, :, 0, 0], legendre_t)
    received = lax.all_to_all(sent, PLACE, 0, 0, tiled=True)
    table, turn = call(
        table_kernel,
        [shape((8 * waves, span), bf16), shape((2, SUB, 8 * waves), f32)],
        [SM],
    )(wavenumbers)
    cells, west, east, photo = call(
        functools.partial(ready_kernel, levels, count, band),
        [
            shape((count, band + 2 * width, SUB, span), f32),
            shape((count, band + 2, SUB, span), f32),
            shape((count, band + 2, SUB, span), f32),
            shape((band + 2, SUB, span), f32),
        ],
        [VM] * 6,
    )(flat, near, far, above, near_top, far_top)

    flat_out, heat_sent = call(
        grid_kernel,
        [shape((flat_rows, LANES), f32), shape((waves, LANES), f32)],
        [SM] * 3 + [VM] * 7,
        [
            pltpu.VMEM((count, band + 2, SUB, span), f32),
            pltpu.VMEM((6, band + 2, SUB, span), f32),
        ],
    )(
        kinetics,
        photolysis,
        heat_weights,
        received,
        cells,
        west,
        east,
        photo,
        table,
        turn,
    )
    heat_received = lax.all_to_all(heat_sent, PLACE, 0, 0, tiled=True)
    heating_spectra = call(
        functools.partial(spectra_kernel, band, heats),
        shape((2, heats, 1, 1, degrees), f32),
        [SM, VM, VM, VM],
        [pltpu.VMEM((lats, LANES), f32)],
    )(wavenumbers, heat_received, quad_weights.reshape(1, lats), legendre_t)
    return (unfold(flat_out, count, band)[:, None], heating_spectra)


def solution(mesh):
    return jax.shard_map(
        body,
        mesh=mesh,
        in_specs=(
            P(None, None, "lev", ("wave", "grp"), None),
            P(("wave", "grp"), None, None),
            P(),
            P(),
            P(None, "lev", ("wave", "grp"), None),
            P(),
            P(),
            P(),
        ),
        out_specs=(
            P(None, "lev", ("wave", "grp"), None),
            P(None, None, "lev", ("wave", "grp"), None),
        ),
        check_vma=False,
    )
```

time: 57.4 us -> 50.4 us (0.88)
  waiting for transfers between devices: 9.7 us -> 0.02 us
  starting transfers between devices: 25 us -> 16.5 us
  Pallas kernels: 0 us -> 7.64 us
  blocking collectives: 4.93 us -> 12.2 us
  matrix products: 4.69 us -> 0 us
  local copies, waits for them, and re-layouts: 9.02 us -> 12.6 us
  other arithmetic: 1.94 us -> 0 us
  between operations: 1.58 us -> 0.78 us
    all_to_all x0 -> x1, blocking collectives: none -> 12.2 us  [body(): heat_received = lax.all_to_all(heat_sent, PLACE, 0, 0, tiled=True)]
    all_to_all x2 -> x1, starting transfers between devices: 17.1 us -> 6.51 us  [body(): received = lax.all_to_all(sent, PLACE, 0, 0, tiled=True)]
    unnamed x19 -> x44, local copies, waits for them, and re-layouts: 4.62 us -> 12.6 us
    pallas_call x0 -> x6, Pallas kernels: none -> 7.64 us  [the longest x1 3.47 us: body(): call(grid_kernel, [shape((flat_rows, LANES), f32), shape((waves, LANES),...]
    all_to_all x2 -> x1, waiting for transfers between devices: 5.45 us -> 0.01 us  [body(): received = lax.all_to_all(sent, PLACE, 0, 0, tiled=True)]
    all_gather x1 -> x0, blocking collectives: 4.93 us -> none  [prefix(): gathered = lax.all_gather(part, axis)]
    dot_general x7 -> x0, matrix products: 4.69 us -> none  [the longest x1 1.95 us: body(): jnp.einsum('kyx,psx->pksy', heating, shared_table, precision=highest)]
    ppermute x4 -> x5, waiting for transfers between devices: 4.26 us -> 0.01 us  [the longest x1 0.01 us: body(): near_top = lax.ppermute(near_top, full, upward(near_pairs))]
  transfers between devices with their start and end apart: 6 -> 6, of which waited for: 2 -> 0; matrix products, arithmetic and copies ran while one was open for 9% -> 0% of each run, Pallas kernels for 0% -> 5%
where the time goes in v2:
time: 50.4 us; the launch traced here: 49.8 us
  starting transfers between devices  16.5 us (33%)
  local copies, waits for them, and re-layouts  12.6 us (25%)
  blocking collectives  12.2 us (24%)
  Pallas kernels  7.64 us (15%)
  between operations  0.78 us (2%)
    unnamed x44, local copies, waits for them, and re-layouts  12.6 us
    all_to_all x1, blocking collectives, body(): heat_received = lax.all_to_all(heat_sent, PLACE, 0, 0, tiled=True)  12.2 us
    all_to_all x1, starting transfers between devices, body(): received = lax.all_to_all(sent, PLACE, 0, 0, tiled=True)  6.51 us
    ppermute x1, starting transfers between devices, body(): above = lax.ppermute(own_top, full, upward([(i, i) for i in range(places)]))  4.45 us
    ppermute x1, starting transfers between devices, body(): near_top = lax.ppermute(near_top, full, upward(near_pairs))  3.73 us
    pallas_call x1, Pallas kernels, body(): call(grid_kernel, [shape((flat_rows, LANES), f32), shape((waves, LANES),...  3.47 us
    pallas_call x1, Pallas kernels, body(): call(functools.partial(spectra_kernel, band, heats), shape((2, heats, 1,...  1.48 us
    pallas_call x1, Pallas kernels, body(): call(fourier_kernel, shape((places, LANES), f32), [SM, VM, VM], [pltpu.VM...  1.33 us
  transfers between devices with their start and end apart: 6, of which 0 were waited for; matrix products, arithmetic and copies ran while one was open for 0% of the time, Pallas kernels for 5%

profile of v2, /device:TPU:0, one launch (start us, length us, event | category | flops | bytes accessed | tf_op | source)
XLA Modules:
  0.0 49.8 jit_solution(18224063131558135007)
XLA Ops:
  0.6 0.0 copy-start
  0.6 1.0 %copy-done = f32[8,1,4,4096]{3,2,1,0:T(4,128)S(1)} copy-done((f32[8,1,4,4096]{3,2,1,0:T(4,128)S(1)}, f32[8,1,4,4096]{3,2,1,0:T(4,128)}, u32[]{:S(2)}) %copy-start) | copy-done | bytes 524312
  1.7 0.0 copy-start.1
  1.7 0.2 shard_map.96
  1.9 0.0 copy-start.2
  1.9 0.5 %collective-permute-start = (f32[8,2,8,512]{3,2,1,0:T(8,128)S(1)}, f32[8,2,8,512]{3,2,1,0:T(8,128)S(1)}, u32[]{:S(2)}, u32[]{:S(2)}) collective-permute-start(f32[8,2,8,512]{3,2,1,0:T(8,128)S(1)} %get-tuple-element.14), channel_id=1, source_target_pairs={{0,1},{1,0},{2,3},{3,2},{8,9},{9,8},{10,11},{11,10},{16,17},{17,16... | collective-permute-start | bytes 786440 | tf_op jit(solution)/shard_map/ppermute | solution.py:388
  2.4 0.7 %collective-permute-start.1 = (f32[8,2,8,512]{3,2,1,0:T(8,128)S(1)}, f32[8,2,8,512]{3,2,1,0:T(8,128)S(1)}, u32[]{:S(2)}, u32[]{:S(2)}) collective-permute-start(f32[8,2,8,512]{3,2,1,0:T(8,128)S(1)} %get-tuple-element.15), channel_id=1, source_target_pairs={{1,2},{2,1},{3,8},{8,3},{9,10},{10,9},{11,16},{16,11},{17,18},{18,... | collective-permute-start | bytes 786440 | tf_op jit(solution)/shard_map/ppermute | solution.py:389
  3.1 4.5 %collective-permute-start.2 = (f32[128,128]{1,0:T(8,128)S(1)}, f32[128,128]{1,0:T(8,128)S(1)}, u32[]{:S(2)}, u32[]{:S(2)}) collective-permute-start(f32[128,128]{1,0:T(8,128)S(1)} %bitcast.34), channel_id=1, source_target_pairs={{0,4},{1,5},{2,6},{3,7},{8,12},{9,13},{10,14},{11,15},{16,20},{17,... | collective-permute-start | bytes 196616 | tf_op jit(solution)/shard_map/ppermute | solution.py:402
  7.5 3.7 %collective-permute-start.3 = (f32[8,512]{1,0:T(8,128)S(1)}, f32[8,512]{1,0:T(8,128)S(1)}, u32[]{:S(2)}, u32[]{:S(2)}) collective-permute-start(f32[8,512]{1,0:T(8,128)S(1)} %get-tuple-element.16), channel_id=1, source_target_pairs={{0,5},{1,4},{2,7},{3,6},{8,13},{9,12},{10,15},{11,14},{16,21},{17,... | collective-permute-start | bytes 49160 | tf_op jit(solution)/shard_map/ppermute | solution.py:403
  11.3 0.7 %collective-permute-start.4 = (f32[8,512]{1,0:T(8,128)S(1)}, f32[8,512]{1,0:T(8,128)S(1)}, u32[]{:S(2)}, u32[]{:S(2)}) collective-permute-start(f32[8,512]{1,0:T(8,128)S(1)} %get-tuple-element.17), channel_id=1, source_target_pairs={{1,6},{2,5},{3,12},{8,7},{9,14},{10,13},{11,20},{16,15},{17,22},{1... | collective-permute-start | bytes 49160 | tf_op jit(solution)/shard_map/ppermute | solution.py:404
  11.9 0.0 copy-start.17
  12.0 0.0 copy-done.2
  12.0 0.6 %copy-done.17 = s32[16]{0:T(128)S(1)} copy-done((s32[16]{0:T(128)S(1)}, s32[16]{0:T(128)}, u32[]{:S(2)}) %copy-start.17) | copy-done | bytes 88
  12.6 0.0 copy-start.15
  12.6 0.7 %copy-done.15 = bf16[2,4,1,1,1024]{4,1,3,2,0:T(4,128)(2,1)S(1)} copy-done((bf16[2,4,1,1,1024]{4,1,3,2,0:T(4,128)(2,1)S(1)}, bf16[2,4,1,1,1024]{4,1,3,2,0:T(4,128)(2,1)}, u32[]{:S(2)}) %copy-start.15) | copy-done | bytes 16408
  13.3 1.3 %shard_map.95 = f32[16,128]{1,0:T(8,128)} custom-call(s32[16]{0:T(128)S(1)} %copy-done.17, bf16[2,4,1024]{2,1,0:T(4,128)(2,1)S(1)} %bitcast.31, bf16[64,1024]{1,0:T(8,128)(2,1)S(1)} %bitcast.27), custom_call_target="tpu_custom_call" | custom-call | flops 1000000 | tf_op jit(solution)/shard_map/pallas_call | solution.py:421
  14.6 6.5 %all-to-all-start = ((f32[16,1,128]{2,1,0:T(1,128)}), f32[16,1,128]{2,1,0:T(1,128)S(1)}, u32[]{:S(2)}, u32[]{:S(2)}) async-start(f32[16,1,128]{2,1,0:T(1,128)} %bitcast.4), calls=%async_computation | async-start | bytes 16384 | tf_op jit(solution)/shard_map/all_to_all | solution.py:427
  21.2 0.7 %shard_map.98 = (bf16[128,512]{1,0:T(8,128)(2,1)S(1)}, f32[2,8,128]{2,1,0:T(8,128)S(1)}) custom-call(s32[16]{0:T(128)S(1)} %copy-done.17), custom_call_target="tpu_custom_call" | custom-call | flops 1000000 | tf_op jit(solution)/shard_map/pallas_call | solution.py:428
  21.9 0.0 copy-start.5
  21.9 0.6 %copy-done.5 = bf16[128,512]{1,0:T(8,128)(2,1)} copy-done((bf16[128,512]{1,0:T(8,128)(2,1)}, bf16[128,512]{1,0:T(8,128)(2,1)S(1)}, u32[]{:S(2)}) %copy-start.5) | copy-done | bytes 131096
  22.5 0.0 collective-permute-done.3.near_top_ref
  22.5 0.6 %copy-done.11 = f32[8,512]{1,0:T(8,128)} copy-done((f32[8,512]{1,0:T(8,128)}, f32[8,512]{1,0:T(8,128)S(1)}, u32[]{:S(2)}) %copy-start.11) | copy-done | bytes 16408
  23.1 0.0 collective-permute-done.4.far_top_ref
  23.1 0.6 %copy-done.13 = f32[8,512]{1,0:T(8,128)} copy-done((f32[8,512]{1,0:T(8,128)}, f32[8,512]{1,0:T(8,128)S(1)}, u32[]{:S(2)}) %copy-start.13) | copy-done | bytes 16408
  23.7 0.0 collective-permute-done.2.above_ref
  23.7 0.6 %copy-done.9 = f32[128,128]{1,0:T(8,128)} copy-done((f32[128,128]{1,0:T(8,128)}, f32[128,128]{1,0:T(8,128)S(1)}, u32[]{:S(2)}) %copy-start.9) | copy-done | bytes 65560
  24.4 0.0 collective-permute-done.near_ref
  24.4 0.0 collective-permute-done.1.far_ref
  24.4 0.7 %copy-done.3 = f32[8,2,8,512]{3,2,1,0:T(8,128)} copy-done((f32[8,2,8,512]{3,2,1,0:T(8,128)}, f32[8,2,8,512]{3,2,1,0:T(8,128)S(1)}, u32[]{:S(2)}) %copy-start.3) | copy-done | bytes 262168
  25.1 0.0 copy-done.1
  25.1 0.9 %copy-done.4 = f32[8,2,8,512]{3,2,1,0:T(8,128)S(1)} copy-done((f32[8,2,8,512]{3,2,1,0:T(8,128)S(1)}, f32[8,2,8,512]{3,2,1,0:T(8,128)}, u32[]{:S(2)}) %copy-start.4) | copy-done | bytes 262168
  26.0 0.8 %copy-done.10 = f32[128,128]{1,0:T(8,128)S(1)} copy-done((f32[128,128]{1,0:T(8,128)S(1)}, f32[128,128]{1,0:T(8,128)}, u32[]{:S(2)}) %copy-start.10) | copy-done | bytes 65560
  26.9 0.7 %copy-done.12 = f32[8,512]{1,0:T(8,128)S(1)} copy-done((f32[8,512]{1,0:T(8,128)S(1)}, f32[8,512]{1,0:T(8,128)}, u32[]{:S(2)}) %copy-start.12) | copy-done | bytes 16408
  27.6 0.7 %copy-done.14 = f32[8,512]{1,0:T(8,128)S(1)} copy-done((f32[8,512]{1,0:T(8,128)S(1)}, f32[8,512]{1,0:T(8,128)}, u32[]{:S(2)}) %copy-start.14) | copy-done | bytes 16408
  28.3 0.5 shard_map.97
  28.8 0.0 copy-start.7
  28.8 0.6 %copy-done.7 = f32[6,8,512]{2,1,0:T(8,128)} copy-done((f32[6,8,512]{2,1,0:T(8,128)}, f32[6,8,512]{2,1,0:T(8,128)S(1)}, u32[]{:S(2)}) %copy-start.7) | copy-done | bytes 98328
  29.4 0.0 all-to-all-done
  29.4 0.7 %copy-done.16 = f32[8,8]{1,0:T(8,128)S(1)} copy-done((f32[8,8]{1,0:T(8,128)S(1)}, f32[8,8]{1,0:T(8,128)}, u32[]{:S(2)}) %copy-start.16) | copy-done | bytes 280
  30.1 0.0 copy-done.19
  30.1 0.0 copy-done.21
  30.1 0.9 %copy-done.6 = bf16[128,512]{1,0:T(8,128)(2,1)S(1)} copy-done((bf16[128,512]{1,0:T(8,128)(2,1)S(1)}, bf16[128,512]{1,0:T(8,128)(2,1)}, u32[]{:S(2)}) %copy-start.6) | copy-done | bytes 131096
  31.0 0.9 %copy-done.8 = f32[6,8,512]{2,1,0:T(8,128)S(1)} copy-done((f32[6,8,512]{2,1,0:T(8,128)S(1)}, f32[6,8,512]{2,1,0:T(8,128)}, u32[]{:S(2)}) %copy-start.8) | copy-done | bytes 98328
  31.9 3.5 %shard_map.99 = (f32[1024,128]{1,0:T(8,128)}, f32[16,128]{1,0:T(8,128)S(1)}) custom-call(f32[8,8]{1,0:T(8,128)S(1)} %copy-done.16, f32[8]{0:T(128)S(1)} %copy-done.21, f32[3,8]{1,0:T(4,128)S(1)} %copy-done.19, f32[16,128]{1,0:T(8,128)S(1)} %bitcast.29, f32[8,8,8,512]{3,2,1,0:T(8,128)S(1)} %get-tuple-element.18.cells_ref, ...), custom_call_target="tpu_custom_call" | custom-call | flops 1000000 | tf_op jit(solution)/shard_map/pallas_call | solution.py:444
  35.4 12.2 %all_to_all.22 = f32[16,1,128]{2,1,0:T(1,128)S(1)} all-to-all(f32[16,1,128]{2,1,0:T(1,128)S(1)} %bitcast.32), channel_id=1, replica_groups=mesh['wave'=4,'lev'=2,'grp'=4] {'wave','grp'}, dimensions={0} | all-to-all | bytes 16384 | tf_op jit(solution)/shard_map/all_to_all | solution.py:464
  47.6 0.7 %copy-done.18 = s32[16]{0:T(128)S(1)} copy-done((s32[16]{0:T(128)S(1)}, s32[16]{0:T(128)}, u32[]{:S(2)}) %copy-start.18) | copy-done | bytes 88
  48.3 0.0 copy-done.20
  48.3 1.5 %shard_map.100 = f32[2,3,1,1,1024]{4,3,2,1,0:T(1,128)} custom-call(s32[16]{0:T(128)S(1)} %copy-done.18, f32[16,128]{1,0:T(8,128)S(1)} %bitcast.30, f32[1,64]{1,0:T(1,128)S(1)} %bitcast.33, bf16[64,1024]{1,0:T(8,128)(2,1)S(1)} %bitcast.28), custom_call_target="tpu_custom_call" | custom-call | flops 1000000 | tf_op jit(solution)/shard_map/pallas_call | solution.py:465
  (16 shorter events, 0.0 us)
Async XLA Ops:
  0.6 1.0 %copy-start = (f32[8,1,4,4096]{3,2,1,0:T(4,128)S(1)}, f32[8,1,4,4096]{3,2,1,0:T(4,128)}, u32[]{:S(2)}) copy-start(f32[8,1,4,4096]{3,2,1,0:T(4,128)} %param.12) | copy-start | bytes 1572868
  1.7 23.4 %copy-start.1 = (f32[8,1,4,4096]{3,2,1,0:T(4,128)S(1)}, f32[8,1,4,4096]{3,2,1,0:T(4,128)}, u32[]{:S(2)}) copy-start(f32[8,1,4,4096]{3,2,1,0:T(4,128)} %param.12) | copy-start | bytes 1572868
  1.9 10.1 %copy-start.2 = (bf16[1,1024,64]{1,2,0:T(8,128)(2,1)S(1)}, bf16[1,1024,64]{1,2,0:T(8,128)(2,1)}, u32[]{:S(2)}) copy-start(bf16[1,1024,64]{1,2,0:T(8,128)(2,1)} %param.9) | copy-start | bytes 393220
  1.9 22.5 %collective-permute-start = (f32[8,2,8,512]{3,2,1,0:T(8,128)S(1)}, f32[8,2,8,512]{3,2,1,0:T(8,128)S(1)}, u32[]{:S(2)}, u32[]{:S(2)}) collective-permute-start(f32[8,2,8,512]{3,2,1,0:T(8,128)S(1)} %get-tuple-element.14), channel_id=1, source_target_pairs={{0,1},{1,0},{2,3},{3,2},{8,9},{9,8},{10,11},{11,10},{16,17},{17,16... | collective-permute-start | bytes 786440 | tf_op jit(solution)/shard_map/ppermute | solution.py:388
  2.4 22.0 %collective-permute-start.1 = (f32[8,2,8,512]{3,2,1,0:T(8,128)S(1)}, f32[8,2,8,512]{3,2,1,0:T(8,128)S(1)}, u32[]{:S(2)}, u32[]{:S(2)}) collective-permute-start(f32[8,2,8,512]{3,2,1,0:T(8,128)S(1)} %get-tuple-element.15), channel_id=1, source_target_pairs={{1,2},{2,1},{3,8},{8,3},{9,10},{10,9},{11,16},{16,11},{17,18},{18,... | collective-permute-start | bytes 786440 | tf_op jit(solution)/shard_map/ppermute | solution.py:389
  3.1 20.7 %collective-permute-start.2 = (f32[128,128]{1,0:T(8,128)S(1)}, f32[128,128]{1,0:T(8,128)S(1)}, u32[]{:S(2)}, u32[]{:S(2)}) collective-permute-start(f32[128,128]{1,0:T(8,128)S(1)} %bitcast.34), channel_id=1, source_target_pairs={{0,4},{1,5},{2,6},{3,7},{8,12},{9,13},{10,14},{11,15},{16,20},{17,... | collective-permute-start | bytes 196616 | tf_op jit(solution)/shard_map/ppermute | solution.py:402
  7.5 15.0 %collective-permute-start.3 = (f32[8,512]{1,0:T(8,128)S(1)}, f32[8,512]{1,0:T(8,128)S(1)}, u32[]{:S(2)}, u32[]{:S(2)}) collective-permute-start(f32[8,512]{1,0:T(8,128)S(1)} %get-tuple-element.16), channel_id=1, source_target_pairs={{0,5},{1,4},{2,7},{3,6},{8,13},{9,12},{10,15},{11,14},{16,21},{17,... | collective-permute-start | bytes 49160 | tf_op jit(solution)/shard_map/ppermute | solution.py:403
  11.3 11.9 %collective-permute-start.4 = (f32[8,512]{1,0:T(8,128)S(1)}, f32[8,512]{1,0:T(8,128)S(1)}, u32[]{:S(2)}, u32[]{:S(2)}) collective-permute-start(f32[8,512]{1,0:T(8,128)S(1)} %get-tuple-element.17), channel_id=1, source_target_pairs={{1,6},{2,5},{3,12},{8,7},{9,14},{10,13},{11,20},{16,15},{17,22},{1... | collective-permute-start | bytes 49160 | tf_op jit(solution)/shard_map/ppermute | solution.py:404
  11.9 0.7 %copy-start.17 = (s32[16]{0:T(128)S(1)}, s32[16]{0:T(128)}, u32[]{:S(2)}) copy-start(s32[16]{0:T(128)} %waves_ref.5) | copy-start | bytes 196
  12.6 0.7 %copy-start.15 = (bf16[2,4,1,1,1024]{4,1,3,2,0:T(4,128)(2,1)S(1)}, bf16[2,4,1,1,1024]{4,1,3,2,0:T(4,128)(2,1)}, u32[]{:S(2)}) copy-start(bf16[2,4,1,1,1024]{4,1,3,2,0:T(4,128)(2,1)} %param.8) | copy-start | bytes 49156
  14.6 14.8 %all-to-all-start = ((f32[16,1,128]{2,1,0:T(1,128)}), f32[16,1,128]{2,1,0:T(1,128)S(1)}, u32[]{:S(2)}, u32[]{:S(2)}) async-start(f32[16,1,128]{2,1,0:T(1,128)} %bitcast.4), calls=%async_computation | async-start | bytes 16384 | tf_op jit(solution)/shard_map/all_to_all | solution.py:427
  21.9 0.7 %copy-start.5 = (bf16[128,512]{1,0:T(8,128)(2,1)}, bf16[128,512]{1,0:T(8,128)(2,1)S(1)}, u32[]{:S(2)}) copy-start(bf16[128,512]{1,0:T(8,128)(2,1)S(1)} %get-tuple-element.22.table_ref) | copy-start | bytes 393220
  22.5 0.6 %copy-start.11 = (f32[8,512]{1,0:T(8,128)}, f32[8,512]{1,0:T(8,128)S(1)}, u32[]{:S(2)}) copy-start(f32[8,512]{1,0:T(8,128)S(1)} %collective-permute-done.3.near_top_ref) | copy-start | bytes 49156
  23.1 0.6 %copy-start.13 = (f32[8,512]{1,0:T(8,128)}, f32[8,512]{1,0:T(8,128)S(1)}, u32[]{:S(2)}) copy-start(f32[8,512]{1,0:T(8,128)S(1)} %collective-permute-done.4.far_top_ref) | copy-start | bytes 49156
  23.7 0.6 %copy-start.9 = (f32[128,128]{1,0:T(8,128)}, f32[128,128]{1,0:T(8,128)S(1)}, u32[]{:S(2)}) copy-start(f32[128,128]{1,0:T(8,128)S(1)} %collective-permute-done.2.above_ref) | copy-start | bytes 196612
  24.4 0.7 %copy-start.3 = (f32[8,2,8,512]{3,2,1,0:T(8,128)}, f32[8,2,8,512]{3,2,1,0:T(8,128)S(1)}, u32[]{:S(2)}) copy-start(f32[8,2,8,512]{3,2,1,0:T(8,128)S(1)} %collective-permute-done.1.far_ref) | copy-start | bytes 786436
  25.1 1.0 %copy-start.4 = (f32[8,2,8,512]{3,2,1,0:T(8,128)S(1)}, f32[8,2,8,512]{3,2,1,0:T(8,128)}, u32[]{:S(2)}) copy-start(f32[8,2,8,512]{3,2,1,0:T(8,128)} %copy-done.3) | copy-start | bytes 786436
  26.0 0.8 %copy-start.10 = (f32[128,128]{1,0:T(8,128)S(1)}, f32[128,128]{1,0:T(8,128)}, u32[]{:S(2)}) copy-start(f32[128,128]{1,0:T(8,128)} %copy-done.9) | copy-start | bytes 196612
  26.9 0.7 %copy-start.12 = (f32[8,512]{1,0:T(8,128)S(1)}, f32[8,512]{1,0:T(8,128)}, u32[]{:S(2)}) copy-start(f32[8,512]{1,0:T(8,128)} %copy-done.11) | copy-start | bytes 49156
  27.6 0.7 %copy-start.14 = (f32[8,512]{1,0:T(8,128)S(1)}, f32[8,512]{1,0:T(8,128)}, u32[]{:S(2)}) copy-start(f32[8,512]{1,0:T(8,128)} %copy-done.13) | copy-start | bytes 49156
  28.8 0.6 %copy-start.7 = (f32[6,8,512]{2,1,0:T(8,128)}, f32[6,8,512]{2,1,0:T(8,128)S(1)}, u32[]{:S(2)}) copy-start(f32[6,8,512]{2,1,0:T(8,128)S(1)} %get-tuple-element.21.photo_ref) | copy-start | bytes 294916
  29.4 0.7 %copy-start.16 = (f32[8,8]{1,0:T(8,128)S(1)}, f32[8,8]{1,0:T(8,128)}, u32[]{:S(2)}) copy-start(f32[8,8]{1,0:T(8,128)} %kinetics_ref.1) | copy-start | bytes 772
  29.4 0.7 %copy-start.19 = (f32[3,8]{1,0:T(4,128)S(1)}, f32[3,8]{1,0:T(4,128)}, u32[]{:S(2)}) copy-start(f32[3,8]{1,0:T(4,128)} %weights_ref.1) | copy-start | bytes 292
  29.4 0.7 %copy-start.21 = (f32[8]{0:T(128)S(1)}, f32[8]{0:T(128)}, u32[]{:S(2)}) copy-start(f32[8]{0:T(128)} %photolysis_ref.1) | copy-start | bytes 100
  30.1 0.9 %copy-start.6 = (bf16[128,512]{1,0:T(8,128)(2,1)S(1)}, bf16[128,512]{1,0:T(8,128)(2,1)}, u32[]{:S(2)}) copy-start(bf16[128,512]{1,0:T(8,128)(2,1)} %copy-done.5) | copy-start | bytes 393220
  31.0 0.9 %copy-start.8 = (f32[6,8,512]{2,1,0:T(8,128)S(1)}, f32[6,8,512]{2,1,0:T(8,128)}, u32[]{:S(2)}) copy-start(f32[6,8,512]{2,1,0:T(8,128)} %copy-done.7) | copy-start | bytes 294916
  47.6 0.7 %copy-start.18 = (s32[16]{0:T(128)S(1)}, s32[16]{0:T(128)}, u32[]{:S(2)}) copy-start(s32[16]{0:T(128)} %waves_ref.5) | copy-start | bytes 196
  47.6 0.7 %copy-start.20 = (f32[64]{0:T(128)S(1)}, f32[64]{0:T(128)}, u32[]{:S(2)}) copy-start(f32[64]{0:T(128)} %param.11) | copy-start | bytes 772

commit v3 on v2

--- a/solution.py
+++ b/solution.py
@@ -11,7 +11,7 @@
 LANES = 128
 SUB = 8
 PLACE = ("wave", "grp")
-VMEM_BYTES = 48 * 1024 * 1024
+VMEM_BYTES = 8 * 1024 * 1024
 f32 = jnp.float32
 bf16 = jnp.bfloat16
 
@@ -58,8 +58,8 @@
 
 
 def store_row(ref, count, band, t, r, value):
-    for j, s in enumerate(row_slices(ref.shape[0], count, band, t, r)):
-        ref[s, :] = value[:, j * LANES : (j + 1) * LANES]
+    for s, tile in zip(row_slices(ref.shape[0], count, band, t, r), value):
+        ref[s, :] = tile
 
 
 def shift(row, forward):
@@ -77,57 +77,85 @@
     return jnp.concatenate([moved[:, : span - LANES], tail], axis=1)
 
 
-def fourier_kernel(waves_ref, spectra_ref, legendre_ref, out_ref, padded):
+def first_kernel(
+    count,
+    band,
+    width,
+    waves_hbm,
+    spectra_hbm,
+    legendre_hbm,
+    flat_hbm,
+    sent_ref,
+    masked_ref,
+    near_ref,
+    far_ref,
+    flat_ref,
+    waves_ref,
+    spectra_ref,
+    legendre_ref,
+    padded,
+    sems,
+):
+    pairs = (
+        (legendre_hbm, legendre_ref),
+        (spectra_hbm, spectra_ref),
+        (waves_hbm, waves_ref),
+        (flat_hbm, flat_ref),
+    )
+    copies = [pltpu.make_async_copy(a, b, sems.at[n]) for n, (a, b) in enumerate(pairs)]
+    for copy in copies:
+        copy.start()
     parts, fields, degrees = spectra_ref.shape
     lats = legendre_ref.shape[0]
-    places = out_ref.shape[0]
-    band = lats // places
+    places = sent_ref.shape[0]
     margin = (SUB - band) // 2
     place = lax.axis_index(PLACE)
-    limit = degrees - waves_ref[place]
-    keep = lax.broadcasted_iota(jnp.int32, (SUB, degrees), 1) < limit
+    padded[...] = jnp.zeros_like(padded)
+    for copy in copies[:3]:
+        copy.wait()
+    slot = lax.broadcasted_iota(jnp.int32, waves_ref.shape, 1)
+    number = jnp.where(slot == place, waves_ref[...].astype(f32), 0.0)
+    limit = degrees - jnp.sum(number, axis=1, keepdims=True)
+    degree = lax.broadcasted_iota(jnp.int32, (1, degrees), 1).astype(f32)
+    keep = jnp.where(degree < limit, 1.0, 0.0)
+    masked = (legendre_ref[...].astype(f32) * keep).astype(bf16)
+    masked_ref[...] = masked
     rows = []
     for p in range(parts):
         block = spectra_ref[p].astype(f32)
-        for f in range(fields):
-            row = jnp.broadcast_to(block[f : f + 1], (SUB, degrees))
-            rows.append(jnp.where(keep, row, 0.0))
+        rows += [jnp.broadcast_to(block[f : f + 1], (SUB, degrees)) for f in range(fields)]
     spread = jnp.concatenate(rows, axis=0).astype(bf16)
-    fourier = lax.dot_general(
-        legendre_ref[...], spread, (((1,), (1,)), ((), ())), preferred_element_type=f32
-    )
-    width = fourier.shape[1]
-    padded[...] = jnp.zeros_like(padded)
-    padded[SUB : SUB + lats, :width] = fourier
+    nt = (((1,), (1,)), ((), ()))
+    fourier = lax.dot_general(masked, spread, nt, preferred_element_type=f32)
+    copies[3].wait()
+    even = lax.axis_index(PLACE) % 2 == 0
+
+    def fill(near_first, far_first):
+        for t in range(count):
+            for r in range(width):
+                near_ref[t, r] = load_row(flat_ref, count, band, t, near_first + r)
+                far_ref[t, r] = load_row(flat_ref, count, band, t, far_first + r)
+
+    @pl.when(even)
+    def _():
+        fill(band - width, 0)
+
+    @pl.when(jnp.logical_not(even))
+    def _():
+        fill(0, band - width)
+
+    padded[SUB : SUB + lats, : parts * fields * SUB] = fourier
     lane = lax.broadcasted_iota(jnp.int32, (places, LANES), 1) % SUB
     total = jnp.zeros((places, LANES), f32)
     for r in range(SUB):
         rows_r = padded[pl.ds(SUB - margin + r, places, stride=band), :]
         total = jnp.where(lane == r, rows_r, total)
-    out_ref[...] = total
-
-
-def edges_kernel(count, band, width, flat_ref, near_ref, far_ref, near_top_ref, far_top_ref):
-    even = lax.axis_index(PLACE) % 2 == 0
-
-    def fill(near_first, far_first, near_edge, far_edge):
-        for t in range(count):
-            for r in range(width):
-                near_ref[t, r] = load_row(flat_ref, count, band, t, near_first + r)
-                far_ref[t, r] = load_row(flat_ref, count, band, t, far_first + r)
-        near_top_ref[...] = load_row(flat_ref, count, band, 0, near_edge)
-        far_top_ref[...] = load_row(flat_ref, count, band, 0, far_edge)
-
-    @pl.when(even)
-    def _():
-        fill(band - width, 0, band - 1, 0)
-
-    @pl.when(jnp.logical_not(even))
-    def _():
-        fill(0, band - width, 0, band - 1)
-
-
-def table_kernel(waves_ref, table_ref, turn_ref):
+    sent_ref[...] = total
+
+
+def table_kernel(
+    waves_ref, kinetics_ref, photolysis_ref, weights_ref, quad_ref, order_ref, table_ref, turn_ref, rows_ref
+):
     span = table_ref.shape[1]
     waves = table_ref.shape[0] // 8
     lons = span * SUB
@@ -158,60 +186,48 @@
         for n, part in enumerate((0, 2, 1, 3) * 2):
             table_ref[n * waves : (n + 1) * waves, columns] = both[part].astype(bf16)
 
-
-def ready_kernel(
-    levels,
-    count,
-    band,
-    flat_ref,
-    near_ref,
-    far_ref,
-    above_ref,
-    near_top_ref,
-    far_top_ref,
-    cells_ref,
-    west_ref,
-    east_ref,
-    photo_ref,
-):
+    count, heats = kinetics_ref.shape[0], weights_ref.shape[0]
+    band = quad_ref.shape[0] // lax.axis_size(PLACE)
+    first = lax.axis_index(PLACE) * band
+    values = [kinetics_ref[i, j] for i in range(count) for j in range(count)]
+    values += [photolysis_ref[i] for i in range(count)]
+    values += [weights_ref[k, i] for k in range(heats) for i in range(count)]
+    values += [quad_ref[first + r] for k in range(heats) for r in range(band)]
+    for n, value in enumerate(values):
+        rows_ref[n : n + 1, :] = jnp.full((1, LANES), value, f32)
+
+
+def ready_kernel(count, band, flat_ref, near_ref, far_ref, order_ref, cells_ref, column_ref):
     even = lax.axis_index(PLACE) % 2 == 0
     width = near_ref.shape[1]
 
-    def fill(north, south, north_top, south_top):
+    def fill(north, south):
         for t in range(count):
             rows = [north[t, r] for r in range(width)]
             rows += [load_row(flat_ref, count, band, t, r) for r in range(band)]
             rows += [south[t, r] for r in range(width)]
             for r, row in enumerate(rows):
                 cells_ref[t, r] = row
-            for r in range(band + 2):
-                row = rows[r + width - 1]
-                west_ref[t, r] = shift(row, True)
-                east_ref[t, r] = shift(row, False)
-        above = [north_top[...]]
-        above += [load_row(above_ref, 1, band, 0, r) for r in range(band)]
-        above += [south_top[...]]
-        for r, row in enumerate(above):
-            photo_ref[r] = 0.2 * jnp.exp(row * (-2.0 / levels))
+            if t == 0:
+                for r in range(band + 2):
+                    column_ref[r] = rows[r + width - 1]
 
     @pl.when(even)
     def _():
-        fill(far_ref, near_ref, far_top_ref, near_top_ref)
+        fill(far_ref, near_ref)
 
     @pl.when(jnp.logical_not(even))
     def _():
-        fill(near_ref, far_ref, near_top_ref, far_top_ref)
+        fill(near_ref, far_ref)
 
 
 def grid_kernel(
-    kinetics_ref,
-    photolysis_ref,
-    weights_ref,
+    levels,
+    heats,
+    rows_ref,
     received_ref,
     cells_ref,
-    west_ref,
-    east_ref,
-    photo_ref,
+    above_ref,
     table_ref,
     turn_ref,
     flat_ref,
@@ -220,16 +236,37 @@
     coeffs,
 ):
     count, depth, _, span = cells_ref.shape
-    rows = west_ref.shape[1]
+    rows = above_ref.shape[0]
     band = rows - 2
     margin = (SUB - band) // 2
     halo = (depth - band) // 2
     waves = table_ref.shape[0] // 8
-    heats = weights_ref.shape[0]
     fields = 4
     lons = span * SUB
+    tiles = span // LANES
     place = lax.axis_index(PLACE)
     places = lax.axis_size(PLACE)
+
+    def constant(n):
+        return jnp.broadcast_to(rows_ref[n : n + 1, :], (SUB, LANES))
+
+    def kinetics(i, j):
+        return constant(i * count + j)
+
+    def photolysis(i):
+        return constant(count * count + i)
+
+    def heat_weight(k, i):
+        return constant(count * (count + 1 + k) + i)
+
+    def cut(value):
+        return [value[:, j * LANES : (j + 1) * LANES] for j in range(tiles)]
+
+    def combine(factors, values):
+        total = [factors[0] * tile for tile in values[0]]
+        for factor, value in zip(factors[1:], values[1:]):
+            total = [old + factor * tile for old, tile in zip(total, value)]
+        return total
 
     lane = lax.broadcasted_iota(jnp.int32, (SUB, 8 * waves), 1)
     real = (lane // waves) % 2 == 0
@@ -272,14 +309,21 @@
         coeffs[5, r] = 0.2 * jnp.exp(0.3 * warmth)
 
     def react(moved, r):
-        lit = photo_ref[r] * moved[0]
-        rate = coeffs[5, r]
+        overhead = jnp.where(lax.axis_index("lev") > 0, above_ref[r], 0.0)
+        photo = 0.2 * jnp.exp(overhead * (-2.0 / levels))
+        lit = cut(photo * moved[0])
+        rate = cut(coeffs[5, r])
+        moved = [cut(value) for value in moved]
         out = []
         for i in range(count):
-            mixed = kinetics_ref[i, 0] * moved[0]
-            for j in range(1, count):
-                mixed = mixed + kinetics_ref[i, j] * moved[j]
-            out.append(moved[i] + rate * mixed + photolysis_ref[i] * lit)
+            mixed = combine([kinetics(i, j) for j in range(count)], moved)
+            source = photolysis(i)
+            out.append(
+                [
+                    moved[i][j] + rate[j] * mixed[j] + source * lit[j]
+                    for j in range(tiles)
+                ]
+            )
         return out
 
     for r in range(rows):
@@ -288,13 +332,13 @@
             at = r + halo - 1
             moved.append(
                 coeffs[0, r] * cells_ref[t, at]
-                + coeffs[1, r] * west_ref[t, r]
-                + coeffs[2, r] * east_ref[t, r]
+                + coeffs[1, r] * shift(cells_ref[t, at], True)
+                + coeffs[2, r] * shift(cells_ref[t, at], False)
                 + coeffs[3, r] * cells_ref[t, at - 1]
                 + coeffs[4, r] * cells_ref[t, at + 1]
             )
         for t, value in enumerate(react(moved, r)):
-            middle[t, r] = value
+            middle[t, r] = jnp.concatenate(value, axis=1)
 
     first = 3 * rows * SUB
     heated = [[None] * band for _ in range(heats)]
@@ -314,10 +358,8 @@
             store_row(flat_ref, count, band, t, r, out[t])
         warm = 1.0 + 0.5 * jnp.tanh(grid[first + r * SUB : first + (r + 1) * SUB])
         for k in range(heats):
-            total = weights_ref[k, 0] * out[0]
-            for i in range(1, count):
-                total = total + weights_ref[k, i] * out[i]
-            heated[k][r] = total * warm
+            total = combine([heat_weight(k, i) for i in range(count)], out)
+            heated[k][r] = jnp.concatenate(total, axis=1) * warm
 
     heat = jnp.concatenate([row for group in heated for row in group], axis=0)
     high, low = split_bf16(heat)
@@ -340,26 +382,26 @@
     re = sums_a + other
     im = pltpu.roll(sums_a, wide - waves, 1) - sums_b
     size = re.shape[0]
-    filler = jnp.zeros((LANES // 2 - size, wide), f32)
-    both = jnp.concatenate([re, filler, im, filler], axis=0) * (1.0 / math.sqrt(lons))
-    sent_ref[...] = both.T[:waves]
-
-
-def spectra_kernel(band, heats, waves_ref, received_ref, quad_ref, legendre_ref, out_ref, spread):
-    lats, degrees = legendre_ref.shape
+    first = count * (count + 1 + heats)
+    quad = rows_ref[first : first + size, :][:, :1]
+    both = jnp.concatenate([re, im], axis=0) * (1.0 / math.sqrt(lons))
+    both = both * jnp.concatenate([quad, quad], axis=0)
+    filler = jnp.zeros((LANES - 2 * size, wide), f32)
+    sent_ref[...] = jnp.concatenate([both, filler], axis=0).T[:waves]
+
+
+def spectra_kernel(band, heats, received_ref, legendre_ref, out_ref, spread):
     places = received_ref.shape[0]
-    place = lax.axis_index(PLACE)
-    limit = degrees - waves_ref[place]
     received = received_ref[...]
     for r in range(band):
         spread[pl.ds(r, places, stride=band), :] = pltpu.roll(received, (LANES - r) % LANES, 1)
-    weighted = (spread[...].T * quad_ref[...]).astype(bf16)
+    size = -(-heats * band // SUB) * SUB
+    weighted = spread[...].T[: 2 * size].astype(bf16)
     out = jnp.dot(weighted, legendre_ref[...], preferred_element_type=f32)
-    keep = lax.broadcasted_iota(jnp.int32, (1, degrees), 1) < limit
     for p in range(2):
         for k in range(heats):
-            at = p * (LANES // 2) + k * band
-            out_ref[p, k, 0] = jnp.where(keep, out[at : at + 1], 0.0)
+            at = p * size + k * band
+            out_ref[p, k, 0] = out[at : at + 1]
 
 
 def body(spectra, legendre, wavenumbers, quad_weights, tracers, kinetics, photolysis, heat_weights):
@@ -380,94 +422,79 @@
     near_pairs = [(i, i ^ 1) for i in range(places)]
     far_pairs = [(i, ((i + 1) ^ 1) - 1) for i in range(1, places - 1)]
 
-    near, far, near_top, far_top = call(
-        functools.partial(edges_kernel, count, band, width),
-        [shape((count, width, SUB, span), f32)] * 2 + [shape((SUB, span), f32)] * 2,
-        [VM],
-    )(flat)
+    sent, masked, near, far, flat = call(
+        functools.partial(first_kernel, count, band, width),
+        [
+            shape((places, LANES), f32),
+            shape((lats, degrees), bf16),
+            shape((count, width, SUB, span), f32),
+            shape((count, width, SUB, span), f32),
+            shape((flat_rows, LANES), f32),
+        ],
+        [pltpu.HBM] * 4,
+        [
+            pltpu.VMEM((1, waves), jnp.int32),
+            pltpu.VMEM((*spectra.shape[:2], degrees), bf16),
+            pltpu.VMEM((lats, degrees), bf16),
+            pltpu.VMEM((lats + 2 * SUB, LANES), f32),
+            pltpu.SemaphoreType.DMA((4,)),
+        ],
+    )(
+        *(
+            pltpu.with_memory_space_constraint(x, pltpu.HBM)
+            for x in (wavenumbers.reshape(1, waves), spectra[:, :, 0, 0], legendre_t, flat)
+        )
+    )
     near = lax.ppermute(near, PLACE, near_pairs)
     far = lax.ppermute(far, PLACE, far_pairs)
-
-    own_top = flat[: flat_rows // count]
-    if levels == 2:
-        full = ("wave", "lev", "grp")
-        grps = lax.axis_size("grp")
-
-        def upward(pairs):
-            def flat_index(place, level):
-                return (place // grps * levels + level) * grps + place % grps
-
-            return [(flat_index(a, 0), flat_index(b, 1)) for a, b in pairs]
-
-        above = lax.ppermute(own_top, full, upward([(i, i) for i in range(places)]))
-        near_top = lax.ppermute(near_top, full, upward(near_pairs))
-        far_top = lax.ppermute(far_top, full, upward(far_pairs))
-    else:
-
-        def over(value):
-            value = lax.ppermute(value, "lev", [(i, i + 1) for i in range(levels - 1)])
-            reach = 1
-            while reach < levels - 1:
-                value = value + lax.ppermute(
-                    value, "lev", [(i, i + reach) for i in range(levels - reach)]
-                )
-                reach *= 2
-            return value
-
-        above = over(own_top)
-        near_top = over(lax.ppermute(near_top, PLACE, near_pairs))
-        far_top = over(lax.ppermute(far_top, PLACE, far_pairs))
-
-    sent = call(
-        fourier_kernel,
-        shape((places, LANES), f32),
-        [SM, VM, VM],
-        [pltpu.VMEM((lats + 2 * SUB, LANES), f32)],
-    )(wavenumbers, spectra[:, :, 0, 0], legendre_t)
     received = lax.all_to_all(sent, PLACE, 0, 0, tiled=True)
-    table, turn = call(
+
+    constants = count * (count + 1 + heats)
+    table, turn, scalars = call(
         table_kernel,
-        [shape((8 * waves, span), bf16), shape((2, SUB, 8 * waves), f32)],
-        [SM],
-    )(wavenumbers)
-    cells, west, east, photo = call(
-        functools.partial(ready_kernel, levels, count, band),
+        [
+            shape((8 * waves, span), bf16),
+            shape((2, SUB, 8 * waves), f32),
+            shape((constants + 2 * SUB, LANES), f32),
+        ],
+        [SM] * 5 + [pl.ANY],
+        flops=20_000_000_000,
+    )(wavenumbers, kinetics, photolysis, heat_weights, quad_weights, sent)
+
+    cells, column = call(
+        functools.partial(ready_kernel, count, band),
         [
             shape((count, band + 2 * width, SUB, span), f32),
-            shape((count, band + 2, SUB, span), f32),
-            shape((count, band + 2, SUB, span), f32),
             shape((band + 2, SUB, span), f32),
         ],
+        [VM] * 3 + [pl.ANY],
+    )(flat, near, far, sent)
+    above = lax.ppermute(column, "lev", [(i, (i + 1) % levels) for i in range(levels)])
+    if levels > 2:
+        above = jnp.where(lax.axis_index("lev") > 0, above, 0.0)
+    reach = 1
+    while reach < levels - 1:
+        above = above + lax.ppermute(
+            above, "lev", [(i, i + reach) for i in range(levels - reach)]
+        )
+        reach *= 2
+
+    flat_out, heat_sent = call(
+        functools.partial(grid_kernel, levels, heats),
+        [shape((flat_rows, LANES), f32), shape((waves, LANES), f32)],
         [VM] * 6,
-    )(flat, near, far, above, near_top, far_top)
-
-    flat_out, heat_sent = call(
-        grid_kernel,
-        [shape((flat_rows, LANES), f32), shape((waves, LANES), f32)],
-        [SM] * 3 + [VM] * 7,
         [
             pltpu.VMEM((count, band + 2, SUB, span), f32),
             pltpu.VMEM((6, band + 2, SUB, span), f32),
         ],
-    )(
-        kinetics,
-        photolysis,
-        heat_weights,
-        received,
-        cells,
-        west,
-        east,
-        photo,
-        table,
-        turn,
-    )
+    )(scalars, received, cells, above, table, turn)
     heat_received = lax.all_to_all(heat_sent, PLACE, 0, 0, tiled=True)
     heating_spectra = call(
         functools.partial(spectra_kernel, band, heats),
         shape((2, heats, 1, 1, degrees), f32),
-        [SM, VM, VM, VM],
+        [VM, VM],
         [pltpu.VMEM((lats, LANES), f32)],
-    )(wavenumbers, heat_received, quad_weights.reshape(1, lats), legendre_t)
+    )(heat_received, masked)
     return (unfold(flat_out, count, band)[:, None], heating_spectra)
 
 

time: 50.4 us -> 34.9 us (0.69)
  local copies, waits for them, and re-layouts: 12.6 us -> 0.03 us
  starting transfers between devices: 16.5 us -> 11.6 us
  waiting for transfers between devices: 0.02 us -> 3.6 us
  Pallas kernels: 7.64 us -> 6.95 us
    unnamed x44 -> x10, local copies, waits for them, and re-layouts: 12.6 us -> 0.03 us
    ppermute x3 -> x1, starting transfers between devices: 8.85 us -> 1.58 us  [body(): lax.ppermute(column, 'lev', [(i, (i + 1) % levels) for i in range(levels)])]
    all_to_all x1, waiting for transfers between devices: 0.01 us -> 3.59 us  [body(): received = lax.all_to_all(sent, PLACE, 0, 0, tiled=True)]
    all_to_all x1, starting transfers between devices: 6.51 us -> 8.79 us  [body(): received = lax.all_to_all(sent, PLACE, 0, 0, tiled=True)]
    pallas_call x1, Pallas kernels: 1.48 us -> 0.89 us  [body(): call(functools.partial(spectra_kernel, band, heats), shape((2, heats, 1,...]
    pallas_call x4 -> x3, Pallas kernels: 5.45 us -> 5.24 us  [the longest x1 3.06 us: body(): call(functools.partial(grid_kernel, levels, heats), [shape((flat_rows, LA...]
  transfers between devices with their start and end apart: 6 -> 4, of which waited for: 0 -> 1; matrix products, arithmetic and copies ran while one was open for 0% -> 0% of each run, Pallas kernels for 5% -> 3%
where the time goes in v3:
time: 34.9 us; the launch traced here: 34.6 us
  blocking collectives  11.7 us (34%)
  starting transfers between devices  11.6 us (33%)
  Pallas kernels  6.95 us (20%)
  waiting for transfers between devices  3.6 us (10%)
  between operations  0.74 us (2%)
    all_to_all x1, blocking collectives, body(): heat_received = lax.all_to_all(heat_sent, PLACE, 0, 0, tiled=True)  11.7 us
    all_to_all x1, starting transfers between devices, body(): received = lax.all_to_all(sent, PLACE, 0, 0, tiled=True)  8.79 us
    all_to_all x1, waiting for transfers between devices, body(): received = lax.all_to_all(sent, PLACE, 0, 0, tiled=True)  3.59 us
    pallas_call x1, Pallas kernels, body(): call(functools.partial(grid_kernel, levels, heats), [shape((flat_rows, LA...  3.06 us
    pallas_call x1, Pallas kernels, body(): call(functools.partial(first_kernel, count, band, width), [shape((places,...  1.97 us
    ppermute x1, starting transfers between devices, body(): lax.ppermute(column, 'lev', [(i, (i + 1) % levels) for i in range(levels)])  1.58 us
    pallas_call x1, Pallas kernels, body(): call(functools.partial(spectra_kernel, band, heats), shape((2, heats, 1,...  0.89 us
    pallas_call x1, Pallas kernels, body(): call(table_kernel, [shape((8 * waves, span), bf16), shape((2, SUB, 8 * wa...  0.83 us
  transfers between devices with their start and end apart: 4, of which 1 were waited for; matrix products, arithmetic and copies ran while one was open for 0% of the time, Pallas kernels for 3%

profile of v3, /device:TPU:0, one launch (start us, length us, event | category | flops | bytes accessed | tf_op | source)
XLA Modules:
  0.0 34.6 jit_solution(5094125281749708949)
XLA Ops:
  0.6 2.0 %shard_map.95 = (f32[16,128]{1,0:T(8,128)}, bf16[64,1024]{1,0:T(8,128)(2,1)S(1)}, f32[8,2,8,512]{3,2,1,0:T(8,128)S(1)}, f32[8,2,8,512]{3,2,1,0:T(8,128)S(1)}, f32[1024,128]{1,0:T(8,128)S(1)}) custom-call(s32[1,16]{1,0:T(1,128)} %bitcast.26, bf16[2,4,1024]{2,1,0:T(4,128)(2,1)} %bitcast.29, bf16[64,1024]{1,0:T(8,128)(2,1)} %bitcast.28, f32[1024,128]{1,0:T(8,128)} %bitcast.27), custom_call_target="tpu_custom_call" | custom-call | flops 1000000 | tf_op jit(solution)/shard_map/pallas_call | solution.py:425
  2.6 0.5 %collective-permute-start = (f32[8,2,8,512]{3,2,1,0:T(8,128)S(1)}, f32[8,2,8,512]{3,2,1,0:T(8,128)S(1)}, u32[]{:S(2)}, u32[]{:S(2)}) collective-permute-start(f32[8,2,8,512]{3,2,1,0:T(8,128)S(1)} %get-tuple-element.17), channel_id=1, source_target_pairs={{0,1},{1,0},{2,3},{3,2},{8,9},{9,8},{10,11},{11,10},{16,17},{17,16... | collective-permute-start | bytes 786440 | tf_op jit(solution)/shard_map/ppermute | solution.py:448
  3.1 0.7 %collective-permute-start.1 = (f32[8,2,8,512]{3,2,1,0:T(8,128)S(1)}, f32[8,2,8,512]{3,2,1,0:T(8,128)S(1)}, u32[]{:S(2)}, u32[]{:S(2)}) collective-permute-start(f32[8,2,8,512]{3,2,1,0:T(8,128)S(1)} %get-tuple-element.18), channel_id=1, source_target_pairs={{1,2},{2,1},{3,8},{8,3},{9,10},{10,9},{11,16},{16,11},{17,18},{18,... | collective-permute-start | bytes 786440 | tf_op jit(solution)/shard_map/ppermute | solution.py:449
  3.8 8.8 %all-to-all-start = ((f32[16,1,128]{2,1,0:T(1,128)}), f32[16,1,128]{2,1,0:T(1,128)S(1)}, u32[]{:S(2)}, u32[]{:S(2)}) async-start(f32[16,1,128]{2,1,0:T(1,128)} %bitcast.8), calls=%async_computation | async-start | bytes 16384 | tf_op jit(solution)/shard_map/all_to_all | solution.py:450
  12.6 0.0 collective-permute-done.near_ref
  12.6 0.0 collective-permute-done.1.far_ref
  12.6 0.0 copy-start.1
  12.6 0.0 copy-start.2
  12.7 0.2 shard_map.97
  12.9 0.0 copy-start
  12.9 0.0 copy-start.3
  12.9 0.0 copy-start.4
  12.9 1.6 %collective-permute-start.2 = (f32[6,8,512]{2,1,0:T(8,128)S(1)}, f32[6,8,512]{2,1,0:T(8,128)S(1)}, u32[]{:S(2)}, u32[]{:S(2)}) collective-permute-start(f32[6,8,512]{2,1,0:T(8,128)S(1)} %get-tuple-element.20), channel_id=1, source_target_pairs={{0,4},{4,0},{1,5},{5,1},{2,6},{6,2},{3,7},{7,3},{8,12},{12,8},{9,1... | collective-permute-start | bytes 294920 | tf_op jit(solution)/shard_map/ppermute | solution.py:472
  14.5 0.0 copy-done.1
  14.5 0.0 copy-done.2
  14.5 0.0 copy-done
  14.5 0.0 copy-done.3
  14.5 0.0 copy-done.4
  14.5 0.8 %shard_map.96 = (bf16[128,512]{1,0:T(8,128)(2,1)S(1)}, f32[2,8,128]{2,1,0:T(8,128)S(1)}, f32[112,128]{1,0:T(8,128)S(1)}) custom-call(s32[16]{0:T(128)S(1)} %copy-done, f32[8,8]{1,0:T(8,128)S(1)} %copy-done.1, f32[8]{0:T(128)S(1)} %copy-done.3, f32[3,8]{1,0:T(4,128)S(1)} %copy-done.2, f32[64]{0:T(128)S(1)} %copy-done.4, f32[16,128]{1,0:T(8,128)} %get-tuple-element.14.order_ref), custom_call_target="tpu_custom_call" | custom-call | flops 20000000000 | tf_op jit(solution)/shard_map/pallas_call | solution.py:453
  15.4 3.6 %all-to-all-done = f32[16,1,128]{2,1,0:T(1,128)S(1)} async-done(((f32[16,1,128]{2,1,0:T(1,128)}), f32[16,1,128]{2,1,0:T(1,128)S(1)}, u32[]{:S(2)}, u32[]{:S(2)}) %all-to-all-start) | async-done | bytes 8224 | tf_op jit(solution)/shard_map/all_to_all | solution.py:450
  18.9 0.0 collective-permute-done.2.above_ref
  18.9 3.1 %shard_map.98 = (f32[1024,128]{1,0:T(8,128)}, f32[16,128]{1,0:T(8,128)S(1)}) custom-call(f32[112,128]{1,0:T(8,128)S(1)} %get-tuple-element.15.rows_ref, f32[16,128]{1,0:T(8,128)S(1)} %bitcast.23, f32[8,8,8,512]{3,2,1,0:T(8,128)S(1)} %get-tuple-element.19.cells_ref, f32[6,8,512]{2,1,0:T(8,128)S(1)} %collective-permute-done.2.above_ref, ...), custom_call_target="tpu_custom_call" | custom-call | flops 1000000 | tf_op jit(solution)/shard_map/pallas_call | solution.py:482
  22.0 11.7 %all_to_all.22 = f32[16,1,128]{2,1,0:T(1,128)S(1)} all-to-all(f32[16,1,128]{2,1,0:T(1,128)S(1)} %bitcast.25), channel_id=1, replica_groups=mesh['wave'=4,'lev'=2,'grp'=4] {'wave','grp'}, dimensions={0} | all-to-all | bytes 16384 | tf_op jit(solution)/shard_map/all_to_all | solution.py:491
  33.7 0.9 %shard_map.99 = f32[2,3,1,1,1024]{4,3,2,1,0:T(1,128)} custom-call(f32[16,128]{1,0:T(8,128)S(1)} %bitcast.24, bf16[64,1024]{1,0:T(8,128)(2,1)S(1)} %get-tuple-element.25.legendre_ref), custom_call_target="tpu_custom_call" | custom-call | flops 1000000 | tf_op jit(solution)/shard_map/pallas_call | solution.py:492
Async XLA Ops:
  2.6 10.0 %collective-permute-start = (f32[8,2,8,512]{3,2,1,0:T(8,128)S(1)}, f32[8,2,8,512]{3,2,1,0:T(8,128)S(1)}, u32[]{:S(2)}, u32[]{:S(2)}) collective-permute-start(f32[8,2,8,512]{3,2,1,0:T(8,128)S(1)} %get-tuple-element.17), channel_id=1, source_target_pairs={{0,1},{1,0},{2,3},{3,2},{8,9},{9,8},{10,11},{11,10},{16,17},{17,16... | collective-permute-start | bytes 786440 | tf_op jit(solution)/shard_map/ppermute | solution.py:448
  3.1 9.5 %collective-permute-start.1 = (f32[8,2,8,512]{3,2,1,0:T(8,128)S(1)}, f32[8,2,8,512]{3,2,1,0:T(8,128)S(1)}, u32[]{:S(2)}, u32[]{:S(2)}) collective-permute-start(f32[8,2,8,512]{3,2,1,0:T(8,128)S(1)} %get-tuple-element.18), channel_id=1, source_target_pairs={{1,2},{2,1},{3,8},{8,3},{9,10},{10,9},{11,16},{16,11},{17,18},{18,... | collective-permute-start | bytes 786440 | tf_op jit(solution)/shard_map/ppermute | solution.py:449
  3.8 15.1 %all-to-all-start = ((f32[16,1,128]{2,1,0:T(1,128)}), f32[16,1,128]{2,1,0:T(1,128)S(1)}, u32[]{:S(2)}, u32[]{:S(2)}) async-start(f32[16,1,128]{2,1,0:T(1,128)} %bitcast.8), calls=%async_computation | async-start | bytes 16384 | tf_op jit(solution)/shard_map/all_to_all | solution.py:450
  12.6 1.9 %copy-start.1 = (f32[8,8]{1,0:T(8,128)S(1)}, f32[8,8]{1,0:T(8,128)}, u32[]{:S(2)}) copy-start(f32[8,8]{1,0:T(8,128)} %kinetics_ref.1) | copy-start | bytes 772
  12.6 1.9 %copy-start.2 = (f32[3,8]{1,0:T(4,128)S(1)}, f32[3,8]{1,0:T(4,128)}, u32[]{:S(2)}) copy-start(f32[3,8]{1,0:T(4,128)} %weights_ref.1) | copy-start | bytes 292
  12.9 1.6 %copy-start = (s32[16]{0:T(128)S(1)}, s32[16]{0:T(128)}, u32[]{:S(2)}) copy-start(s32[16]{0:T(128)} %waves_ref.1) | copy-start | bytes 196
  12.9 1.6 %copy-start.3 = (f32[8]{0:T(128)S(1)}, f32[8]{0:T(128)}, u32[]{:S(2)}) copy-start(f32[8]{0:T(128)} %photolysis_ref.1) | copy-start | bytes 100
  12.9 1.6 %copy-start.4 = (f32[64]{0:T(128)S(1)}, f32[64]{0:T(128)}, u32[]{:S(2)}) copy-start(f32[64]{0:T(128)} %quad_ref.1) | copy-start | bytes 772
  12.9 6.0 %collective-permute-start.2 = (f32[6,8,512]{2,1,0:T(8,128)S(1)}, f32[6,8,512]{2,1,0:T(8,128)S(1)}, u32[]{:S(2)}, u32[]{:S(2)}) collective-permute-start(f32[6,8,512]{2,1,0:T(8,128)S(1)} %get-tuple-element.20), channel_id=1, source_target_pairs={{0,4},{4,0},{1,5},{5,1},{2,6},{6,2},{3,7},{7,3},{8,12},{12,8},{9,1... | collective-permute-start | bytes 294920 | tf_op jit(solution)/shard_map/ppermute | solution.py:472

commit v4 on v3

--- a/solution.py
+++ b/solution.py
@@ -77,7 +77,7 @@
     return jnp.concatenate([moved[:, : span - LANES], tail], axis=1)
 
 
-def first_kernel(
+def edges_kernel(
     count,
     band,
     width,
@@ -85,34 +85,51 @@
     spectra_hbm,
     legendre_hbm,
     flat_hbm,
-    sent_ref,
-    masked_ref,
     near_ref,
     far_ref,
-    flat_ref,
     waves_ref,
     spectra_ref,
     legendre_ref,
-    padded,
+    flat_ref,
     sems,
 ):
     pairs = (
+        (flat_hbm, flat_ref),
         (legendre_hbm, legendre_ref),
         (spectra_hbm, spectra_ref),
         (waves_hbm, waves_ref),
-        (flat_hbm, flat_ref),
     )
     copies = [pltpu.make_async_copy(a, b, sems.at[n]) for n, (a, b) in enumerate(pairs)]
     for copy in copies:
         copy.start()
+    copies[0].wait()
+    even = lax.axis_index(PLACE) % 2 == 0
+
+    def fill(near_first, far_first):
+        for t in range(count):
+            for r in range(width):
+                near_ref[t, r] = load_row(flat_ref, count, band, t, near_first + r)
+                far_ref[t, r] = load_row(flat_ref, count, band, t, far_first + r)
+
+    @pl.when(even)
+    def _():
+        fill(band - width, 0)
+
+    @pl.when(jnp.logical_not(even))
+    def _():
+        fill(0, band - width)
+
+    for copy in copies[1:]:
+        copy.wait()
+
+
+def fourier_kernel(band, waves_ref, spectra_ref, legendre_ref, sent_ref, masked_ref, padded):
     parts, fields, degrees = spectra_ref.shape
     lats = legendre_ref.shape[0]
     places = sent_ref.shape[0]
     margin = (SUB - band) // 2
     place = lax.axis_index(PLACE)
     padded[...] = jnp.zeros_like(padded)
-    for copy in copies[:3]:
-        copy.wait()
     slot = lax.broadcasted_iota(jnp.int32, waves_ref.shape, 1)
     number = jnp.where(slot == place, waves_ref[...].astype(f32), 0.0)
     limit = degrees - jnp.sum(number, axis=1, keepdims=True)
@@ -127,23 +144,6 @@
     spread = jnp.concatenate(rows, axis=0).astype(bf16)
     nt = (((1,), (1,)), ((), ()))
     fourier = lax.dot_general(masked, spread, nt, preferred_element_type=f32)
-    copies[3].wait()
-    even = lax.axis_index(PLACE) % 2 == 0
-
-    def fill(near_first, far_first):
-        for t in range(count):
-            for r in range(width):
-                near_ref[t, r] = load_row(flat_ref, count, band, t, near_first + r)
-                far_ref[t, r] = load_row(flat_ref, count, band, t, far_first + r)
-
-    @pl.when(even)
-    def _():
-        fill(band - width, 0)
-
-    @pl.when(jnp.logical_not(even))
-    def _():
-        fill(0, band - width)
-
     padded[SUB : SUB + lats, : parts * fields * SUB] = fourier
     lane = lax.broadcasted_iota(jnp.int32, (places, LANES), 1) % SUB
     total = jnp.zeros((places, LANES), f32)
@@ -221,52 +221,70 @@
         fill(near_ref, far_ref)
 
 
-def grid_kernel(
-    levels,
+class Scalars:
+    def __init__(self, ref, count, heats):
+        self.ref, self.count, self.heats = ref, count, heats
+
+    def row(self, n):
+        return jnp.broadcast_to(self.ref[n : n + 1, :], (SUB, LANES))
+
+    def kinetics(self, i, j):
+        return self.row(i * self.count + j)
+
+    def photolysis(self, i):
+        return self.row(self.count * self.count + i)
+
+    def weight(self, k, i):
+        return self.row(self.count * (self.count + 1 + k) + i)
+
+    def quad(self, size):
+        first = self.count * (self.count + 1 + self.heats)
+        return self.ref[first : first + size, :][:, :1]
+
+
+def cut(value):
+    return [value[:, j : j + LANES] for j in range(0, value.shape[1], LANES)]
+
+
+def combine(factors, values):
+    total = [factors[0] * tile for tile in values[0]]
+    for factor, value in zip(factors[1:], values[1:]):
+        total = [old + factor * tile for old, tile in zip(total, value)]
+    return total
+
+
+def stencil(coeffs, r, centre, north, south):
+    return (
+        coeffs[0, r] * centre
+        + coeffs[1, r] * shift(centre, True)
+        + coeffs[2, r] * shift(centre, False)
+        + coeffs[3, r] * north
+        + coeffs[4, r] * south
+    )
+
+
+def first_substep_kernel(
     heats,
     rows_ref,
     received_ref,
     cells_ref,
-    above_ref,
     table_ref,
     turn_ref,
-    flat_ref,
-    sent_ref,
-    middle,
-    coeffs,
+    coeffs_ref,
+    base_ref,
+    lead_ref,
+    warm_ref,
 ):
     count, depth, _, span = cells_ref.shape
-    rows = above_ref.shape[0]
+    rows = lead_ref.shape[0]
     band = rows - 2
     margin = (SUB - band) // 2
     halo = (depth - band) // 2
     waves = table_ref.shape[0] // 8
     fields = 4
-    lons = span * SUB
-    tiles = span // LANES
     place = lax.axis_index(PLACE)
     places = lax.axis_size(PLACE)
-
-    def constant(n):
-        return jnp.broadcast_to(rows_ref[n : n + 1, :], (SUB, LANES))
-
-    def kinetics(i, j):
-        return constant(i * count + j)
-
-    def photolysis(i):
-        return constant(count * count + i)
-
-    def heat_weight(k, i):
-        return constant(count * (count + 1 + k) + i)
-
-    def cut(value):
-        return [value[:, j * LANES : (j + 1) * LANES] for j in range(tiles)]
-
-    def combine(factors, values):
-        total = [factors[0] * tile for tile in values[0]]
-        for factor, value in zip(factors[1:], values[1:]):
-            total = [old + factor * tile for old, tile in zip(total, value)]
-        return total
+    scalars = Scalars(rows_ref, count, heats)
 
     lane = lax.broadcasted_iota(jnp.int32, (SUB, 8 * waves), 1)
     real = (lane // waves) % 2 == 0
@@ -301,65 +319,84 @@
             courant_x = jnp.where(inside, courant_x, 0.0)
             courant_y = jnp.where(inside, courant_y, 0.0)
             own = jnp.where(inside, own, 0.0)
-        coeffs[0, r] = own
-        coeffs[1, r] = jnp.maximum(courant_x, 0.0)
-        coeffs[2, r] = -jnp.minimum(courant_x, 0.0)
-        coeffs[3, r] = jnp.maximum(courant_y, 0.0)
-        coeffs[4, r] = -jnp.minimum(courant_y, 0.0)
-        coeffs[5, r] = 0.2 * jnp.exp(0.3 * warmth)
-
-    def react(moved, r):
-        overhead = jnp.where(lax.axis_index("lev") > 0, above_ref[r], 0.0)
-        photo = 0.2 * jnp.exp(overhead * (-2.0 / levels))
-        lit = cut(photo * moved[0])
-        rate = cut(coeffs[5, r])
+        coeffs_ref[0, r] = own
+        coeffs_ref[1, r] = jnp.maximum(courant_x, 0.0)
+        coeffs_ref[2, r] = -jnp.minimum(courant_x, 0.0)
+        coeffs_ref[3, r] = jnp.maximum(courant_y, 0.0)
+        coeffs_ref[4, r] = -jnp.minimum(courant_y, 0.0)
+        coeffs_ref[5, r] = 0.2 * jnp.exp(0.3 * warmth)
+    first = 3 * rows * SUB
+    for r in range(band):
+        warm_ref[r] = 1.0 + 0.5 * jnp.tanh(grid[first + r * SUB : first + (r + 1) * SUB])
+
+    for r in range(rows):
+        at = r + halo - 1
+        moved = [
+            stencil(coeffs_ref, r, cells_ref[t, at], cells_ref[t, at - 1], cells_ref[t, at + 1])
+            for t in range(count)
+        ]
+        lead_ref[r] = moved[0]
+        moved = [cut(value) for value in moved]
+        rate = cut(coeffs_ref[5, r])
+        for i in range(count):
+            mixed = combine([scalars.kinetics(i, j) for j in range(count)], moved)
+            out = [a + b * c for a, b, c in zip(moved[i], rate, mixed)]
+            base_ref[i, r] = jnp.concatenate(out, axis=1)
+
+
+def second_substep_kernel(
+    levels,
+    heats,
+    rows_ref,
+    above_ref,
+    table_ref,
+    turn_ref,
+    coeffs_ref,
+    base_ref,
+    lead_ref,
+    warm_ref,
+    flat_ref,
+    sent_ref,
+    middle,
+):
+    count, rows, _, span = base_ref.shape
+    band = rows - 2
+    waves = table_ref.shape[0] // 8
+    lons = span * SUB
+    scalars = Scalars(rows_ref, count, heats)
+    turn_cos, turn_sin = turn_ref[0], turn_ref[1]
+    covered = lax.axis_index("lev") > 0
+    photo = []
+    for r in range(rows):
+        overhead = jnp.where(covered, above_ref[r], 0.0)
+        photo.append(0.2 * jnp.exp(overhead * (-2.0 / levels)))
+        lit = cut(photo[r] * lead_ref[r])
+        for t in range(count):
+            source = scalars.photolysis(t)
+            parts = [old + source * tile for old, tile in zip(cut(base_ref[t, r]), lit)]
+            middle[t, r] = jnp.concatenate(parts, axis=1)
+
+    heated = [[None] * band for _ in range(heats)]
+    for r in range(band):
+        moved = [
+            stencil(coeffs_ref, r + 1, middle[t, r + 1], middle[t, r], middle[t, r + 2])
+            for t in range(count)
+        ]
+        lit = cut(photo[r + 1] * moved[0])
+        rate = cut(coeffs_ref[5, r + 1])
         moved = [cut(value) for value in moved]
         out = []
         for i in range(count):
-            mixed = combine([kinetics(i, j) for j in range(count)], moved)
-            source = photolysis(i)
+            mixed = combine([scalars.kinetics(i, j) for j in range(count)], moved)
+            source = scalars.photolysis(i)
             out.append(
-                [
-                    moved[i][j] + rate[j] * mixed[j] + source * lit[j]
-                    for j in range(tiles)
-                ]
+                [a + b * c + source * d for a, b, c, d in zip(moved[i], rate, mixed, lit)]
             )
-        return out
-
-    for r in range(rows):
-        moved = []
-        for t in range(count):
-            at = r + halo - 1
-            moved.append(
-                coeffs[0, r] * cells_ref[t, at]
-                + coeffs[1, r] * shift(cells_ref[t, at], True)
-                + coeffs[2, r] * shift(cells_ref[t, at], False)
-                + coeffs[3, r] * cells_ref[t, at - 1]
-                + coeffs[4, r] * cells_ref[t, at + 1]
-            )
-        for t, value in enumerate(react(moved, r)):
-            middle[t, r] = jnp.concatenate(value, axis=1)
-
-    first = 3 * rows * SUB
-    heated = [[None] * band for _ in range(heats)]
-    for r in range(band):
-        moved = []
-        for t in range(count):
-            row = middle[t, r + 1]
-            moved.append(
-                coeffs[0, r + 1] * row
-                + coeffs[1, r + 1] * shift(row, True)
-                + coeffs[2, r + 1] * shift(row, False)
-                + coeffs[3, r + 1] * middle[t, r]
-                + coeffs[4, r + 1] * middle[t, r + 2]
-            )
-        out = react(moved, r + 1)
         for t in range(count):
             store_row(flat_ref, count, band, t, r, out[t])
-        warm = 1.0 + 0.5 * jnp.tanh(grid[first + r * SUB : first + (r + 1) * SUB])
         for k in range(heats):
-            total = combine([heat_weight(k, i) for i in range(count)], out)
-            heated[k][r] = jnp.concatenate(total, axis=1) * warm
+            total = combine([scalars.weight(k, i) for i in range(count)], out)
+            heated[k][r] = jnp.concatenate(total, axis=1) * warm_ref[r]
 
     heat = jnp.concatenate([row for group in heated for row in group], axis=0)
     high, low = split_bf16(heat)
@@ -382,8 +419,7 @@
     re = sums_a + other
     im = pltpu.roll(sums_a, wide - waves, 1) - sums_b
     size = re.shape[0]
-    first = count * (count + 1 + heats)
-    quad = rows_ref[first : first + size, :][:, :1]
+    quad = scalars.quad(size)
     both = jnp.concatenate([re, im], axis=0) * (1.0 / math.sqrt(lons))
     both = both * jnp.concatenate([quad, quad], axis=0)
     filler = jnp.zeros((LANES - 2 * size, wide), f32)
@@ -422,23 +458,19 @@
     near_pairs = [(i, i ^ 1) for i in range(places)]
     far_pairs = [(i, ((i + 1) ^ 1) - 1) for i in range(1, places - 1)]
 
-    sent, masked, near, far, flat = call(
-        functools.partial(first_kernel, count, band, width),
+    halo = shape((count, width, SUB, span), f32)
+    near, far, waves_in, spectra_in, legendre_in, flat = call(
+        functools.partial(edges_kernel, count, band, width),
         [
-            shape((places, LANES), f32),
+            halo,
+            halo,
+            shape((1, waves), jnp.int32),
+            shape((*spectra.shape[:2], degrees), bf16),
             shape((lats, degrees), bf16),
-            shape((count, width, SUB, span), f32),
-            shape((count, width, SUB, span), f32),
             shape((flat_rows, LANES), f32),
         ],
         [pltpu.HBM] * 4,
-        [
-            pltpu.VMEM((1, waves), jnp.int32),
-            pltpu.VMEM((*spectra.shape[:2], degrees), bf16),
-            pltpu.VMEM((lats, degrees), bf16),
-            pltpu.VMEM((lats + 2 * SUB, LANES), f32),
-            pltpu.SemaphoreType.DMA((4,)),
-        ],
+        [pltpu.SemaphoreType.DMA((4,))],
     )(
         *(
             pltpu.with_memory_space_constraint(x, pltpu.HBM)
@@ -447,6 +479,13 @@
     )
     near = lax.ppermute(near, PLACE, near_pairs)
     far = lax.ppermute(far, PLACE, far_pairs)
+    sent, masked = call(
+        functools.partial(fourier_kernel, band),
+        [shape((places, LANES), f32), shape((lats, degrees), bf16)],
+        [VM] * 3,
+        [pltpu.VMEM((lats + 2 * SUB, LANES), f32)],
+        flops=1000000,
+    )(waves_in, spectra_in, legendre_in)
     received = lax.all_to_all(sent, PLACE, 0, 0, tiled=True)
 
     constants = count * (count + 1 + heats)
@@ -458,7 +497,7 @@
             shape((constants + 2 * SUB, LANES), f32),
         ],
         [SM] * 5 + [pl.ANY],
-        flops=20_000_000_000,
+        flops=20000000000,
     )(wavenumbers, kinetics, photolysis, heat_weights, quad_weights, sent)
 
     cells, column = call(
@@ -479,15 +518,24 @@
         )
         reach *= 2
 
+    field = shape((band + 2, SUB, span), f32)
+    coeffs, base, lead, warm = call(
+        functools.partial(first_substep_kernel, heats),
+        [
+            shape((6, band + 2, SUB, span), f32),
+            shape((count, band + 2, SUB, span), f32),
+            field,
+            shape((band, SUB, span), f32),
+        ],
+        [VM] * 5,
+        flops=1000000,
+    )(scalars, received, cells, table, turn)
     flat_out, heat_sent = call(
-        functools.partial(grid_kernel, levels, heats),
+        functools.partial(second_substep_kernel, levels, heats),
         [shape((flat_rows, LANES), f32), shape((waves, LANES), f32)],
-        [VM] * 6,
-        [
-            pltpu.VMEM((count, band + 2, SUB, span), f32),
-            pltpu.VMEM((6, band + 2, SUB, span), f32),
-        ],
-    )(scalars, received, cells, above, table, turn)
+        [VM] * 8,
+        [pltpu.VMEM((count, band + 2, SUB, span), f32)],
+    )(scalars, above, table, turn, coeffs, base, lead, warm)
     heat_received = lax.all_to_all(heat_sent, PLACE, 0, 0, tiled=True)
     heating_spectra = call(
         functools.partial(spectra_kernel, band, heats),

time: 34.9 us -> 33.3 us (0.954)
  blocking collectives: 11.7 us -> 9.93 us
    all_to_all x1, blocking collectives: 11.7 us -> 9.93 us  [body(): heat_received = lax.all_to_all(heat_sent, PLACE, 0, 0, tiled=True)]
    pallas_call x2 -> x4, Pallas kernels: 5.03 us -> 5.23 us  [the longest x1 1.98 us: body(): call(functools.partial(second_substep_kernel, levels, heats), [shape((fla...]
  transfers between devices with their start and end apart: 4 -> 4, of which waited for: 1 -> 1; matrix products, arithmetic and copies ran while one was open for 0% -> 0% of each run, Pallas kernels for 3% -> 9%
where the time goes in v4:
time: 33.3 us; the launch traced here: 33 us
  starting transfers between devices  11.6 us (35%)
  blocking collectives  9.93 us (30%)
  Pallas kernels  7.16 us (22%)
  waiting for transfers between devices  3.6 us (11%)
  between operations  0.76 us (2%)
    all_to_all x1, blocking collectives, body(): heat_received = lax.all_to_all(heat_sent, PLACE, 0, 0, tiled=True)  9.93 us
    all_to_all x1, starting transfers between devices, body(): received = lax.all_to_all(sent, PLACE, 0, 0, tiled=True)  8.78 us
    all_to_all x1, waiting for transfers between devices, body(): received = lax.all_to_all(sent, PLACE, 0, 0, tiled=True)  3.59 us
    pallas_call x1, Pallas kernels, body(): call(functools.partial(second_substep_kernel, levels, heats), [shape((fla...  1.98 us
    ppermute x1, starting transfers between devices, body(): lax.ppermute(column, 'lev', [(i, (i + 1) % levels) for i in range(levels)])  1.58 us
    pallas_call x1, Pallas kernels, body(): call(functools.partial(edges_kernel, count, band, width), [halo, halo, sh...  1.25 us
    pallas_call x1, Pallas kernels, body(): call(functools.partial(first_substep_kernel, heats), [shape((6, band + 2,...  1.12 us
    pallas_call x1, Pallas kernels, body(): call(functools.partial(spectra_kernel, band, heats), shape((2, heats, 1,...  0.89 us
  transfers between devices with their start and end apart: 4, of which 1 were waited for; matrix products, arithmetic and copies ran while one was open for 0% of the time, Pallas kernels for 9%

profile of v4, /device:TPU:0, one launch (start us, length us, event | category | flops | bytes accessed | tf_op | source)
XLA Modules:
  0.0 33.0 jit_solution(12590085588186109957)
XLA Ops:
  0.6 1.3 %shard_map.95 = (f32[8,2,8,512]{3,2,1,0:T(8,128)S(1)}, f32[8,2,8,512]{3,2,1,0:T(8,128)S(1)}, s32[1,16]{1,0:T(1,128)S(1)}, bf16[2,4,1024]{2,1,0:T(4,128)(2,1)S(1)...) custom-call(s32[1,16]{1,0:T(1,128)} %bitcast.26, bf16[2,4,1024]{2,1,0:T(4,128)(2,1)} %bitcast.29, ...), custom_call_target="tpu_custom_call" | custom-call | flops 1000000 | tf_op jit(solution)/shard_map/pallas_call | solution.py:462
  1.9 0.5 %collective-permute-start = (f32[8,2,8,512]{3,2,1,0:T(8,128)S(1)}, f32[8,2,8,512]{3,2,1,0:T(8,128)S(1)}, u32[]{:S(2)}, u32[]{:S(2)}) collective-permute-start(f32[8,2,8,512]{3,2,1,0:T(8,128)S(1)} %get-tuple-element.27), channel_id=1, source_target_pairs={{0,1},{1,0},{2,3},{3,2},{8,9},{9,8},{10,11},{11,10},{16,17},{17,16... | collective-permute-start | bytes 786440 | tf_op jit(solution)/shard_map/ppermute | solution.py:480
  2.4 0.7 %collective-permute-start.1 = (f32[8,2,8,512]{3,2,1,0:T(8,128)S(1)}, f32[8,2,8,512]{3,2,1,0:T(8,128)S(1)}, u32[]{:S(2)}, u32[]{:S(2)}) collective-permute-start(f32[8,2,8,512]{3,2,1,0:T(8,128)S(1)} %get-tuple-element.28), channel_id=1, source_target_pairs={{1,2},{2,1},{3,8},{8,3},{9,10},{10,9},{11,16},{16,11},{17,18},{18,... | collective-permute-start | bytes 786440 | tf_op jit(solution)/shard_map/ppermute | solution.py:481
  3.1 0.9 %shard_map.96 = (f32[16,128]{1,0:T(8,128)}, bf16[64,1024]{1,0:T(8,128)(2,1)S(1)}) custom-call(s32[1,16]{1,0:T(1,128)S(1)} %get-tuple-element.21.waves_ref, bf16[2,4,1024]{2,1,0:T(4,128)(2,1)S(1)} %get-tuple-element.22.spectra_ref, bf16[64,1024]{1,0:T(8,128)(2,1)S(1)} %get-tuple-element.23.legendre_ref), custom_call_target="tpu_custom_call" | custom-call | flops 1000000 | tf_op jit(solution)/shard_map/pallas_call | solution.py:482
  4.0 8.8 %all-to-all-start = ((f32[16,1,128]{2,1,0:T(1,128)}), f32[16,1,128]{2,1,0:T(1,128)S(1)}, u32[]{:S(2)}, u32[]{:S(2)}) async-start(f32[16,1,128]{2,1,0:T(1,128)} %bitcast.8), calls=%async_computation | async-start | bytes 16384 | tf_op jit(solution)/shard_map/all_to_all | solution.py:489
  12.8 0.0 collective-permute-done.near_ref
  12.8 0.0 collective-permute-done.1.far_ref
  12.8 0.0 copy-start.1
  12.8 0.0 copy-start.2
  12.8 0.2 shard_map.98
  13.0 0.0 copy-start
  13.0 0.0 copy-start.3
  13.0 0.0 copy-start.4
  13.1 1.6 %collective-permute-start.2 = (f32[6,8,512]{2,1,0:T(8,128)S(1)}, f32[6,8,512]{2,1,0:T(8,128)S(1)}, u32[]{:S(2)}, u32[]{:S(2)}) collective-permute-start(f32[6,8,512]{2,1,0:T(8,128)S(1)} %get-tuple-element.29), channel_id=1, source_target_pairs={{0,4},{4,0},{1,5},{5,1},{2,6},{6,2},{3,7},{7,3},{8,12},{12,8},{9,1... | collective-permute-start | bytes 294920 | tf_op jit(solution)/shard_map/ppermute | solution.py:511
  14.6 0.0 copy-done.1
  14.6 0.0 copy-done.2
  14.6 0.0 copy-done
  14.6 0.0 copy-done.3
  14.7 0.0 copy-done.4
  14.7 0.8 %shard_map.97 = (bf16[128,512]{1,0:T(8,128)(2,1)S(1)}, f32[2,8,128]{2,1,0:T(8,128)S(1)}, f32[112,128]{1,0:T(8,128)S(1)}) custom-call(s32[16]{0:T(128)S(1)} %copy-done, f32[8,8]{1,0:T(8,128)S(1)} %copy-done.1, f32[8]{0:T(128)S(1)} %copy-done.3, f32[3,8]{1,0:T(4,128)S(1)} %copy-done.2, f32[64]{0:T(128)S(1)} %copy-done.4, f32[16,128]{1,0:T(8,128)} %get-tuple-element.24.order_ref), custom_call_target="tpu_custom_call" | custom-call | flops 20000000000 | tf_op jit(solution)/shard_map/pallas_call | solution.py:492
  15.5 3.6 %all-to-all-done = f32[16,1,128]{2,1,0:T(1,128)S(1)} async-done(((f32[16,1,128]{2,1,0:T(1,128)}), f32[16,1,128]{2,1,0:T(1,128)S(1)}, u32[]{:S(2)}, u32[]{:S(2)}) %all-to-all-start) | async-done | bytes 8224 | tf_op jit(solution)/shard_map/all_to_all | solution.py:489
  19.1 1.1 %shard_map.99 = (f32[6,6,8,512]{3,2,1,0:T(8,128)S(1)}, f32[8,6,8,512]{3,2,1,0:T(8,128)S(1)}, f32[6,8,512]{2,1,0:T(8,128)S(1)}, f32[4,8,512]{2,1,0:T(8,128)S(1)}) custom-call(f32[112,128]{1,0:T(8,128)S(1)} %get-tuple-element.25.rows_ref, f32[16,128]{1,0:T(8,128)S(1)} %bitcast.23, f32[8,8,8,512]{3,2,1,0:T(8,128)S(1)} %get-tuple-element.32.cells_ref, ...), custom_call_target="tpu_custom_call" | custom-call | flops 1000000 | tf_op jit(solution)/shard_map/pallas_call | solution.py:522
  20.2 0.0 collective-permute-done.2.above_ref
  20.2 2.0 %shard_map.100 = (f32[1024,128]{1,0:T(8,128)}, f32[16,128]{1,0:T(8,128)S(1)}) custom-call(f32[112,128]{1,0:T(8,128)S(1)} %get-tuple-element.25.rows_ref, f32[6,8,512]{2,1,0:T(8,128)S(1)} %collective-permute-done.2.above_ref, bf16[128,512]{1,0:T(8,128)(2,1)S(1)} %get-tuple-element.30.table_ref, f32[2,8,128]{2,1,0:T(8,128)S(1)} %get-tuple-element.31.turn_ref, ...), custom_call_target="tpu_custom_call" | custom-call | flops 1000000 | tf_op jit(solution)/shard_map/pallas_call | solution.py:533
  22.2 9.9 %all_to_all.22 = f32[16,1,128]{2,1,0:T(1,128)S(1)} all-to-all(f32[16,1,128]{2,1,0:T(1,128)S(1)} %bitcast.25), channel_id=1, replica_groups=mesh['wave'=4,'lev'=2,'grp'=4] {'wave','grp'}, dimensions={0} | all-to-all | bytes 16384 | tf_op jit(solution)/shard_map/all_to_all | solution.py:539
  32.1 0.9 %shard_map.101 = f32[2,3,1,1,1024]{4,3,2,1,0:T(1,128)} custom-call(f32[16,128]{1,0:T(8,128)S(1)} %bitcast.24, bf16[64,1024]{1,0:T(8,128)(2,1)S(1)} %get-tuple-element.39.legendre_ref), custom_call_target="tpu_custom_call" | custom-call | flops 1000000 | tf_op jit(solution)/shard_map/pallas_call | solution.py:540
Async XLA Ops:
  1.9 10.9 %collective-permute-start = (f32[8,2,8,512]{3,2,1,0:T(8,128)S(1)}, f32[8,2,8,512]{3,2,1,0:T(8,128)S(1)}, u32[]{:S(2)}, u32[]{:S(2)}) collective-permute-start(f32[8,2,8,512]{3,2,1,0:T(8,128)S(1)} %get-tuple-element.27), channel_id=1, source_target_pairs={{0,1},{1,0},{2,3},{3,2},{8,9},{9,8},{10,11},{11,10},{16,17},{17,16... | collective-permute-start | bytes 786440 | tf_op jit(solution)/shard_map/ppermute | solution.py:480
  2.4 10.4 %collective-permute-start.1 = (f32[8,2,8,512]{3,2,1,0:T(8,128)S(1)}, f32[8,2,8,512]{3,2,1,0:T(8,128)S(1)}, u32[]{:S(2)}, u32[]{:S(2)}) collective-permute-start(f32[8,2,8,512]{3,2,1,0:T(8,128)S(1)} %get-tuple-element.28), channel_id=1, source_target_pairs={{1,2},{2,1},{3,8},{8,3},{9,10},{10,9},{11,16},{16,11},{17,18},{18,... | collective-permute-start | bytes 786440 | tf_op jit(solution)/shard_map/ppermute | solution.py:481
  4.0 15.1 %all-to-all-start = ((f32[16,1,128]{2,1,0:T(1,128)}), f32[16,1,128]{2,1,0:T(1,128)S(1)}, u32[]{:S(2)}, u32[]{:S(2)}) async-start(f32[16,1,128]{2,1,0:T(1,128)} %bitcast.8), calls=%async_computation | async-start | bytes 16384 | tf_op jit(solution)/shard_map/all_to_all | solution.py:489
  12.8 1.9 %copy-start.1 = (f32[8,8]{1,0:T(8,128)S(1)}, f32[8,8]{1,0:T(8,128)}, u32[]{:S(2)}) copy-start(f32[8,8]{1,0:T(8,128)} %kinetics_ref.1) | copy-start | bytes 772
  12.8 1.9 %copy-start.2 = (f32[3,8]{1,0:T(4,128)S(1)}, f32[3,8]{1,0:T(4,128)}, u32[]{:S(2)}) copy-start(f32[3,8]{1,0:T(4,128)} %weights_ref.1) | copy-start | bytes 292
  13.0 1.6 %copy-start = (s32[16]{0:T(128)S(1)}, s32[16]{0:T(128)}, u32[]{:S(2)}) copy-start(s32[16]{0:T(128)} %waves_ref.1) | copy-start | bytes 196
  13.0 1.6 %copy-start.3 = (f32[8]{0:T(128)S(1)}, f32[8]{0:T(128)}, u32[]{:S(2)}) copy-start(f32[8]{0:T(128)} %photolysis_ref.1) | copy-start | bytes 100
  13.0 1.6 %copy-start.4 = (f32[64]{0:T(128)S(1)}, f32[64]{0:T(128)}, u32[]{:S(2)}) copy-start(f32[64]{0:T(128)} %quad_ref.1) | copy-start | bytes 772
  13.1 7.2 %collective-permute-start.2 = (f32[6,8,512]{2,1,0:T(8,128)S(1)}, f32[6,8,512]{2,1,0:T(8,128)S(1)}, u32[]{:S(2)}, u32[]{:S(2)}) collective-permute-start(f32[6,8,512]{2,1,0:T(8,128)S(1)} %get-tuple-element.29), channel_id=1, source_target_pairs={{0,4},{4,0},{1,5},{5,1},{2,6},{6,2},{3,7},{7,3},{8,12},{12,8},{9,1... | collective-permute-start | bytes 294920 | tf_op jit(solution)/shard_map/ppermute | solution.py:511

commit v5 on v4

--- a/solution.py
+++ b/solution.py
@@ -21,9 +21,9 @@
     return high, value - high.astype(f32)
 
 
-def call(body, out_shape, in_spaces, scratch=(), flops=1_000_000):
+def call(body, out_shape, in_spaces, scratch=(), flops=1_000_000, out_space=pltpu.VMEM):
     several = isinstance(out_shape, (list, tuple))
-    spec = pl.BlockSpec(memory_space=pltpu.VMEM)
+    spec = pl.BlockSpec(memory_space=out_space)
     return pl.pallas_call(
         body,
         out_shape=out_shape,
@@ -85,28 +85,25 @@
     spectra_hbm,
     legendre_hbm,
     flat_hbm,
+    far_ref,
     near_ref,
-    far_ref,
     waves_ref,
     spectra_ref,
     legendre_ref,
     flat_ref,
     sems,
 ):
-    pairs = (
-        (flat_hbm, flat_ref),
-        (legendre_hbm, legendre_ref),
-        (spectra_hbm, spectra_ref),
-        (waves_hbm, waves_ref),
-    )
+    each = flat_hbm.shape[0] // count
+    pairs = [(flat_hbm.at[pl.ds(t * each, each)], flat_ref.at[pl.ds(t * each, each)]) for t in range(count)]
+    pairs += [(legendre_hbm, legendre_ref), (spectra_hbm, spectra_ref), (waves_hbm, waves_ref)]
     copies = [pltpu.make_async_copy(a, b, sems.at[n]) for n, (a, b) in enumerate(pairs)]
     for copy in copies:
         copy.start()
-    copies[0].wait()
     even = lax.axis_index(PLACE) % 2 == 0
 
     def fill(near_first, far_first):
         for t in range(count):
+            copies[t].wait()
             for r in range(width):
                 near_ref[t, r] = load_row(flat_ref, count, band, t, near_first + r)
                 far_ref[t, r] = load_row(flat_ref, count, band, t, far_first + r)
@@ -119,7 +116,7 @@
     def _():
         fill(0, band - width)
 
-    for copy in copies[1:]:
+    for copy in copies[count:]:
         copy.wait()
 
 
@@ -154,7 +151,7 @@
 
 
 def table_kernel(
-    waves_ref, kinetics_ref, photolysis_ref, weights_ref, quad_ref, order_ref, table_ref, turn_ref, rows_ref
+    waves_ref, kinetics_ref, photolysis_ref, weights_ref, quad_ref, order_ref, table_ref, turned_ref, turn_ref, rows_ref
 ):
     span = table_ref.shape[1]
     waves = table_ref.shape[0] // 8
@@ -185,6 +182,8 @@
         both = split_bf16(cosine) + split_bf16(-sine)
         for n, part in enumerate((0, 2, 1, 3) * 2):
             table_ref[n * waves : (n + 1) * waves, columns] = both[part].astype(bf16)
+        stacked = jnp.concatenate([both[part].astype(f32) for part in (0, 2, 1, 3) * 2], axis=0)
+        turned_ref[columns, :] = stacked.T.astype(bf16)
 
     count, heats = kinetics_ref.shape[0], weights_ref.shape[0]
     band = quad_ref.shape[0] // lax.axis_size(PLACE)
@@ -192,6 +191,20 @@
     values = [kinetics_ref[i, j] for i in range(count) for j in range(count)]
     values += [photolysis_ref[i] for i in range(count)]
     values += [weights_ref[k, i] for k in range(heats) for i in range(count)]
+    yields = [photolysis_ref[i] for i in range(count)]
+
+    def product(row, column):
+        total = row[0] * column[0]
+        for a, b in zip(row[1:], column[1:]):
+            total = total + a * b
+        return total
+
+    mixed = [product([kinetics_ref[i, j] for j in range(count)], yields) for i in range(count)]
+    weights = [[weights_ref[k, i] for i in range(count)] for k in range(heats)]
+    values += mixed
+    values += [product(row, yields) for row in weights]
+    values += [product(row, mixed) for row in weights]
+    values += [0.0] * (-len(values) % SUB)
     values += [quad_ref[first + r] for k in range(heats) for r in range(band)]
     for n, value in enumerate(values):
         rows_ref[n : n + 1, :] = jnp.full((1, LANES), value, f32)
@@ -221,6 +234,11 @@
         fill(near_ref, far_ref)
 
 
+def scalar_rows(count, heats):
+    rows = count * (count + 2 + heats) + 2 * heats
+    return -(-rows // SUB) * SUB
+
+
 class Scalars:
     def __init__(self, ref, count, heats):
         self.ref, self.count, self.heats = ref, count, heats
@@ -237,8 +255,17 @@
     def weight(self, k, i):
         return self.row(self.count * (self.count + 1 + k) + i)
 
+    def mixed_yield(self, i):
+        return self.row(self.count * (self.count + 1 + self.heats) + i)
+
+    def heat_yield(self, k):
+        return self.row(self.count * (self.count + 2 + self.heats) + k)
+
+    def heat_mixed_yield(self, k):
+        return self.row(self.count * (self.count + 2 + self.heats) + self.heats + k)
+
     def quad(self, size):
-        first = self.count * (self.count + 1 + self.heats)
+        first = scalar_rows(self.count, self.heats)
         return self.ref[first : first + size, :][:, :1]
 
 
@@ -263,7 +290,7 @@
     )
 
 
-def first_substep_kernel(
+def substeps_kernel(
     heats,
     rows_ref,
     received_ref,
@@ -273,7 +300,10 @@
     coeffs_ref,
     base_ref,
     lead_ref,
+    second_lead_ref,
+    heat_ref,
     warm_ref,
+    middle,
 ):
     count, depth, _, span = cells_ref.shape
     rows = lead_ref.shape[0]
@@ -341,68 +371,76 @@
         for i in range(count):
             mixed = combine([scalars.kinetics(i, j) for j in range(count)], moved)
             out = [a + b * c for a, b, c in zip(moved[i], rate, mixed)]
-            base_ref[i, r] = jnp.concatenate(out, axis=1)
-
-
-def second_substep_kernel(
-    levels,
-    heats,
-    rows_ref,
-    above_ref,
-    table_ref,
-    turn_ref,
-    coeffs_ref,
-    base_ref,
-    lead_ref,
-    warm_ref,
-    flat_ref,
-    sent_ref,
-    middle,
-):
-    count, rows, _, span = base_ref.shape
-    band = rows - 2
-    waves = table_ref.shape[0] // 8
-    lons = span * SUB
-    scalars = Scalars(rows_ref, count, heats)
-    turn_cos, turn_sin = turn_ref[0], turn_ref[1]
-    covered = lax.axis_index("lev") > 0
-    photo = []
-    for r in range(rows):
-        overhead = jnp.where(covered, above_ref[r], 0.0)
-        photo.append(0.2 * jnp.exp(overhead * (-2.0 / levels)))
-        lit = cut(photo[r] * lead_ref[r])
-        for t in range(count):
-            source = scalars.photolysis(t)
-            parts = [old + source * tile for old, tile in zip(cut(base_ref[t, r]), lit)]
-            middle[t, r] = jnp.concatenate(parts, axis=1)
-
-    heated = [[None] * band for _ in range(heats)]
+            middle[i, r] = jnp.concatenate(out, axis=1)
+
     for r in range(band):
         moved = [
             stencil(coeffs_ref, r + 1, middle[t, r + 1], middle[t, r], middle[t, r + 2])
             for t in range(count)
         ]
-        lit = cut(photo[r + 1] * moved[0])
+        second_lead_ref[r] = moved[0]
+        moved = [cut(value) for value in moved]
         rate = cut(coeffs_ref[5, r + 1])
-        moved = [cut(value) for value in moved]
-        out = []
+        outs = []
         for i in range(count):
             mixed = combine([scalars.kinetics(i, j) for j in range(count)], moved)
-            source = scalars.photolysis(i)
-            out.append(
-                [a + b * c + source * d for a, b, c, d in zip(moved[i], rate, mixed, lit)]
-            )
-        for t in range(count):
-            store_row(flat_ref, count, band, t, r, out[t])
+            outs.append([a + b * c for a, b, c in zip(moved[i], rate, mixed)])
+            base_ref[i, r] = jnp.concatenate(outs[i], axis=1)
         for k in range(heats):
-            total = combine([scalars.weight(k, i) for i in range(count)], out)
-            heated[k][r] = jnp.concatenate(total, axis=1) * warm_ref[r]
+            total = combine([scalars.weight(k, i) for i in range(count)], outs)
+            heat_ref[k, r] = jnp.concatenate(total, axis=1)
+
+
+def analysis_kernel(
+    levels,
+    count,
+    rows_ref,
+    above_ref,
+    turned_ref,
+    turn_ref,
+    coeffs_ref,
+    lead_ref,
+    second_lead_ref,
+    heat_ref,
+    warm_ref,
+    u_ref,
+    v_ref,
+    sent_ref,
+):
+    rows, _, span = lead_ref.shape
+    band = rows - 2
+    heats = heat_ref.shape[0]
+    waves = turned_ref.shape[1] // 8
+    lons = span * SUB
+    scalars = Scalars(rows_ref, count, heats)
+    turn_cos, turn_sin = turn_ref[0], turn_ref[1]
+    covered = lax.axis_index("lev") > 0
+    photo, source = [], []
+    for r in range(rows):
+        overhead = jnp.where(covered, above_ref[r], 0.0)
+        photo.append(0.2 * jnp.exp(overhead * (-2.0 / levels)))
+        source.append(photo[r] * lead_ref[r])
+
+    heated = [[None] * band for _ in range(heats)]
+    for r in range(band):
+        moved = cut(stencil(coeffs_ref, r + 1, source[r + 1], source[r], source[r + 2]))
+        rate, light = cut(coeffs_ref[5, r + 1]), cut(photo[r + 1])
+        own = scalars.photolysis(0)
+        v = [a * b for a, b in zip(rate, moved)]
+        lead = cut(second_lead_ref[r])
+        u = [m + p * (a + own * m) for m, p, a in zip(moved, light, lead)]
+        u_ref[r] = jnp.concatenate(u, axis=1)
+        v_ref[r] = jnp.concatenate(v, axis=1)
+        for k in range(heats):
+            by_u, by_v = scalars.heat_yield(k), scalars.heat_mixed_yield(k)
+            parts = cut(heat_ref[k, r])
+            parts = [a + by_u * b + by_v * c for a, b, c in zip(parts, u, v)]
+            heated[k][r] = jnp.concatenate(parts, axis=1) * warm_ref[r]
 
     heat = jnp.concatenate([row for group in heated for row in group], axis=0)
     high, low = split_bf16(heat)
-    nt = (((1,), (1,)), ((), ()))
-    by_high = lax.dot_general(high, table_ref[...], nt, preferred_element_type=f32)
-    by_low = lax.dot_general(low.astype(bf16), table_ref[...], nt, preferred_element_type=f32)
+    by_high = jnp.dot(high, turned_ref[...], preferred_element_type=f32)
+    by_low = jnp.dot(low.astype(bf16), turned_ref[...], preferred_element_type=f32)
     wide = 8 * waves
     total = by_high + pltpu.roll(by_high, wide - 2 * waves, 1) + by_low
     sums_a, sums_b = [], []
@@ -426,8 +464,24 @@
     sent_ref[...] = jnp.concatenate([both, filler], axis=0).T[:waves]
 
 
-def spectra_kernel(band, heats, received_ref, legendre_ref, out_ref, spread):
+def last_kernel(
+    band,
+    heats,
+    received_ref,
+    legendre_ref,
+    rows_ref,
+    base_ref,
+    u_ref,
+    v_ref,
+    spectra_hbm,
+    flat_hbm,
+    spread,
+    spectra_ref,
+    flat_ref,
+    sems,
+):
     places = received_ref.shape[0]
+    count = base_ref.shape[0]
     received = received_ref[...]
     for r in range(band):
         spread[pl.ds(r, places, stride=band), :] = pltpu.roll(received, (LANES - r) % LANES, 1)
@@ -437,7 +491,21 @@
     for p in range(2):
         for k in range(heats):
             at = p * size + k * band
-            out_ref[p, k, 0] = out[at : at + 1]
+            spectra_ref[p, k, 0] = out[at : at + 1]
+    copies = [pltpu.make_async_copy(spectra_ref, spectra_hbm, sems.at[count])]
+    copies[0].start()
+    scalars = Scalars(rows_ref, count, heats)
+    each = flat_hbm.shape[0] // count
+    for t in range(count):
+        by_u, by_v = scalars.photolysis(t), scalars.mixed_yield(t)
+        for r in range(band):
+            parts = zip(cut(base_ref[t, r]), cut(u_ref[r]), cut(v_ref[r]))
+            store_row(flat_ref, count, band, t, r, [a + by_u * b + by_v * c for a, b, c in parts])
+        mine = pl.ds(t * each, each)
+        copies.append(pltpu.make_async_copy(flat_ref.at[mine], flat_hbm.at[mine], sems.at[t]))
+        copies[-1].start()
+    for copy in copies:
+        copy.wait()
 
 
 def body(spectra, legendre, wavenumbers, quad_weights, tracers, kinetics, photolysis, heat_weights):
@@ -459,7 +527,7 @@
     far_pairs = [(i, ((i + 1) ^ 1) - 1) for i in range(1, places - 1)]
 
     halo = shape((count, width, SUB, span), f32)
-    near, far, waves_in, spectra_in, legendre_in, flat = call(
+    far, near, waves_in, spectra_in, legendre_in, flat = call(
         functools.partial(edges_kernel, count, band, width),
         [
             halo,
@@ -470,15 +538,15 @@
             shape((flat_rows, LANES), f32),
         ],
         [pltpu.HBM] * 4,
-        [pltpu.SemaphoreType.DMA((4,))],
+        [pltpu.SemaphoreType.DMA((count + 3,))],
     )(
         *(
             pltpu.with_memory_space_constraint(x, pltpu.HBM)
             for x in (wavenumbers.reshape(1, waves), spectra[:, :, 0, 0], legendre_t, flat)
         )
     )
+    far = lax.ppermute(far, PLACE, far_pairs)
     near = lax.ppermute(near, PLACE, near_pairs)
-    far = lax.ppermute(far, PLACE, far_pairs)
     sent, masked = call(
         functools.partial(fourier_kernel, band),
         [shape((places, LANES), f32), shape((lats, degrees), bf16)],
@@ -488,11 +556,12 @@
     )(waves_in, spectra_in, legendre_in)
     received = lax.all_to_all(sent, PLACE, 0, 0, tiled=True)
 
-    constants = count * (count + 1 + heats)
-    table, turn, scalars = call(
+    constants = scalar_rows(count, heats)
+    table, turned, turn, scalars = call(
         table_kernel,
         [
             shape((8 * waves, span), bf16),
+            shape((span, 8 * waves), bf16),
             shape((2, SUB, 8 * waves), f32),
             shape((constants + 2 * SUB, LANES), f32),
         ],
@@ -518,31 +587,38 @@
         )
         reach *= 2
 
-    field = shape((band + 2, SUB, span), f32)
-    coeffs, base, lead, warm = call(
-        functools.partial(first_substep_kernel, heats),
+    inner, outer = (band, SUB, span), (band + 2, SUB, span)
+    coeffs, base, lead, second_lead, heat, warm = call(
+        functools.partial(substeps_kernel, heats),
         [
-            shape((6, band + 2, SUB, span), f32),
-            shape((count, band + 2, SUB, span), f32),
-            field,
-            shape((band, SUB, span), f32),
+            shape((6, *outer), f32),
+            shape((count, *inner), f32),
+            shape(outer, f32),
+            shape(inner, f32),
+            shape((heats, *inner), f32),
+            shape(inner, f32),
         ],
         [VM] * 5,
-        flops=1000000,
+        [pltpu.VMEM((count, *outer), f32)],
     )(scalars, received, cells, table, turn)
-    flat_out, heat_sent = call(
-        functools.partial(second_substep_kernel, levels, heats),
-        [shape((flat_rows, LANES), f32), shape((waves, LANES), f32)],
-        [VM] * 8,
-        [pltpu.VMEM((count, band + 2, SUB, span), f32)],
-    )(scalars, above, table, turn, coeffs, base, lead, warm)
+    u, v, heat_sent = call(
+        functools.partial(analysis_kernel, levels, count),
+        [shape(inner, f32), shape(inner, f32), shape((waves, LANES), f32)],
+        [VM] * 9,
+    )(scalars, above, turned, turn, coeffs, lead, second_lead, heat, warm)
     heat_received = lax.all_to_all(heat_sent, PLACE, 0, 0, tiled=True)
-    heating_spectra = call(
-        functools.partial(spectra_kernel, band, heats),
-        shape((2, heats, 1, 1, degrees), f32),
-        [VM, VM],
-        [pltpu.VMEM((lats, LANES), f32)],
-    )(heat_received, masked)
+    heating_spectra, flat_out = call(
+        functools.partial(last_kernel, band, heats),
+        [shape((2, heats, 1, 1, degrees), f32), shape((flat_rows, LANES), f32)],
+        [VM] * 6,
+        [
+            pltpu.VMEM((lats, LANES), f32),
+            pltpu.VMEM((2, heats, 1, 1, degrees), f32),
+            pltpu.VMEM((flat_rows, LANES), f32),
+            pltpu.SemaphoreType.DMA((count + 1,)),
+        ],
+        out_space=pltpu.HBM,
+    )(heat_received, masked, scalars, base, u, v)
     return (unfold(flat_out, count, band)[:, None], heating_spectra)
 
 

time: 33.3 us -> 32.1 us (0.964)
  blocking collectives: 9.93 us -> 9.22 us
    all_to_all x1, blocking collectives: 9.93 us -> 9.22 us  [body(): heat_received = lax.all_to_all(heat_sent, PLACE, 0, 0, tiled=True)]
  transfers between devices with their start and end apart: 4 -> 4, of which waited for: 1 -> 1; matrix products, arithmetic and copies ran while one was open for 0% -> 0% of each run, Pallas kernels for 9% -> 12%
where the time goes in v5:
time: 32.1 us; the launch traced here: 31.9 us
  starting transfers between devices  11.5 us (36%)
  blocking collectives  9.22 us (29%)
  Pallas kernels  6.85 us (21%)
  waiting for transfers between devices  3.46 us (11%)
  between operations  0.76 us (2%)
    all_to_all x1, blocking collectives, body(): heat_received = lax.all_to_all(heat_sent, PLACE, 0, 0, tiled=True)  9.22 us
    all_to_all x1, starting transfers between devices, body(): received = lax.all_to_all(sent, PLACE, 0, 0, tiled=True)  8.78 us
    all_to_all x1, waiting for transfers between devices, body(): received = lax.all_to_all(sent, PLACE, 0, 0, tiled=True)  3.45 us
    pallas_call x1, Pallas kernels, body(): call(functools.partial(substeps_kernel, heats), [shape((6, *outer), f32),...  1.86 us
    ppermute x1, starting transfers between devices, body(): lax.ppermute(column, 'lev', [(i, (i + 1) % levels) for i in range(levels)])  1.58 us
    pallas_call x1, Pallas kernels, body(): call(functools.partial(edges_kernel, count, band, width), [halo, halo, sh...  1.27 us
    pallas_call x1, Pallas kernels, body(): call(functools.partial(last_kernel, band, heats), [shape((2, heats, 1, 1,...  1.16 us
    pallas_call x1, Pallas kernels, body(): call(table_kernel, [shape((8 * waves, span), bf16), shape((span, 8 * wave...  0.97 us
  transfers between devices with their start and end apart: 4, of which 1 were waited for; matrix products, arithmetic and copies ran while one was open for 0% of the time, Pallas kernels for 12%

profile of v5, /device:TPU:0, one launch (start us, length us, event | category | flops | bytes accessed | tf_op | source)
XLA Modules:
  0.0 31.9 jit_solution(7603795171988855595)
XLA Ops:
  0.6 1.3 %shard_map.95 = (f32[8,2,8,512]{3,2,1,0:T(8,128)S(1)}, f32[8,2,8,512]{3,2,1,0:T(8,128)S(1)}, s32[1,16]{1,0:T(1,128)S(1)}, bf16[2,4,1024]{2,1,0:T(4,128)(2,1)S(1)...) custom-call(s32[1,16]{1,0:T(1,128)} %bitcast.26, bf16[2,4,1024]{2,1,0:T(4,128)(2,1)} %bitcast.29, ...), custom_call_target="tpu_custom_call" | custom-call | flops 1000000 | tf_op jit(solution)/shard_map/pallas_call | solution.py:530
  1.9 0.5 %collective-permute-start = (f32[8,2,8,512]{3,2,1,0:T(8,128)S(1)}, f32[8,2,8,512]{3,2,1,0:T(8,128)S(1)}, u32[]{:S(2)}, u32[]{:S(2)}) collective-permute-start(f32[8,2,8,512]{3,2,1,0:T(8,128)S(1)} %get-tuple-element.33), channel_id=1, source_target_pairs={{0,1},{1,0},{2,3},{3,2},{8,9},{9,8},{10,11},{11,10},{16,17},{17,16... | collective-permute-start | bytes 786440 | tf_op jit(solution)/shard_map/ppermute | solution.py:549
  2.4 0.7 %collective-permute-start.1 = (f32[8,2,8,512]{3,2,1,0:T(8,128)S(1)}, f32[8,2,8,512]{3,2,1,0:T(8,128)S(1)}, u32[]{:S(2)}, u32[]{:S(2)}) collective-permute-start(f32[8,2,8,512]{3,2,1,0:T(8,128)S(1)} %get-tuple-element.34), channel_id=1, source_target_pairs={{1,2},{2,1},{3,8},{8,3},{9,10},{10,9},{11,16},{16,11},{17,18},{18,... | collective-permute-start | bytes 786440 | tf_op jit(solution)/shard_map/ppermute | solution.py:548
  3.1 0.9 %shard_map.96 = (f32[16,128]{1,0:T(8,128)}, bf16[64,1024]{1,0:T(8,128)(2,1)S(1)}) custom-call(s32[1,16]{1,0:T(1,128)S(1)} %get-tuple-element.27.waves_ref, bf16[2,4,1024]{2,1,0:T(4,128)(2,1)S(1)} %get-tuple-element.28.spectra_ref, bf16[64,1024]{1,0:T(8,128)(2,1)S(1)} %get-tuple-element.29.legendre_ref), custom_call_target="tpu_custom_call" | custom-call | flops 1000000 | tf_op jit(solution)/shard_map/pallas_call | solution.py:550
  4.0 8.8 %all-to-all-start = ((f32[16,1,128]{2,1,0:T(1,128)}), f32[16,1,128]{2,1,0:T(1,128)S(1)}, u32[]{:S(2)}, u32[]{:S(2)}) async-start(f32[16,1,128]{2,1,0:T(1,128)} %bitcast.8), calls=%async_computation | async-start | bytes 16384 | tf_op jit(solution)/shard_map/all_to_all | solution.py:557
  12.8 0.0 collective-permute-done.near_ref
  12.8 0.0 collective-permute-done.1.far_ref
  12.8 0.0 copy-start.1
  12.8 0.0 copy-start.2
  12.8 0.2 shard_map.98
  13.0 0.0 copy-start
  13.0 0.0 copy-start.3
  13.1 0.0 copy-start.4
  13.1 1.6 %collective-permute-start.2 = (f32[6,8,512]{2,1,0:T(8,128)S(1)}, f32[6,8,512]{2,1,0:T(8,128)S(1)}, u32[]{:S(2)}, u32[]{:S(2)}) collective-permute-start(f32[6,8,512]{2,1,0:T(8,128)S(1)} %get-tuple-element.35), channel_id=1, source_target_pairs={{0,4},{4,0},{1,5},{5,1},{2,6},{6,2},{3,7},{7,3},{8,12},{12,8},{9,1... | collective-permute-start | bytes 294920 | tf_op jit(solution)/shard_map/ppermute | solution.py:580
  14.6 0.0 copy-done.1
  14.7 0.0 copy-done.2
  14.7 0.0 copy-done
  14.7 0.0 copy-done.3
  14.7 0.0 copy-done.4
  14.7 1.0 %shard_map.97 = (bf16[128,512]{1,0:T(8,128)(2,1)S(1)}, bf16[512,128]{1,0:T(8,128)(2,1)S(1)}, f32[2,8,128]{2,1,0:T(8,128)S(1)}, f32[128,128]{1,0:T(8,128)S(1)}) custom-call(s32[16]{0:T(128)S(1)} %copy-done, f32[8,8]{1,0:T(8,128)S(1)} %copy-done.1, f32[8]{0:T(128)S(1)} %copy-done.3, f32[3,8]{1,0:T(4,128)S(1)} %copy-done.2, f32[64]{0:T(128)S(1)} %copy-done.4, ...), custom_call_target="tpu_custom_call" | custom-call | flops 20000000000 | tf_op jit(solution)/shard_map/pallas_call | solution.py:560
  15.7 3.5 %all-to-all-done = f32[16,1,128]{2,1,0:T(1,128)S(1)} async-done(((f32[16,1,128]{2,1,0:T(1,128)}), f32[16,1,128]{2,1,0:T(1,128)S(1)}, u32[]{:S(2)}, u32[]{:S(2)}) %all-to-all-start) | async-done | bytes 8224 | tf_op jit(solution)/shard_map/all_to_all | solution.py:557
  19.1 1.9 %shard_map.99 = (f32[6,6,8,512]{3,2,1,0:T(8,128)S(1)}, f32[8,4,8,512]{3,2,1,0:T(8,128)S(1)}, f32[6,8,512]{2,1,0:T(8,128)S(1)}, f32[4,8,512]{2,1,0:T(8,128)S(1)},...) custom-call(f32[128,128]{1,0:T(8,128)S(1)} %get-tuple-element.31.rows_ref, f32[16,128]{1,0:T(8,128)S(1)} %bitcast.23, ...), custom_call_target="tpu_custom_call" | custom-call | flops 1000000 | tf_op jit(solution)/shard_map/pallas_call | solution.py:591
  21.0 0.0 collective-permute-done.2.above_ref
  21.0 0.5 %shard_map.100 = (f32[4,8,512]{2,1,0:T(8,128)S(1)}, f32[4,8,512]{2,1,0:T(8,128)S(1)}, f32[16,128]{1,0:T(8,128)S(1)}) custom-call(f32[128,128]{1,0:T(8,128)S(1)} %get-tuple-element.31.rows_ref, f32[6,8,512]{2,1,0:T(8,128)S(1)} %collective-permute-done.2.above_ref, bf16[512,128]{1,0:T(8,128)(2,1)S(1)} %get-tuple-element.36.turned_ref, ...), custom_call_target="tpu_custom_call" | custom-call | flops 1000000 | tf_op jit(solution)/shard_map/pallas_call | solution.py:604
  21.5 9.2 %all_to_all.22 = f32[16,1,128]{2,1,0:T(1,128)S(1)} all-to-all(f32[16,1,128]{2,1,0:T(1,128)S(1)} %bitcast.25), channel_id=1, replica_groups=mesh['wave'=4,'lev'=2,'grp'=4] {'wave','grp'}, dimensions={0} | all-to-all | bytes 16384 | tf_op jit(solution)/shard_map/all_to_all | solution.py:609
  30.7 1.2 %shard_map.101 = (f32[2,3,1,1,1024]{4,3,2,1,0:T(1,128)}, f32[1024,128]{1,0:T(8,128)}) custom-call(f32[16,128]{1,0:T(8,128)S(1)} %bitcast.24, bf16[64,1024]{1,0:T(8,128)(2,1)S(1)} %get-tuple-element.46.legendre_ref, f32[128,128]{1,0:T(8,128)S(1)} %get-tuple-element.31.rows_ref, f32[8,4,8,512]{3,2,1,0:T(8,128)S(1)} %get-tuple-element.47.base_ref, ...), custom_call_target="tpu_custom_call" | custom-call | flops 1000000 | tf_op jit(solution)/shard_map/pallas_call | solution.py:610
Async XLA Ops:
  1.9 10.9 %collective-permute-start = (f32[8,2,8,512]{3,2,1,0:T(8,128)S(1)}, f32[8,2,8,512]{3,2,1,0:T(8,128)S(1)}, u32[]{:S(2)}, u32[]{:S(2)}) collective-permute-start(f32[8,2,8,512]{3,2,1,0:T(8,128)S(1)} %get-tuple-element.33), channel_id=1, source_target_pairs={{0,1},{1,0},{2,3},{3,2},{8,9},{9,8},{10,11},{11,10},{16,17},{17,16... | collective-permute-start | bytes 786440 | tf_op jit(solution)/shard_map/ppermute | solution.py:549
  2.4 10.4 %collective-permute-start.1 = (f32[8,2,8,512]{3,2,1,0:T(8,128)S(1)}, f32[8,2,8,512]{3,2,1,0:T(8,128)S(1)}, u32[]{:S(2)}, u32[]{:S(2)}) collective-permute-start(f32[8,2,8,512]{3,2,1,0:T(8,128)S(1)} %get-tuple-element.34), channel_id=1, source_target_pairs={{1,2},{2,1},{3,8},{8,3},{9,10},{10,9},{11,16},{16,11},{17,18},{18,... | collective-permute-start | bytes 786440 | tf_op jit(solution)/shard_map/ppermute | solution.py:548
  4.0 15.1 %all-to-all-start = ((f32[16,1,128]{2,1,0:T(1,128)}), f32[16,1,128]{2,1,0:T(1,128)S(1)}, u32[]{:S(2)}, u32[]{:S(2)}) async-start(f32[16,1,128]{2,1,0:T(1,128)} %bitcast.8), calls=%async_computation | async-start | bytes 16384 | tf_op jit(solution)/shard_map/all_to_all | solution.py:557
  12.8 1.9 %copy-start.1 = (f32[8,8]{1,0:T(8,128)S(1)}, f32[8,8]{1,0:T(8,128)}, u32[]{:S(2)}) copy-start(f32[8,8]{1,0:T(8,128)} %kinetics_ref.1) | copy-start | bytes 772
  12.8 1.8 %copy-start.2 = (f32[3,8]{1,0:T(4,128)S(1)}, f32[3,8]{1,0:T(4,128)}, u32[]{:S(2)}) copy-start(f32[3,8]{1,0:T(4,128)} %weights_ref.1) | copy-start | bytes 292
  13.0 1.6 %copy-start = (s32[16]{0:T(128)S(1)}, s32[16]{0:T(128)}, u32[]{:S(2)}) copy-start(s32[16]{0:T(128)} %waves_ref.1) | copy-start | bytes 196
  13.0 1.6 %copy-start.3 = (f32[8]{0:T(128)S(1)}, f32[8]{0:T(128)}, u32[]{:S(2)}) copy-start(f32[8]{0:T(128)} %photolysis_ref.1) | copy-start | bytes 100
  13.1 1.6 %copy-start.4 = (f32[64]{0:T(128)S(1)}, f32[64]{0:T(128)}, u32[]{:S(2)}) copy-start(f32[64]{0:T(128)} %quad_ref.1) | copy-start | bytes 772
  13.1 7.9 %collective-permute-start.2 = (f32[6,8,512]{2,1,0:T(8,128)S(1)}, f32[6,8,512]{2,1,0:T(8,128)S(1)}, u32[]{:S(2)}, u32[]{:S(2)}) collective-permute-start(f32[6,8,512]{2,1,0:T(8,128)S(1)} %get-tuple-element.35), channel_id=1, source_target_pairs={{0,4},{4,0},{1,5},{5,1},{2,6},{6,2},{3,7},{7,3},{8,12},{12,8},{9,1... | collective-permute-start | bytes 294920 | tf_op jit(solution)/shard_map/ppermute | solution.py:580

commit v6 on v5

--- a/solution.py
+++ b/solution.py
@@ -35,10 +35,10 @@
     )
 
 
-def fold(tracers):
+def halves(tracers):
     count, band, lons = tracers.shape
-    cut = tracers.reshape(count, band, lons // LANES, LANES)
-    return cut.transpose(0, 2, 1, 3).reshape(-1, LANES)
+    cut = tracers.reshape(count, 2, band // 2, lons // LANES, LANES)
+    return cut.transpose(0, 3, 1, 2, 4).reshape(-1, 2, band // 2, LANES)
 
 
 def unfold(flat, count, band):
@@ -78,45 +78,29 @@
 
 
 def edges_kernel(
-    count,
-    band,
-    width,
     waves_hbm,
     spectra_hbm,
     legendre_hbm,
-    flat_hbm,
+    halves_hbm,
+    near_ref,
     far_ref,
-    near_ref,
     waves_ref,
     spectra_ref,
     legendre_ref,
-    flat_ref,
     sems,
 ):
-    each = flat_hbm.shape[0] // count
-    pairs = [(flat_hbm.at[pl.ds(t * each, each)], flat_ref.at[pl.ds(t * each, each)]) for t in range(count)]
-    pairs += [(legendre_hbm, legendre_ref), (spectra_hbm, spectra_ref), (waves_hbm, waves_ref)]
+    odd = lax.axis_index(PLACE) % 2
+    pairs = (
+        (halves_hbm.at[:, 1 - odd], near_ref),
+        (halves_hbm.at[:, odd], far_ref),
+        (legendre_hbm, legendre_ref),
+        (spectra_hbm, spectra_ref),
+        (waves_hbm, waves_ref),
+    )
     copies = [pltpu.make_async_copy(a, b, sems.at[n]) for n, (a, b) in enumerate(pairs)]
     for copy in copies:
         copy.start()
-    even = lax.axis_index(PLACE) % 2 == 0
-
-    def fill(near_first, far_first):
-        for t in range(count):
-            copies[t].wait()
-            for r in range(width):
-                near_ref[t, r] = load_row(flat_ref, count, band, t, near_first + r)
-                far_ref[t, r] = load_row(flat_ref, count, band, t, far_first + r)
-
-    @pl.when(even)
-    def _():
-        fill(band - width, 0)
-
-    @pl.when(jnp.logical_not(even))
-    def _():
-        fill(0, band - width)
-
-    for copy in copies[count:]:
+    for copy in copies:
         copy.wait()
 
 
@@ -210,28 +194,35 @@
         rows_ref[n : n + 1, :] = jnp.full((1, LANES), value, f32)
 
 
-def ready_kernel(count, band, flat_ref, near_ref, far_ref, order_ref, cells_ref, column_ref):
+def ready_kernel(
+    count,
+    width,
+    own_far_ref,
+    own_near_ref,
+    near_ref,
+    far_ref,
+    order_ref,
+    cells_ref,
+    column_ref,
+):
     even = lax.axis_index(PLACE) % 2 == 0
-    width = near_ref.shape[1]
-
-    def fill(north, south):
+
+    def fill(*refs):
         for t in range(count):
-            rows = [north[t, r] for r in range(width)]
-            rows += [load_row(flat_ref, count, band, t, r) for r in range(band)]
-            rows += [south[t, r] for r in range(width)]
+            rows = [load_row(ref, count, width, t, r) for ref in refs for r in range(width)]
             for r, row in enumerate(rows):
                 cells_ref[t, r] = row
             if t == 0:
-                for r in range(band + 2):
+                for r in range(len(rows) - 2 * (width - 1)):
                     column_ref[r] = rows[r + width - 1]
 
     @pl.when(even)
     def _():
-        fill(far_ref, near_ref)
+        fill(far_ref, own_far_ref, own_near_ref, near_ref)
 
     @pl.when(jnp.logical_not(even))
     def _():
-        fill(near_ref, far_ref)
+        fill(near_ref, own_near_ref, own_far_ref, far_ref)
 
 
 def scalar_rows(count, heats):
@@ -515,38 +506,42 @@
     waves = wavenumbers.shape[0]
     heats = heat_weights.shape[0]
     lats, degrees = legendre.shape[2], legendre.shape[1]
-    width = 2
+    width = band // 2
     span = lons // SUB
     flat_rows = count * band * lons // LANES
     VM, SM = pltpu.VMEM, pltpu.SMEM
     legendre_t = legendre[0].T
-    flat = fold(tracers[:, 0])
     shape = jax.ShapeDtypeStruct
 
     near_pairs = [(i, i ^ 1) for i in range(places)]
     far_pairs = [(i, ((i + 1) ^ 1) - 1) for i in range(1, places - 1)]
 
-    halo = shape((count, width, SUB, span), f32)
-    far, near, waves_in, spectra_in, legendre_in, flat = call(
-        functools.partial(edges_kernel, count, band, width),
+    half = shape((count * lons // LANES, band // 2, LANES), f32)
+    own_near, own_far, waves_in, spectra_in, legendre_in = call(
+        edges_kernel,
         [
-            halo,
-            halo,
+            half,
+            half,
             shape((1, waves), jnp.int32),
             shape((*spectra.shape[:2], degrees), bf16),
             shape((lats, degrees), bf16),
-            shape((flat_rows, LANES), f32),
         ],
         [pltpu.HBM] * 4,
-        [pltpu.SemaphoreType.DMA((count + 3,))],
+        [pltpu.SemaphoreType.DMA((5,))],
     )(
         *(
             pltpu.with_memory_space_constraint(x, pltpu.HBM)
-            for x in (wavenumbers.reshape(1, waves), spectra[:, :, 0, 0], legendre_t, flat)
+            for x in (
+                wavenumbers.reshape(1, waves),
+                spectra[:, :, 0, 0],
+                legendre_t,
+                halves(tracers[:, 0]),
+            )
         )
     )
-    far = lax.ppermute(far, PLACE, far_pairs)
-    near = lax.ppermute(near, PLACE, near_pairs)
+    own_far, own_near = own_far.reshape(-1, LANES), own_near.reshape(-1, LANES)
+    near = lax.ppermute(own_near, PLACE, near_pairs)
+    far = lax.ppermute(own_far, PLACE, far_pairs)
     sent, masked = call(
         functools.partial(fourier_kernel, band),
         [shape((places, LANES), f32), shape((lats, degrees), bf16)],
@@ -570,13 +565,13 @@
     )(wavenumbers, kinetics, photolysis, heat_weights, quad_weights, sent)
 
     cells, column = call(
-        functools.partial(ready_kernel, count, band),
+        functools.partial(ready_kernel, count, width),
         [
             shape((count, band + 2 * width, SUB, span), f32),
             shape((band + 2, SUB, span), f32),
         ],
-        [VM] * 3 + [pl.ANY],
-    )(flat, near, far, sent)
+        [VM] * 4 + [pl.ANY],
+    )(own_far, own_near, near, far, sent)
     above = lax.ppermute(column, "lev", [(i, (i + 1) % levels) for i in range(levels)])
     if levels > 2:
         above = jnp.where(lax.axis_index("lev") > 0, above, 0.0)

time: 32.1 us -> 32 us (level)
    ppermute x2, starting transfers between devices: 1.18 us -> 5.03 us  [the longest x1 4.35 us: body(): near = lax.ppermute(own_near, PLACE, near_pairs)]
    all_to_all x1, starting transfers between devices: 8.78 us -> 4.98 us  [body(): received = lax.all_to_all(sent, PLACE, 0, 0, tiled=True)]
where the time goes in v6:
time: 32 us; the launch traced here: 31.8 us
  starting transfers between devices  11.6 us (36%)
  blocking collectives  9.24 us (29%)
  Pallas kernels  6.72 us (21%)
  waiting for transfers between devices  3.43 us (11%)
  between operations  0.76 us (2%)
    all_to_all x1, blocking collectives, body(): heat_received = lax.all_to_all(heat_sent, PLACE, 0, 0, tiled=True)  9.24 us
    all_to_all x1, starting transfers between devices, body(): received = lax.all_to_all(sent, PLACE, 0, 0, tiled=True)  4.98 us
    ppermute x1, starting transfers between devices, body(): near = lax.ppermute(own_near, PLACE, near_pairs)  4.35 us
    all_to_all x1, waiting for transfers between devices, body(): received = lax.all_to_all(sent, PLACE, 0, 0, tiled=True)  3.42 us
    pallas_call x1, Pallas kernels, body(): call(functools.partial(substeps_kernel, heats), [shape((6, *outer), f32),...  1.86 us
    ppermute x1, starting transfers between devices, body(): lax.ppermute(column, 'lev', [(i, (i + 1) % levels) for i in range(levels)])  1.59 us
    pallas_call x1, Pallas kernels, body(): call(functools.partial(last_kernel, band, heats), [shape((2, heats, 1, 1,...  1.16 us
    pallas_call x1, Pallas kernels, body(): call(edges_kernel, [half, half, shape((1, waves), jnp.int32), shape((*spe...  1.13 us
  transfers between devices with their start and end apart: 4, of which 1 were waited for; matrix products, arithmetic and copies ran while one was open for 0% of the time, Pallas kernels for 12%

profile of v6, /device:TPU:0, one launch (start us, length us, event | category | flops | bytes accessed | tf_op | source)
XLA Modules:
  0.0 31.8 jit_solution(18016290343903078139)
XLA Ops:
  0.6 1.1 %shard_map.95 = (f32[256,2,128]{2,1,0:T(2,128)S(1)}, f32[256,2,128]{2,1,0:T(2,128)S(1)}, s32[1,16]{1,0:T(1,128)S(1)}, bf16[2,4,1024]{2,1,0:T(4,128)(2,1)S(1)}, bf16[64,1024]{1,0:T(8,128)(2,1)S(1)}) custom-call(s32[1,16]{1,0:T(1,128)} %bitcast.32, bf16[2,4,1024]{2,1,0:T(4,128)(2,1)} %bitcast.35, bf16[64,1024]{1,0:T(8,128)(2,1)} %bitcast.34, ...), custom_call_target="tpu_custom_call" | custom-call | flops 1000000 | tf_op jit(solution)/shard_map/pallas_call | solution.py:520
  1.8 0.7 %collective-permute-start.1 = (f32[512,128]{1,0:T(8,128)S(1)}, f32[512,128]{1,0:T(8,128)S(1)}, u32[]{:S(2)}, u32[]{:S(2)}) collective-permute-start(f32[512,128]{1,0:T(8,128)S(1)} %bitcast.27), channel_id=1, source_target_pairs={{1,2},{2,1},{3,8},{8,3},{9,10},{10,9},{11,16},{16,11},{17,18},{18,... | collective-permute-start | bytes 786440 | tf_op jit(solution)/shard_map/ppermute | solution.py:544
  2.4 4.3 %collective-permute-start = (f32[512,128]{1,0:T(8,128)S(1)}, f32[512,128]{1,0:T(8,128)S(1)}, u32[]{:S(2)}, u32[]{:S(2)}) collective-permute-start(f32[512,128]{1,0:T(8,128)S(1)} %bitcast.25), channel_id=1, source_target_pairs={{0,1},{1,0},{2,3},{3,2},{8,9},{9,8},{10,11},{11,10},{16,17},{17,16... | collective-permute-start | bytes 786440 | tf_op jit(solution)/shard_map/ppermute | solution.py:543
  6.8 0.9 %shard_map.96 = (f32[16,128]{1,0:T(8,128)}, bf16[64,1024]{1,0:T(8,128)(2,1)S(1)}) custom-call(s32[1,16]{1,0:T(1,128)S(1)} %get-tuple-element.26.waves_ref, bf16[2,4,1024]{2,1,0:T(4,128)(2,1)S(1)} %get-tuple-element.27.spectra_ref, bf16[64,1024]{1,0:T(8,128)(2,1)S(1)} %get-tuple-element.28.legendre_ref), custom_call_target="tpu_custom_call" | custom-call | flops 1000000 | tf_op jit(solution)/shard_map/pallas_call | solution.py:545
  7.7 5.0 %all-to-all-start = ((f32[16,1,128]{2,1,0:T(1,128)}), f32[16,1,128]{2,1,0:T(1,128)S(1)}, u32[]{:S(2)}, u32[]{:S(2)}) async-start(f32[16,1,128]{2,1,0:T(1,128)} %bitcast.10), calls=%async_computation | async-start | bytes 16384 | tf_op jit(solution)/shard_map/all_to_all | solution.py:552
  12.7 0.0 copy-start.1
  12.7 0.0 copy-start.2
  12.7 0.0 collective-permute-done.1.far_ref
  12.7 0.0 collective-permute-done.near_ref
  12.7 0.2 shard_map.98
  12.9 0.0 copy-start
  13.0 0.0 copy-start.3
  13.0 0.0 copy-start.4
  13.0 1.6 %collective-permute-start.2 = (f32[6,8,512]{2,1,0:T(8,128)S(1)}, f32[6,8,512]{2,1,0:T(8,128)S(1)}, u32[]{:S(2)}, u32[]{:S(2)}) collective-permute-start(f32[6,8,512]{2,1,0:T(8,128)S(1)} %get-tuple-element.33), channel_id=1, source_target_pairs={{0,4},{4,0},{1,5},{5,1},{2,6},{6,2},{3,7},{7,3},{8,12},{12,8},{9,1... | collective-permute-start | bytes 294920 | tf_op jit(solution)/shard_map/ppermute | solution.py:575
  14.6 0.0 copy-done.1
  14.6 0.0 copy-done.2
  14.6 0.0 copy-done
  14.6 0.0 copy-done.3
  14.6 0.0 copy-done.4
  14.6 1.0 %shard_map.97 = (bf16[128,512]{1,0:T(8,128)(2,1)S(1)}, bf16[512,128]{1,0:T(8,128)(2,1)S(1)}, f32[2,8,128]{2,1,0:T(8,128)S(1)}, f32[128,128]{1,0:T(8,128)S(1)}) custom-call(s32[16]{0:T(128)S(1)} %copy-done, f32[8,8]{1,0:T(8,128)S(1)} %copy-done.1, f32[8]{0:T(128)S(1)} %copy-done.3, f32[3,8]{1,0:T(4,128)S(1)} %copy-done.2, f32[64]{0:T(128)S(1)} %copy-done.4, ...), custom_call_target="tpu_custom_call" | custom-call | flops 20000000000 | tf_op jit(solution)/shard_map/pallas_call | solution.py:555
  15.6 3.4 %all-to-all-done = f32[16,1,128]{2,1,0:T(1,128)S(1)} async-done(((f32[16,1,128]{2,1,0:T(1,128)}), f32[16,1,128]{2,1,0:T(1,128)S(1)}, u32[]{:S(2)}, u32[]{:S(2)}) %all-to-all-start) | async-done | bytes 8224 | tf_op jit(solution)/shard_map/all_to_all | solution.py:552
  19.0 1.9 %shard_map.99 = (f32[6,6,8,512]{3,2,1,0:T(8,128)S(1)}, f32[8,4,8,512]{3,2,1,0:T(8,128)S(1)}, f32[6,8,512]{2,1,0:T(8,128)S(1)}, f32[4,8,512]{2,1,0:T(8,128)S(1)},...) custom-call(f32[128,128]{1,0:T(8,128)S(1)} %get-tuple-element.30.rows_ref, f32[16,128]{1,0:T(8,128)S(1)} %bitcast.29, ...), custom_call_target="tpu_custom_call" | custom-call | flops 1000000 | tf_op jit(solution)/shard_map/pallas_call | solution.py:586
  20.9 0.0 collective-permute-done.2.above_ref
  20.9 0.5 %shard_map.100 = (f32[4,8,512]{2,1,0:T(8,128)S(1)}, f32[4,8,512]{2,1,0:T(8,128)S(1)}, f32[16,128]{1,0:T(8,128)S(1)}) custom-call(f32[128,128]{1,0:T(8,128)S(1)} %get-tuple-element.30.rows_ref, f32[6,8,512]{2,1,0:T(8,128)S(1)} %collective-permute-done.2.above_ref, bf16[512,128]{1,0:T(8,128)(2,1)S(1)} %get-tuple-element.34.turned_ref, ...), custom_call_target="tpu_custom_call" | custom-call | flops 1000000 | tf_op jit(solution)/shard_map/pallas_call | solution.py:599
  21.4 9.2 %all_to_all.22 = f32[16,1,128]{2,1,0:T(1,128)S(1)} all-to-all(f32[16,1,128]{2,1,0:T(1,128)S(1)} %bitcast.31), channel_id=1, replica_groups=mesh['wave'=4,'lev'=2,'grp'=4] {'wave','grp'}, dimensions={0} | all-to-all | bytes 16384 | tf_op jit(solution)/shard_map/all_to_all | solution.py:604
  30.6 1.2 %shard_map.101 = (f32[2,3,1,1,1024]{4,3,2,1,0:T(1,128)}, f32[1024,128]{1,0:T(8,128)}) custom-call(f32[16,128]{1,0:T(8,128)S(1)} %bitcast.30, bf16[64,1024]{1,0:T(8,128)(2,1)S(1)} %get-tuple-element.44.legendre_ref, f32[128,128]{1,0:T(8,128)S(1)} %get-tuple-element.30.rows_ref, f32[8,4,8,512]{3,2,1,0:T(8,128)S(1)} %get-tuple-element.45.base_ref, ...), custom_call_target="tpu_custom_call" | custom-call | flops 1000000 | tf_op jit(solution)/shard_map/pallas_call | solution.py:605
Async XLA Ops:
  1.8 10.9 %collective-permute-start.1 = (f32[512,128]{1,0:T(8,128)S(1)}, f32[512,128]{1,0:T(8,128)S(1)}, u32[]{:S(2)}, u32[]{:S(2)}) collective-permute-start(f32[512,128]{1,0:T(8,128)S(1)} %bitcast.27), channel_id=1, source_target_pairs={{1,2},{2,1},{3,8},{8,3},{9,10},{10,9},{11,16},{16,11},{17,18},{18,... | collective-permute-start | bytes 786440 | tf_op jit(solution)/shard_map/ppermute | solution.py:544
  2.4 10.2 %collective-permute-start = (f32[512,128]{1,0:T(8,128)S(1)}, f32[512,128]{1,0:T(8,128)S(1)}, u32[]{:S(2)}, u32[]{:S(2)}) collective-permute-start(f32[512,128]{1,0:T(8,128)S(1)} %bitcast.25), channel_id=1, source_target_pairs={{0,1},{1,0},{2,3},{3,2},{8,9},{9,8},{10,11},{11,10},{16,17},{17,16... | collective-permute-start | bytes 786440 | tf_op jit(solution)/shard_map/ppermute | solution.py:543
  7.7 11.3 %all-to-all-start = ((f32[16,1,128]{2,1,0:T(1,128)}), f32[16,1,128]{2,1,0:T(1,128)S(1)}, u32[]{:S(2)}, u32[]{:S(2)}) async-start(f32[16,1,128]{2,1,0:T(1,128)} %bitcast.10), calls=%async_computation | async-start | bytes 16384 | tf_op jit(solution)/shard_map/all_to_all | solution.py:552
  12.7 1.9 %copy-start.1 = (f32[8,8]{1,0:T(8,128)S(1)}, f32[8,8]{1,0:T(8,128)}, u32[]{:S(2)}) copy-start(f32[8,8]{1,0:T(8,128)} %kinetics_ref.1) | copy-start | bytes 772
  12.7 1.9 %copy-start.2 = (f32[3,8]{1,0:T(4,128)S(1)}, f32[3,8]{1,0:T(4,128)}, u32[]{:S(2)}) copy-start(f32[3,8]{1,0:T(4,128)} %weights_ref.1) | copy-start | bytes 292
  12.9 1.6 %copy-start = (s32[16]{0:T(128)S(1)}, s32[16]{0:T(128)}, u32[]{:S(2)}) copy-start(s32[16]{0:T(128)} %waves_ref.1) | copy-start | bytes 196
  13.0 1.6 %copy-start.3 = (f32[8]{0:T(128)S(1)}, f32[8]{0:T(128)}, u32[]{:S(2)}) copy-start(f32[8]{0:T(128)} %photolysis_ref.1) | copy-start | bytes 100
  13.0 1.6 %copy-start.4 = (f32[64]{0:T(128)S(1)}, f32[64]{0:T(128)}, u32[]{:S(2)}) copy-start(f32[64]{0:T(128)} %quad_ref.1) | copy-start | bytes 772
  13.0 7.9 %collective-permute-start.2 = (f32[6,8,512]{2,1,0:T(8,128)S(1)}, f32[6,8,512]{2,1,0:T(8,128)S(1)}, u32[]{:S(2)}, u32[]{:S(2)}) collective-permute-start(f32[6,8,512]{2,1,0:T(8,128)S(1)} %get-tuple-element.33), channel_id=1, source_target_pairs={{0,4},{4,0},{1,5},{5,1},{2,6},{6,2},{3,7},{7,3},{8,12},{12,8},{9,1... | collective-permute-start | bytes 294920 | tf_op jit(solution)/shard_map/ppermute | solution.py:575
